TPU v7x, 32 devices: a whole 2x2x4 slice. The times are simulated.
32 devices in a mesh: dp: 16 (over z, x, core), tensor: 2 (over y).
Axes of the slice: x: 2, y: 2, z: 4, core: 2. Of those that a mesh axis runs over, the one named last changes fastest.
Arguments:
- inputs: bfloat16 [16, 2, 320, 2048], P(None, 'tensor', 'dp'), may hold values from -6 to 6
- lengths: int32 [16], replicated, may hold values from 160 to 640, as said below
- dealing: int32 [16], replicated, may hold values from 0 to 15, each once
- w_query: bfloat16 [2048, 2048], P('dp', 'tensor'), may hold values from -0.125 to 0.125
- w_key: bfloat16 [2048, 2048], P('dp', 'tensor'), may hold values from -0.125 to 0.125
- w_value: bfloat16 [2048, 2048], P('dp', 'tensor'), may hold values from -0.125 to 0.125
- b_query: float32 [2048], replicated, may hold values from -3 to 3
- b_value: float32 [2048], replicated, may hold values from -3 to 3
- w_out: bfloat16 [2048, 2048], P('tensor', 'dp'), may hold values from -0.5 to 0.5
- b_out: float32 [2048], replicated, may hold values from -3 to 3
- gain_first: float32 [2048], replicated, may hold values from 0.5 to 1.5
- shift_first: float32 [2048], replicated, may hold values from -3 to 3
- w_up: bfloat16 [2048, 8192], P('dp', 'tensor'), may hold values from -0.125 to 0.125
- b_up: float32 [8192], replicated, may hold values from -3 to 3
- w_down: bfloat16 [8192, 2048], P('tensor', 'dp'), may hold values from -0.0625 to 0.0625
- b_down: float32 [2048], replicated, may hold values from -3 to 3
- gain_second: float32 [2048], replicated, may hold values from 0.5 to 1.5
- shift_second: float32 [2048], replicated, may hold values from -3 to 3
- cotangent: bfloat16 [16, 640, 2048], P('dp', 'tensor'), may hold values from -6 to 6
Outputs:
- output: bfloat16 [16, 640, 2048], P('dp', 'tensor')
- grad_inputs: bfloat16 [16, 2, 320, 2048], P(None, 'tensor', 'dp')
- grad_w_query: float32 [2048, 2048], P('dp', 'tensor')
- grad_w_key: float32 [2048, 2048], P('dp', 'tensor')
- grad_w_value: float32 [2048, 2048], P('dp', 'tensor')
- grad_b_query: float32 [2048], replicated
- grad_b_value: float32 [2048], replicated
- grad_w_out: float32 [2048, 2048], P('tensor', 'dp')
- grad_b_out: float32 [2048], replicated
- grad_gain_first: float32 [2048], replicated
- grad_shift_first: float32 [2048], replicated
- grad_w_up: float32 [2048, 8192], P('dp', 'tensor')
- grad_b_up: float32 [8192], replicated
- grad_w_down: float32 [8192, 2048], P('tensor', 'dp')
- grad_b_down: float32 [2048], replicated
- grad_gain_second: float32 [2048], replicated
- grad_shift_second: float32 [2048], replicated
Inputs may be any that keep to these rules, and one draw needn't show every extreme that they name: `lengths`: every sequence has 160 live tokens or more; one sequence has all 640.
All inputs are finite; a program needn't handle non-finite values.
Results may differ from a plain program's by a relative error of at most 0.017.
Values may be sent and summed in bfloat16 or wider, within the bound.
A program may use at most 256 MiB of HBM per device.

v0:
```python
from functools import partial

import jax
import jax.numpy as jnp
from jax import lax
from jax.sharding import PartitionSpec as P

HEAD_DIM = 128


EPSILON = 1e-05
MASKED = -1e30


def norm_forward(values, scale_gain, bias_shift):
    center = values - jnp.mean(values, axis=-1, keepdims=True)
    inverse = lax.rsqrt(jnp.mean(center * center, axis=-1, keepdims=True) + EPSILON)
    normed = center * inverse
    return (normed * scale_gain + bias_shift, normed, inverse)


def norm_backward(grad_out, scale_gain, normed, inverse):
    scaled = grad_out * scale_gain
    grad_in = inverse * (
        scaled
        - jnp.mean(scaled, axis=-1, keepdims=True)
        - normed * jnp.mean(scaled * normed, axis=-1, keepdims=True)
    )
    return (grad_in, jnp.sum(grad_out * normed, axis=0), jnp.sum(grad_out, axis=0))


def contract_rows(left, right):
    return lax.dot_general(
        left, right, (((0,), (0,)), ((), ())), preferred_element_type=jnp.float32
    )


def contract_cols(left, right):
    return lax.dot_general(
        left, right, (((1,), (1,)), ((), ())), preferred_element_type=jnp.float32
    )


def attention_scores(query_rows, key_rows, key_valid, factor):
    scores = (
        jnp.einsum("qhd,khd->hqk", query_rows, key_rows, preferred_element_type=jnp.float32)
        * factor
    )
    return jnp.where(key_valid[None, None, :], scores, MASKED)


def place_slice(local_sum, full_size, offset):
    return lax.dynamic_update_slice_in_dim(
        jnp.zeros((full_size,), jnp.float32), local_sum, offset, 0
    )


def shards(
    inputs,
    lengths,
    dealing,
    w_query,
    w_key,
    w_value,
    b_query,
    b_value,
    w_out,
    b_out,
    gain_first,
    shift_first,
    w_up,
    b_up,
    w_down,
    b_down,
    gain_second,
    shift_second,
    cotangent,
):
    group_index = lax.axis_index("dp")
    tensor_index = lax.axis_index("tensor")
    ordered = jnp.take(inputs, dealing, axis=0)
    arrived = lax.all_to_all(ordered, "dp", split_axis=0, concat_axis=2, tiled=True)
    features = arrived.shape[3]
    half_rows = arrived.shape[2]
    own_rows = arrived.reshape(half_rows, features)
    seq_len = half_rows * lax.axis_size("tensor")
    length = lengths[dealing[group_index]]
    key_valid = jnp.arange(seq_len) < length
    factor = HEAD_DIM ** (-0.5)
    gathered = (
        lax.all_gather(w_query, "dp", axis=0, tiled=True),
        lax.all_gather(w_key, "dp", axis=0, tiled=True),
        lax.all_gather(w_value, "dp", axis=0, tiled=True),
        lax.all_gather(w_out, "dp", axis=1, tiled=True),
        lax.all_gather(w_up, "dp", axis=0, tiled=True),
        lax.all_gather(w_down, "dp", axis=1, tiled=True),
    )
    query_full, key_full, value_full, out_full, up_full, down_full = gathered
    head_cols = query_full.shape[1]
    heads_local = head_cols // HEAD_DIM
    up_cols = up_full.shape[1]
    query_bias = lax.dynamic_slice_in_dim(b_query, tensor_index * head_cols, head_cols)
    value_bias = lax.dynamic_slice_in_dim(b_value, tensor_index * head_cols, head_cols)
    up_bias = lax.dynamic_slice_in_dim(b_up, tensor_index * up_cols, up_cols)
    full_in = lax.all_gather(own_rows, "tensor", axis=0, tiled=True)
    query_rows = (
        jnp.dot(full_in, query_full, preferred_element_type=jnp.float32) + query_bias
    ).astype(jnp.bfloat16)
    key_rows = jnp.dot(full_in, key_full, preferred_element_type=jnp.float32).astype(jnp.bfloat16)
    value_rows = (
        jnp.dot(full_in, value_full, preferred_element_type=jnp.float32) + value_bias
    ).astype(jnp.bfloat16)
    query_rows = query_rows.reshape(seq_len, heads_local, HEAD_DIM)
    key_rows = key_rows.reshape(seq_len, heads_local, HEAD_DIM)
    value_rows = value_rows.reshape(seq_len, heads_local, HEAD_DIM)
    scores = attention_scores(query_rows, key_rows, key_valid, factor)
    row_max = jnp.max(scores, axis=-1, keepdims=True)
    expanded = jnp.exp(scores - row_max)
    row_sum = jnp.sum(expanded, axis=-1, keepdims=True)
    log_norm = row_max + jnp.log(row_sum)
    softmax_low = (expanded / row_sum).astype(jnp.bfloat16)
    mixed_heads = jnp.einsum(
        "hqk,khd->qhd", softmax_low, value_rows, preferred_element_type=jnp.float32
    )
    mixed_heads = mixed_heads.astype(jnp.bfloat16).reshape(seq_len, head_cols)
    attn_part = jnp.dot(mixed_heads, out_full, preferred_element_type=jnp.float32)
    attended = lax.psum_scatter(attn_part, "tensor", scatter_dimension=0, tiled=True) + b_out
    hidden, normed_first, inverse_first = norm_forward(
        own_rows.astype(jnp.float32) + attended, gain_first, shift_first
    )
    full_hidden = lax.all_gather(hidden.astype(jnp.bfloat16), "tensor", axis=0, tiled=True)
    upward = jnp.dot(full_hidden, up_full, preferred_element_type=jnp.float32) + up_bias
    active = jax.nn.gelu(upward, approximate=True).astype(jnp.bfloat16)
    down_part = jnp.dot(active, down_full, preferred_element_type=jnp.float32)
    downward = (
        lax.psum_scatter(
            down_part.astype(jnp.bfloat16), "tensor", scatter_dimension=0, tiled=True
        ).astype(jnp.float32)
        + b_down
    )
    result, normed_second, inverse_second = norm_forward(
        hidden + downward, gain_second, shift_second
    )
    output = result.astype(jnp.bfloat16).reshape(cotangent.shape)
    gathered = (
        lax.all_gather(w_query, "dp", axis=0, tiled=True),
        lax.all_gather(w_key, "dp", axis=0, tiled=True),
        lax.all_gather(w_value, "dp", axis=0, tiled=True),
        lax.all_gather(w_out, "dp", axis=1, tiled=True),
        lax.all_gather(w_up, "dp", axis=0, tiled=True),
        lax.all_gather(w_down, "dp", axis=1, tiled=True),
    )
    query_full, key_full, value_full, out_full, up_full, down_full = gathered
    grad_result = cotangent.reshape(half_rows, features).astype(jnp.float32)
    grad_second, grad_gain_second, grad_shift_second = norm_backward(
        grad_result, gain_second, normed_second, inverse_second
    )
    grad_down = grad_second.astype(jnp.bfloat16)
    grad_b_down = jnp.sum(grad_down.astype(jnp.float32), axis=0)
    full_grad_down = lax.all_gather(grad_down, "tensor", axis=0, tiled=True)
    grad_active = contract_cols(full_grad_down, down_full)
    grad_w_down = contract_rows(active, full_grad_down)
    _, gelu_pull = jax.vjp(partial(jax.nn.gelu, approximate=True), upward)
    grad_up = gelu_pull(grad_active)[0].astype(jnp.bfloat16)
    grad_up_bias = jnp.sum(grad_up.astype(jnp.float32), axis=0)
    grad_w_up = contract_rows(full_hidden, grad_up)
    hidden_part = contract_cols(grad_up, up_full)
    grad_hidden = grad_second + lax.psum_scatter(
        hidden_part.astype(jnp.bfloat16), "tensor", scatter_dimension=0, tiled=True
    ).astype(jnp.float32)
    grad_first, grad_gain_first, grad_shift_first = norm_backward(
        grad_hidden, gain_first, normed_first, inverse_first
    )
    grad_attended = grad_first.astype(jnp.bfloat16)
    grad_b_out = jnp.sum(grad_attended.astype(jnp.float32), axis=0)
    full_grad_attended = lax.all_gather(grad_attended, "tensor", axis=0, tiled=True)
    grad_mixed = contract_cols(full_grad_attended, out_full).astype(jnp.bfloat16)
    grad_w_out = contract_rows(mixed_heads, full_grad_attended)
    grad_mixed = grad_mixed.reshape(seq_len, heads_local, HEAD_DIM)
    scores = attention_scores(query_rows, key_rows, key_valid, factor)
    softmax_again = jnp.exp(scores - log_norm)
    grad_values = jnp.einsum(
        "hqk,qhd->khd",
        softmax_again.astype(jnp.bfloat16),
        grad_mixed,
        preferred_element_type=jnp.float32,
    ).astype(jnp.bfloat16)
    grad_softmax = jnp.einsum(
        "qhd,khd->hqk", grad_mixed, value_rows, preferred_element_type=jnp.float32
    )
    row_inner = jnp.sum(softmax_again * grad_softmax, axis=-1, keepdims=True)
    grad_scores = (softmax_again * (grad_softmax - row_inner)).astype(jnp.bfloat16)
    grad_queries = (
        (
            jnp.einsum("hqk,khd->qhd", grad_scores, key_rows, preferred_element_type=jnp.float32)
            * factor
        )
        .astype(jnp.bfloat16)
        .reshape(seq_len, head_cols)
    )
    grad_keys = (
        (
            jnp.einsum("hqk,qhd->khd", grad_scores, query_rows, preferred_element_type=jnp.float32)
            * factor
        )
        .astype(jnp.bfloat16)
        .reshape(seq_len, head_cols)
    )
    grad_values = grad_values.reshape(seq_len, head_cols)
    grad_w_query = contract_rows(full_in, grad_queries)
    grad_w_key = contract_rows(full_in, grad_keys)
    grad_w_value = contract_rows(full_in, grad_values)
    grad_query_bias = jnp.sum(grad_queries.astype(jnp.float32), axis=0)
    grad_value_bias = jnp.sum(grad_values.astype(jnp.float32), axis=0)
    input_part = (
        contract_cols(grad_queries, query_full)
        + contract_cols(grad_keys, key_full)
        + contract_cols(grad_values, value_full)
    )
    grad_own = grad_first + lax.psum_scatter(
        input_part.astype(jnp.bfloat16), "tensor", scatter_dimension=0, tiled=True
    ).astype(jnp.float32)
    grad_sent = grad_own.astype(jnp.bfloat16).reshape(1, 1, half_rows, features)
    returned = lax.all_to_all(grad_sent, "dp", split_axis=2, concat_axis=0, tiled=True)
    grad_inputs = jnp.zeros_like(returned).at[dealing].set(returned)
    weight_sums = (
        lax.psum_scatter(grad_w_query, "dp", scatter_dimension=0, tiled=True),
        lax.psum_scatter(grad_w_key, "dp", scatter_dimension=0, tiled=True),
        lax.psum_scatter(grad_w_value, "dp", scatter_dimension=0, tiled=True),
        lax.psum_scatter(grad_w_out, "dp", scatter_dimension=1, tiled=True),
        lax.psum_scatter(grad_w_up, "dp", scatter_dimension=0, tiled=True),
        lax.psum_scatter(grad_w_down, "dp", scatter_dimension=1, tiled=True),
    )
    full_cols = b_query.shape[0]
    full_up = b_up.shape[0]
    small_sums = lax.psum(
        (
            place_slice(grad_query_bias, full_cols, tensor_index * head_cols),
            place_slice(grad_value_bias, full_cols, tensor_index * head_cols),
            grad_b_out,
            place_slice(grad_up_bias, full_up, tensor_index * up_cols),
            grad_b_down,
            grad_gain_first,
            grad_shift_first,
            grad_gain_second,
            grad_shift_second,
        ),
        ("dp", "tensor"),
    )
    return (
        output,
        grad_inputs,
        weight_sums[0],
        weight_sums[1],
        weight_sums[2],
        small_sums[0],
        small_sums[1],
        weight_sums[3],
        small_sums[2],
        small_sums[5],
        small_sums[6],
        weight_sums[4],
        small_sums[3],
        weight_sums[5],
        small_sums[4],
        small_sums[7],
        small_sums[8],
    )


def solution(mesh):
    in_specs = (
        P(None, "tensor", "dp", None),
        P(),
        P(),
        P("dp", "tensor"),
        P("dp", "tensor"),
        P("dp", "tensor"),
        P(),
        P(),
        P("tensor", "dp"),
        P(),
        P(),
        P(),
        P("dp", "tensor"),
        P(),
        P("tensor", "dp"),
        P(),
        P(),
        P(),
        P("dp", "tensor", None),
    )
    out_specs = (
        P("dp", "tensor", None),
        P(None, "tensor", "dp", None),
        P("dp", "tensor"),
        P("dp", "tensor"),
        P("dp", "tensor"),
        P(),
        P(),
        P("tensor", "dp"),
        P(),
        P(),
        P(),
        P("dp", "tensor"),
        P(),
        P("tensor", "dp"),
        P(),
        P(),
        P(),
    )
    return jax.shard_map(shards, mesh=mesh, in_specs=in_specs, out_specs=out_specs, check_vma=False)
```

profile of v0, /device:TPU:0, one launch (start us, length us, event | category | flops | bytes accessed | tf_op | source)
XLA Modules:
  0.0 2264.9 jit_solution(4876017756425494981)
XLA Ops:
  11.5 43.2 %all_to_all.21 = bf16[16,1,20,2048]{3,2,1,0:T(8,128)(2,1)S(1)} all-to-all(bf16[16,1,20,2048]{3,2,1,0:T(8,128)(2,1)S(1)} %fusion.27), channel_id=1, replica_groups=mesh['dp'=16,'tensor'=2] {'dp'}, dimensions={0} | all-to-all | bytes 2621440 | tf_op jit(solution)/shard_map/all_to_all | solution.py:82
  62.5 33.0 %all-gather.11.cloned.1.call-done = bf16[640,2048]{1,0:T(8,128)(2,1)} async-done(((bf16[320,2048]{1,0:T(8,128)(2,1)}), bf16[640,2048]{1,0:T(8,128)(2,1)}) %all-gather.11.cloned.1.call-update) | async-done | bytes 2621456 | tf_op jit(solution)/shard_map/all_gather | solution.py:105
  95.5 52.9 %all-gather.15.cloned.1.call-done = bf16[2048,1024]{1,0:T(8,128)(2,1)} async-done(((bf16[128,1024]{1,0:T(8,128)(2,1)}), bf16[2048,1024]{1,0:T(8,128)(2,1)}) %all-gather.15.cloned.1.call-update) | async-done | bytes 4194320 | tf_op jit(solution)/shard_map/all_gather | solution.py:91
  148.4 5.9 add_convert_fusion.3
  155.3 44.4 %all-gather.17.cloned.1.call-done = bf16[2048,1024]{1,0:T(8,128)(2,1)} async-done(((bf16[128,1024]{1,0:T(8,128)(2,1)}), bf16[2048,1024]{1,0:T(8,128)(2,1)}) %all-gather.17.cloned.1.call-update) | async-done | bytes 4194320 | tf_op jit(solution)/shard_map/all_gather | solution.py:92
  199.7 6.9 convolution_convert_fusion.3
  211.4 4.7 copy-done
  217.8 33.0 %all-gather.13.cloned.1.call-done = bf16[2048,1024]{1,0:T(8,128)(2,1)} async-done(((bf16[128,1024]{1,0:T(8,128)(2,1)}), bf16[2048,1024]{1,0:T(8,128)(2,1)}) %all-gather.13.cloned.1.call-update) | async-done | bytes 4194320 | tf_op jit(solution)/shard_map/all_gather | solution.py:93
  250.8 6.0 fusion.28
  261.3 43.2 %all-gather.19.cloned.1.call-done = bf16[1024,2048]{1,0:T(8,128)(2,1)} async-done(((bf16[1024,128]{1,0:T(8,128)(2,1)}), bf16[1024,2048]{1,0:T(8,128)(2,1)}) %all-gather.19.cloned.1.call-update) | async-done | bytes 4194320 | tf_op jit(solution)/shard_map/all_gather | solution.py:94
  304.6 7.5 fusion.43
  312.1 64.0 %reduce-scatter.11.cloned.1.call-done = f32[320,2048]{1,0:T(8,128)} async-done(((f32[640,2048]{1,0:T(8,128)}), f32[320,2048]{1,0:T(8,128)}) %reduce-scatter.11.cloned.1.call-update) | async-done | bytes 2621456 | tf_op jit(solution)/shard_map/reduce_scatter | solution.py:127
  382.5 37.6 %all-gather.21.cloned.1.call-done = bf16[640,2048]{1,0:T(8,128)(2,1)} async-done(((bf16[320,2048]{1,0:T(8,128)(2,1)}), bf16[640,2048]{1,0:T(8,128)(2,1)}) %all-gather.21.cloned.1.call-update) | async-done | bytes 2621456 | tf_op jit(solution)/shard_map/all_gather | solution.py:131
  420.1 129.3 %all-gather.23.cloned.1.call-done = bf16[2048,4096]{1,0:T(8,128)(2,1)} async-done(((bf16[128,4096]{1,0:T(8,128)(2,1)}), bf16[2048,4096]{1,0:T(8,128)(2,1)}) %all-gather.23.cloned.1.call-update) | async-done | bytes 16777232 | tf_op jit(solution)/shard_map/all_gather | solution.py:95
  549.4 17.6 fusion.44
  567.0 113.3 %all-gather.25.cloned.1.call-done = bf16[4096,2048]{1,0:T(8,128)(2,1)} async-done(((bf16[4096,128]{1,0:T(8,128)(2,1)}), bf16[4096,2048]{1,0:T(8,128)(2,1)}) %all-gather.25.cloned.1.call-update) | async-done | bytes 16777232 | tf_op jit(solution)/shard_map/all_gather | solution.py:96
  680.4 21.0 convolution_convert_fusion.1
  701.6 35.7 %reduce-scatter.13.cloned.1.call-done = bf16[320,2048]{1,0:T(8,128)(2,1)} async-done(((bf16[640,2048]{1,0:T(8,128)(2,1)}), bf16[320,2048]{1,0:T(8,128)(2,1)}) %reduce-scatter.13.cloned.1.call-update) | async-done | bytes 1310736 | tf_op jit(solution)/shard_map/reduce_scatter | solution.py:136
  742.4 4.3 convert_reduce_fusion.2
  746.8 39.1 %all-gather.27.cloned.1.call-done = bf16[640,2048]{1,0:T(8,128)(2,1)} async-done(((bf16[320,2048]{1,0:T(8,128)(2,1)}), bf16[640,2048]{1,0:T(8,128)(2,1)}) %all-gather.27.cloned.1.call-update) | async-done | bytes 2621456 | tf_op jit(solution)/shard_map/all_gather | solution.py:160
  785.9 24.5 %convert_reduce_fusion = (f32[4096]{0:T(1024)S(1)}, bf16[640,4096]{1,0:T(8,128)(2,1)}) fusion(f32[640,4096]{1,0:T(8,128)} %fusion.44, f32[4096]{0:T(1024)S(1)} %dynamic_slice.19, bf16[640,2048]{1,0:T(8,128)(2,1)} %all-gather.27.cloned.1.call-done, bf16[4096,2048]{1,0:T(8,128)(2,1)} %all-gather.25.cloned.1.call-done), kind=kOutput, calls=%fused_computation.18 | convolution fusion | flops 10797707264 | bytes 35160064 | tf_op jit(solution)/shard_map/dot_general | solution.py:39
  810.4 17.2 convolution_convert_fusion
  827.9 37.5 %reduce-scatter.15.cloned.1.call-done = bf16[320,2048]{1,0:T(8,128)(2,1)} async-done(((bf16[640,2048]{1,0:T(8,128)(2,1)}), bf16[320,2048]{1,0:T(8,128)(2,1)}) %reduce-scatter.15.cloned.1.call-update) | async-done | bytes 1310736 | tf_op jit(solution)/shard_map/reduce_scatter | solution.py:168
  865.3 4.0 multiply_reduce_fusion.1
  873.1 39.1 %all-gather.29.cloned.1.call-done = bf16[640,2048]{1,0:T(8,128)(2,1)} async-done(((bf16[320,2048]{1,0:T(8,128)(2,1)}), bf16[640,2048]{1,0:T(8,128)(2,1)}) %all-gather.29.cloned.1.call-update) | async-done | bytes 2621456 | tf_op jit(solution)/shard_map/all_gather | solution.py:176
  912.2 5.9 convolution_convert_fusion.2
  918.8 8.1 convert_reduce_fusion.4
  926.9 10.5 multiply_reduce_fusion
  937.4 7.0 multiply_convert_fusion
  954.2 4.3 add_convert_fusion
  961.9 8.8 fusion.49
  972.1 7.5 fusion.48
  979.6 7.5 fusion.47
  988.9 7.1 fusion.50
  997.7 23.3 %fusion.37 = f32[4096,2048]{1,0:T(8,128)} fusion(bf16[640,2048]{1,0:T(8,128)(2,1)S(1)} %copy-done.33, f32[640,4096]{1,0:T(8,128)} %fusion.44, f32[4096]{0:T(1024)S(1)} %dynamic_slice.19), kind=kOutput, calls=%fused_computation.92 | convolution fusion | flops 10763632640 | bytes 46678016 | tf_op jit(solution)/shard_map/dot_general | solution.py:33
  1022.8 20.1 fusion.51
  1049.0 9.4 reduce.5
  1058.4 3.7 reshape.190
  1062.0 37.5 %all_to_all.22 = bf16[16,2,20480]{2,1,0:T(2,128)(2,1)} all-to-all(bf16[16,2,20480]{2,1,0:T(2,128)(2,1)S(1)} %reshape.190), channel_id=1, replica_groups=mesh['dp'=16,'tensor'=2] {'dp'}, dimensions={0} | all-to-all | bytes 2621440 | tf_op jit(solution)/shard_map/all_to_all | solution.py:224
  1099.6 4.5 reshape.191
  1104.1 8.7 bitcast_reduce_fusion
  1118.1 13.6 all-reduce.3.cloned.1.call-done
  1131.7 110.8 %reduce-scatter.23.cloned.1.call-done = f32[128,1024]{1,0:T(8,128)} async-done(((f32[2048,1024]{1,0:T(8,128)}), f32[128,1024]{1,0:T(8,128)}) %reduce-scatter.23.cloned.1.call-update) | async-done | bytes 524304 | tf_op jit(solution)/shard_map/reduce_scatter | solution.py:229
  1242.5 109.5 %reduce-scatter.21.cloned.1.call-done = f32[128,1024]{1,0:T(8,128)} async-done(((f32[2048,1024]{1,0:T(8,128)}), f32[128,1024]{1,0:T(8,128)}) %reduce-scatter.21.cloned.1.call-update) | async-done | bytes 524304 | tf_op jit(solution)/shard_map/reduce_scatter | solution.py:228
  1352.0 109.5 %reduce-scatter.19.cloned.1.call-done = f32[128,1024]{1,0:T(8,128)} async-done(((f32[2048,1024]{1,0:T(8,128)}), f32[128,1024]{1,0:T(8,128)}) %reduce-scatter.19.cloned.1.call-update) | async-done | bytes 524304 | tf_op jit(solution)/shard_map/reduce_scatter | solution.py:227
  1461.5 109.8 %reduce-scatter.25.cloned.1.call-done = f32[1024,128]{1,0:T(8,128)} async-done(((f32[1024,2048]{1,0:T(8,128)}), f32[1024,128]{1,0:T(8,128)}) %reduce-scatter.25.cloned.1.call-update) | async-done | bytes 524304 | tf_op jit(solution)/shard_map/reduce_scatter | solution.py:230
  1571.3 337.7 %reduce-scatter.29.cloned.1.call-done = f32[4096,128]{1,0:T(8,128)} async-done(((f32[4096,2048]{1,0:T(8,128)}), f32[4096,128]{1,0:T(8,128)}) %reduce-scatter.29.cloned.1.call-update) | async-done | bytes 2097168 | tf_op jit(solution)/shard_map/reduce_scatter | solution.py:232
  1909.0 337.2 %reduce-scatter.27.cloned.1.call-done = f32[128,4096]{1,0:T(8,128)} async-done(((f32[2048,4096]{1,0:T(8,128)}), f32[128,4096]{1,0:T(8,128)}) %reduce-scatter.27.cloned.1.call-update) | async-done | bytes 2097168 | tf_op jit(solution)/shard_map/reduce_scatter | solution.py:231
  (189 shorter events, 80.9 us)
Async XLA Ops:
  7.2 88.4 %all-gather.11.cloned.1.call-start = ((), (), s32[]{:S(2)}) async-start(), calls=%async_computation.12 | async-start | bytes 3932160 | tf_op jit(solution)/shard_map/all_gather | solution.py:105
  54.7 3.9 copy-start.35
  54.7 5.8 copy-start.28
  54.7 6.5 copy-start.36
  56.0 92.5 %all-gather.15.cloned.1.call-start = ((), (), s32[]{:S(2)}) async-start(), calls=%async_computation.14 | async-start | bytes 4456448 | tf_op jit(solution)/shard_map/all_gather | solution.py:91
  56.7 143.0 %all-gather.17.cloned.1.call-start = ((), (), s32[]{:S(2)}) async-start(), calls=%async_computation.15 | async-start | bytes 4456448 | tf_op jit(solution)/shard_map/all_gather | solution.py:92
  57.5 193.3 %all-gather.13.cloned.1.call-start = ((), (), s32[]{:S(2)}) async-start(), calls=%async_computation.13 | async-start | bytes 4456448 | tf_op jit(solution)/shard_map/all_gather | solution.py:93
  58.0 246.5 %all-gather.19.cloned.1.call-start = ((), (), s32[]{:S(2)}) async-start(), calls=%async_computation.16 | async-start | bytes 4456448 | tf_op jit(solution)/shard_map/all_gather | solution.py:94
  58.6 317.4 %reduce-scatter.11.cloned.1.call-start = ((), (), s32[]{:S(2)}) async-start(), calls=%async_computation.17 | async-start | bytes 7864320 | tf_op jit(solution)/shard_map/reduce_scatter | solution.py:127
  155.3 53.1 %copy-start.7 = (bf16[640,1024]{0,1:T(8,128)(2,1)}, bf16[640,1024]{0,1:T(8,128)(2,1)S(1)}, u32[]{:S(2)}) copy-start(bf16[640,1024]{0,1:T(8,128)(2,1)S(1)} %copy.85) | copy-start | bytes 3932164
  208.4 3.1 copy-start.3
  211.4 4.7 copy-start
  216.1 34.7 %dynamic-slice-start = ((f32[2048]{0:T(1024)}, s32[]{:T(128)}), f32[1024]{0:T(1024)S(1)}, s32[]{:S(2)}) async-start(f32[2048]{0:T(1024)} %param.26, s32[]{:T(128)} %select_n.41), calls=%async_computation.37 | async-start | bytes 8704 | tf_op jit(solution)/shard_map/dynamic_slice | solution.py:103
  250.8 7.1 copy-start.1
  261.3 50.7 %copy-start.37 = (bf16[8,128,640]{2,1,0:T(8,128)(2,1)}, bf16[8,128,640]{2,1,0:T(8,128)(2,1)S(1)}, u32[]{:S(2)}) copy-start(bf16[8,128,640]{2,1,0:T(8,128)(2,1)S(1)} %fusion.23) | copy-start | bytes 3932164
  312.0 64.0 %copy-start.22 = (f32[2048]{0:T(1024)S(1)}, f32[2048]{0:T(1024)}, u32[]{:S(2)}) copy-start(f32[2048]{0:T(1024)} %param.28) | copy-start | bytes 24580
  312.1 108.1 %all-gather.21.cloned.1.call-start = ((), (), s32[]{:S(2)}) async-start(), calls=%async_computation.18 | async-start | bytes 3932160 | tf_op jit(solution)/shard_map/all_gather | solution.py:131
  380.9 168.5 %all-gather.23.cloned.1.call-start = ((), (), s32[]{:S(2)}) async-start(), calls=%async_computation.19 | async-start | bytes 17825792 | tf_op jit(solution)/shard_map/all_gather | solution.py:95
  381.7 298.7 %all-gather.25.cloned.1.call-start = ((), (), s32[]{:S(2)}) async-start(), calls=%async_computation.20 | async-start | bytes 17825792 | tf_op jit(solution)/shard_map/all_gather | solution.py:96
  382.4 354.9 %reduce-scatter.13.cloned.1.call-start = ((), (), s32[]{:S(2)}) async-start(), calls=%async_computation.21 | async-start | bytes 3932160 | tf_op jit(solution)/shard_map/reduce_scatter | solution.py:136
  701.4 35.9 %copy-start.23 = (f32[2048]{0:T(1024)S(1)}, f32[2048]{0:T(1024)}, u32[]{:S(2)}) copy-start(f32[2048]{0:T(1024)} %param.34) | copy-start | bytes 24580
  701.4 84.5 %all-gather.27.cloned.1.call-start = ((), (), s32[]{:S(2)}) async-start(), calls=%async_computation.22 | async-start | bytes 3932160 | tf_op jit(solution)/shard_map/all_gather | solution.py:160
  739.9 2.5 copy-start.24
  746.7 118.6 %reduce-scatter.15.cloned.1.call-start = ((), (), s32[]{:S(2)}) async-start(), calls=%async_computation.23 | async-start | bytes 3932160 | tf_op jit(solution)/shard_map/reduce_scatter | solution.py:168
  827.6 84.6 %all-gather.29.cloned.1.call-start = ((), (), s32[]{:S(2)}) async-start(), calls=%async_computation.24 | async-start | bytes 3932160 | tf_op jit(solution)/shard_map/all_gather | solution.py:176
  865.3 4.1 copy-start.2
  865.3 4.1 copy-start.10
  873.0 169.9 %reduce-scatter.17.cloned.1.call-start = ((), (), s32[]{:S(2)}) async-start(), calls=%async_computation.25 | async-start | bytes 3932160 | tf_op jit(solution)/shard_map/reduce_scatter | solution.py:220
  918.8 8.1 copy-start.12
  918.8 18.6 slice-start
  918.8 18.5 slice-start.1
  926.9 10.5 slice-start.2
  926.9 10.5 slice-start.3
  937.4 7.0 copy-start.4
  946.0 2.2 copy-start.30
  948.2 3.0 copy-start.14
  948.2 2.9 copy-start.29
  951.2 3.0 copy-start.13
  951.2 3.0 copy-start.31
  958.5 173.1 %all-reduce.3.cloned.1.call-start = ((), (), s32[]{:S(2)}) async-start(), calls=%async_computation.32 | async-start | bytes 196608 | tf_op jit(solution)/shard_map/psum | solution.py:236
  961.7 280.8 %reduce-scatter.23.cloned.1.call-start = ((), (), s32[]{:S(2)}) async-start(), calls=%async_computation.28 | async-start | bytes 8912896 | tf_op jit(solution)/shard_map/reduce_scatter | solution.py:229
  970.8 381.2 %reduce-scatter.21.cloned.1.call-start = ((), (), s32[]{:S(2)}) async-start(), calls=%async_computation.27 | async-start | bytes 8912896 | tf_op jit(solution)/shard_map/reduce_scatter | solution.py:228
  979.6 481.9 %reduce-scatter.19.cloned.1.call-start = ((), (), s32[]{:S(2)}) async-start(), calls=%async_computation.26 | async-start | bytes 8912896 | tf_op jit(solution)/shard_map/reduce_scatter | solution.py:227
  987.1 584.1 %reduce-scatter.25.cloned.1.call-start = ((), (), s32[]{:S(2)}) async-start(), calls=%async_computation.29 | async-start | bytes 8912896 | tf_op jit(solution)/shard_map/reduce_scatter | solution.py:230
  996.0 1.8 copy-start.33
  996.0 913.0 %reduce-scatter.29.cloned.1.call-start = ((), (), s32[]{:S(2)}) async-start(), calls=%async_computation.31 | async-start | bytes 35651584 | tf_op jit(solution)/shard_map/reduce_scatter | solution.py:232
  1021.0 1225.1 %reduce-scatter.27.cloned.1.call-start = ((), (), s32[]{:S(2)}) async-start(), calls=%async_computation.30 | async-start | bytes 35651584 | tf_op jit(solution)/shard_map/reduce_scatter | solution.py:231
  1112.8 2.4 copy-start.27
  (16 other events, 18.6 us)
Sparse Core Ops, SparseCore 0:
  56.1 39.4 all-gather.10
  97.7 50.6 all-gather.14
  150.6 49.0 all-gather.16
  201.7 49.0 all-gather.12
  252.8 51.7 all-gather.18
  312.2 63.8 reduce-scatter.10
  381.1 39.0 all-gather.20
  422.5 126.8 all-gather.22
  551.8 128.5 all-gather.24
  701.5 35.7 reduce-scatter.12
  746.8 39.0 all-gather.26
  827.7 37.5 reduce-scatter.14
  873.1 39.0 all-gather.28
  958.7 37.5 reduce-scatter.16
  1004.3 127.3 all-reduce.2
  1136.7 105.7 reduce-scatter.22
  1247.5 104.4 reduce-scatter.20
  1357.0 104.3 reduce-scatter.18
  1466.7 104.5 reduce-scatter.24
  1576.5 332.4 reduce-scatter.28
  1914.4 331.6 reduce-scatter.26
where the time goes:
time: 2270 us; the launch traced here: 2260 us
  waiting for transfers between devices  1830 us (81%)
  matrix products  226 us (10%)
  blocking collectives  80.8 us (4%)
  local copies, waits for them, and re-layouts  61.9 us (3%)
  other arithmetic  43.5 us (2%)
    reduce_scatter x1, waiting for transfers between devices, shards(): lax.psum_scatter(grad_w_down, 'dp', scatter_dimension=1, tiled=True)  338 us
    reduce_scatter x1, waiting for transfers between devices, shards(): lax.psum_scatter(grad_w_up, 'dp', scatter_dimension=0, tiled=True)  337 us
    all_gather x1, waiting for transfers between devices, shards(): lax.all_gather(w_up, 'dp', axis=0, tiled=True)  129 us
    all_gather x1, waiting for transfers between devices, shards(): lax.all_gather(w_down, 'dp', axis=1, tiled=True)  113 us
    reduce_scatter x1, waiting for transfers between devices, shards(): lax.psum_scatter(grad_w_value, 'dp', scatter_dimension=0, tiled=True)  111 us
    reduce_scatter x1, waiting for transfers between devices, shards(): lax.psum_scatter(grad_w_out, 'dp', scatter_dimension=1, tiled=True)  110 us
    reduce_scatter x1, waiting for transfers between devices, shards(): lax.psum_scatter(grad_w_key, 'dp', scatter_dimension=0, tiled=True)  110 us
    reduce_scatter x1, waiting for transfers between devices, shards(): lax.psum_scatter(grad_w_query, 'dp', scatter_dimension=0, tiled=True)  109 us
  transfers between devices with their start and end apart: 21, of which 20 were waited for; matrix products, arithmetic and copies ran while one was open for 7% of the time, Pallas kernels for 0%

commit v1 on v0

--- a/solution.py
+++ b/solution.py
@@ -124,7 +124,12 @@
     )
     mixed_heads = mixed_heads.astype(jnp.bfloat16).reshape(seq_len, head_cols)
     attn_part = jnp.dot(mixed_heads, out_full, preferred_element_type=jnp.float32)
-    attended = lax.psum_scatter(attn_part, "tensor", scatter_dimension=0, tiled=True) + b_out
+    attended = (
+        lax.psum_scatter(
+            attn_part.astype(jnp.bfloat16), "tensor", scatter_dimension=0, tiled=True
+        ).astype(jnp.float32)
+        + b_out
+    )
     hidden, normed_first, inverse_first = norm_forward(
         own_rows.astype(jnp.float32) + attended, gain_first, shift_first
     )
@@ -224,12 +229,12 @@
     returned = lax.all_to_all(grad_sent, "dp", split_axis=2, concat_axis=0, tiled=True)
     grad_inputs = jnp.zeros_like(returned).at[dealing].set(returned)
     weight_sums = (
-        lax.psum_scatter(grad_w_query, "dp", scatter_dimension=0, tiled=True),
-        lax.psum_scatter(grad_w_key, "dp", scatter_dimension=0, tiled=True),
-        lax.psum_scatter(grad_w_value, "dp", scatter_dimension=0, tiled=True),
-        lax.psum_scatter(grad_w_out, "dp", scatter_dimension=1, tiled=True),
-        lax.psum_scatter(grad_w_up, "dp", scatter_dimension=0, tiled=True),
-        lax.psum_scatter(grad_w_down, "dp", scatter_dimension=1, tiled=True),
+        lax.psum_scatter(grad_w_query.astype(jnp.bfloat16), "dp", scatter_dimension=0, tiled=True).astype(jnp.float32),
+        lax.psum_scatter(grad_w_key.astype(jnp.bfloat16), "dp", scatter_dimension=0, tiled=True).astype(jnp.float32),
+        lax.psum_scatter(grad_w_value.astype(jnp.bfloat16), "dp", scatter_dimension=0, tiled=True).astype(jnp.float32),
+        lax.psum_scatter(grad_w_out.astype(jnp.bfloat16), "dp", scatter_dimension=1, tiled=True).astype(jnp.float32),
+        lax.psum_scatter(grad_w_up.astype(jnp.bfloat16), "dp", scatter_dimension=0, tiled=True).astype(jnp.float32),
+        lax.psum_scatter(grad_w_down.astype(jnp.bfloat16), "dp", scatter_dimension=1, tiled=True).astype(jnp.float32),
     )
     full_cols = b_query.shape[0]
     full_up = b_up.shape[0]

time: 2270 us -> 1800 us (0.79)
  waiting for transfers between devices: 1830 us -> 1360 us
  blocking collectives: 80.8 us -> 43.2 us
  local copies, waits for them, and re-layouts: 61.9 us -> 90.4 us
    reduce_scatter x7 -> x5, waiting for transfers between devices: 1180 us -> 426 us  [the longest x1 178 us: shards(): lax.psum_scatter(grad_w_up.astype(jnp.bfloat16), 'dp', scatter_dimension=...]
    unnamed x21 -> x23, waiting for transfers between devices: 4.06 us -> 165 us
    psum x1, waiting for transfers between devices: 13.6 us -> 129 us  [shards(): lax.psum((place_slice(grad_query_bias, full_cols, tensor_index * head_col...]
    all_to_all x1 -> x0, blocking collectives: 37.5 us -> none  [shards(): lax.all_to_all(grad_sent, 'dp', split_axis=2, concat_axis=0, tiled=True)]
    unnamed x98 -> x104, local copies, waits for them, and re-layouts: 40.9 us -> 68.9 us
  transfers between devices with their start and end apart: 21 -> 22, of which waited for: 20 -> 19; matrix products, arithmetic and copies ran while one was open for 7% -> 11% of each run, Pallas kernels for 0% -> 0%
where the time goes in v1:
time: 1800 us; the launch traced here: 1790 us
  waiting for transfers between devices  1360 us (76%)
  matrix products  222 us (12%)
  local copies, waits for them, and re-layouts  90.4 us (5%)
  other arithmetic  54.9 us (3%)
  blocking collectives  43.2 us (2%)
    reduce_scatter x1, waiting for transfers between devices, shards(): lax.psum_scatter(grad_w_up.astype(jnp.bfloat16), 'dp', scatter_dimension=...  178 us
    unnamed x23, waiting for transfers between devices  165 us
    psum x1, waiting for transfers between devices, shards(): lax.psum((place_slice(grad_query_bias, full_cols, tensor_index * head_col...  129 us
    all_gather x1, waiting for transfers between devices, shards(): lax.all_gather(w_up, 'dp', axis=0, tiled=True)  129 us
    all_gather x1, waiting for transfers between devices, shards(): lax.all_gather(w_down, 'dp', axis=1, tiled=True)  113 us
    reduce_scatter x1, waiting for transfers between devices, shards(): lax.psum_scatter(grad_w_query.astype(jnp.bfloat16), 'dp', scatter_dimensi...  74.3 us
    reduce_scatter x1, waiting for transfers between devices, shards(): lax.psum_scatter(grad_w_key.astype(jnp.bfloat16), 'dp', scatter_dimension...  73.4 us
    dot_general x6, matrix products, contract_rows(): lax.dot_general(left, right, (((0,), (0,)), ((), ())), preferred_element_...  71.6 us
  transfers between devices with their start and end apart: 22, of which 19 were waited for; matrix products, arithmetic and copies ran while one was open for 11% of the time, Pallas kernels for 0%

profile of v1, /device:TPU:0, one launch (start us, length us, event | category | flops | bytes accessed | tf_op | source)
XLA Modules:
  0.0 1793.6 jit_solution(18121387637887489258)
XLA Ops:
  11.5 43.2 %all_to_all.21 = bf16[16,1,20,2048]{3,2,1,0:T(8,128)(2,1)S(1)} all-to-all(bf16[16,1,20,2048]{3,2,1,0:T(8,128)(2,1)S(1)} %fusion.28), channel_id=1, replica_groups=mesh['dp'=16,'tensor'=2] {'dp'}, dimensions={0} | all-to-all | bytes 2621440 | tf_op jit(solution)/shard_map/all_to_all | solution.py:82
  62.5 33.0 %all-gather.11.cloned.1.call-done = bf16[640,2048]{1,0:T(8,128)(2,1)} async-done(((bf16[320,2048]{1,0:T(8,128)(2,1)}), bf16[640,2048]{1,0:T(8,128)(2,1)}) %all-gather.11.cloned.1.call-update) | async-done | bytes 2621456 | tf_op jit(solution)/shard_map/all_gather | solution.py:105
  95.5 52.9 %all-gather.15.cloned.1.call-done = bf16[2048,1024]{1,0:T(8,128)(2,1)} async-done(((bf16[128,1024]{1,0:T(8,128)(2,1)}), bf16[2048,1024]{1,0:T(8,128)(2,1)}) %all-gather.15.cloned.1.call-update) | async-done | bytes 4194320 | tf_op jit(solution)/shard_map/all_gather | solution.py:91
  148.4 5.9 add_convert_fusion.3
  155.3 44.4 %all-gather.17.cloned.1.call-done = bf16[2048,1024]{1,0:T(8,128)(2,1)} async-done(((bf16[128,1024]{1,0:T(8,128)(2,1)}), bf16[2048,1024]{1,0:T(8,128)(2,1)}) %all-gather.17.cloned.1.call-update) | async-done | bytes 4194320 | tf_op jit(solution)/shard_map/all_gather | solution.py:92
  199.7 6.9 convolution_convert_fusion.10
  211.5 4.7 copy-done
  217.9 32.9 %all-gather.13.cloned.1.call-done = bf16[2048,1024]{1,0:T(8,128)(2,1)} async-done(((bf16[128,1024]{1,0:T(8,128)(2,1)}), bf16[2048,1024]{1,0:T(8,128)(2,1)}) %all-gather.13.cloned.1.call-update) | async-done | bytes 4194320 | tf_op jit(solution)/shard_map/all_gather | solution.py:93
  250.8 6.0 fusion.29
  261.3 43.2 %all-gather.19.cloned.1.call-done = bf16[1024,2048]{1,0:T(8,128)(2,1)} async-done(((bf16[1024,128]{1,0:T(8,128)(2,1)}), bf16[1024,2048]{1,0:T(8,128)(2,1)}) %all-gather.19.cloned.1.call-update) | async-done | bytes 4194320 | tf_op jit(solution)/shard_map/all_gather | solution.py:94
  304.6 6.6 convolution_convert_fusion.6
  311.2 35.8 %reduce-scatter.15.cloned.1.call-done = bf16[320,2048]{1,0:T(8,128)(2,1)} async-done(((bf16[640,2048]{1,0:T(8,128)(2,1)}), bf16[320,2048]{1,0:T(8,128)(2,1)}) %reduce-scatter.15.cloned.1.call-update) | async-done | bytes 1310736 | tf_op jit(solution)/shard_map/reduce_scatter | solution.py:128
  353.2 37.6 %all-gather.21.cloned.1.call-done = bf16[640,2048]{1,0:T(8,128)(2,1)} async-done(((bf16[320,2048]{1,0:T(8,128)(2,1)}), bf16[640,2048]{1,0:T(8,128)(2,1)}) %all-gather.21.cloned.1.call-update) | async-done | bytes 2621456 | tf_op jit(solution)/shard_map/all_gather | solution.py:136
  390.8 129.3 %all-gather.23.cloned.1.call-done = bf16[2048,4096]{1,0:T(8,128)(2,1)} async-done(((bf16[128,4096]{1,0:T(8,128)(2,1)}), bf16[2048,4096]{1,0:T(8,128)(2,1)}) %all-gather.23.cloned.1.call-update) | async-done | bytes 16777232 | tf_op jit(solution)/shard_map/all_gather | solution.py:95
  520.1 17.7 fusion.42
  537.8 113.3 %all-gather.25.cloned.1.call-done = bf16[4096,2048]{1,0:T(8,128)(2,1)} async-done(((bf16[4096,128]{1,0:T(8,128)(2,1)}), bf16[4096,2048]{1,0:T(8,128)(2,1)}) %all-gather.25.cloned.1.call-update) | async-done | bytes 16777232 | tf_op jit(solution)/shard_map/all_gather | solution.py:96
  651.1 21.0 %convolution_convert_fusion.8 = bf16[640,2048]{1,0:T(8,128)(2,1)} fusion(bf16[4096,2048]{1,0:T(8,128)(2,1)} %all-gather.25.cloned.1.call-done, f32[640,4096]{1,0:T(8,128)} %fusion.42, f32[4096]{0:T(1024)S(1)} %dynamic_slice.19), kind=kOutput, calls=%fused_computation.40 | convolution fusion | flops 10764943360 | bytes 29900800 | tf_op jit(solution)/shard_map/dot_general | solution.py:139
  672.2 35.9 %reduce-scatter.17.cloned.1.call-done = bf16[320,2048]{1,0:T(8,128)(2,1)} async-done(((bf16[640,2048]{1,0:T(8,128)(2,1)}), bf16[320,2048]{1,0:T(8,128)(2,1)}) %reduce-scatter.17.cloned.1.call-update) | async-done | bytes 1310736 | tf_op jit(solution)/shard_map/reduce_scatter | solution.py:141
  718.0 39.0 %all-gather.27.cloned.1.call-done = bf16[640,2048]{1,0:T(8,128)(2,1)} async-done(((bf16[320,2048]{1,0:T(8,128)(2,1)}), bf16[640,2048]{1,0:T(8,128)(2,1)}) %all-gather.27.cloned.1.call-update) | async-done | bytes 2621456 | tf_op jit(solution)/shard_map/all_gather | solution.py:165
  756.9 25.1 %convert_reduce_fusion = (f32[4096]{0:T(1024)}, bf16[640,4096]{1,0:T(8,128)(2,1)}) fusion(f32[640,4096]{1,0:T(8,128)} %fusion.42, f32[4096]{0:T(1024)S(1)} %dynamic_slice.19, bf16[640,2048]{1,0:T(8,128)(2,1)} %all-gather.27.cloned.1.call-done, bf16[4096,2048]{1,0:T(8,128)(2,1)} %all-gather.25.cloned.1.call-done), kind=kOutput, calls=%fused_computation.20 | convolution fusion | flops 10797707264 | bytes 35160064 | tf_op jit(solution)/shard_map/dot_general | solution.py:39
  782.1 17.2 convolution_convert_fusion.7
  799.5 37.5 %reduce-scatter.19.cloned.1.call-done = bf16[320,2048]{1,0:T(8,128)(2,1)} async-done(((bf16[640,2048]{1,0:T(8,128)(2,1)}), bf16[320,2048]{1,0:T(8,128)(2,1)}) %reduce-scatter.19.cloned.1.call-update) | async-done | bytes 1310736 | tf_op jit(solution)/shard_map/reduce_scatter | solution.py:173
  837.0 4.4 multiply_reduce_fusion.1
  845.5 39.1 %all-gather.29.cloned.1.call-done = bf16[640,2048]{1,0:T(8,128)(2,1)} async-done(((bf16[320,2048]{1,0:T(8,128)(2,1)}), bf16[640,2048]{1,0:T(8,128)(2,1)}) %all-gather.29.cloned.1.call-update) | async-done | bytes 2621456 | tf_op jit(solution)/shard_map/all_gather | solution.py:181
  884.6 5.9 convolution_convert_fusion.9
  891.2 7.1 convert_reduce_fusion.4
  898.4 10.4 multiply_reduce_fusion
  908.8 7.0 multiply_convert_fusion
  925.6 4.4 add_convert_fusion
  930.3 7.6 convolution_convert_fusion.2
  937.8 6.4 copy.84
  944.3 6.8 convolution_convert_fusion.3
  952.5 6.9 convolution_convert_fusion.4
  959.4 6.9 convolution_convert_fusion.5
  968.2 24.4 %convolution_convert_fusion = bf16[4096,2048]{1,0:T(8,128)(2,1)} fusion(bf16[640,2048]{1,0:T(8,128)(2,1)S(1)} %copy-done.35, f32[640,4096]{1,0:T(8,128)} %fusion.42, f32[4096]{0:T(1024)S(1)} %dynamic_slice.19), kind=kOutput, calls=%fused_computation.2 | convolution fusion | flops 10772021248 | bytes 29900800 | tf_op jit(solution)/shard_map/dot_general | solution.py:33
  992.6 21.1 %copy.86 = bf16[4096,2048]{0,1:T(8,128)(2,1)} copy(bf16[4096,2048]{1,0:T(8,128)(2,1)} %convolution_convert_fusion) | data formatting | bytes 33554432
  1015.5 18.9 %convolution_convert_fusion.1 = bf16[2048,4096]{1,0:T(8,128)(2,1)} fusion(bf16[640,2048]{1,0:T(8,128)(2,1)S(1)} %copy-done.34, bf16[640,4096]{1,0:T(8,128)(2,1)} %get-tuple-element.71), kind=kOutput, calls=%fused_computation.3 | convolution fusion | flops 10745806848 | bytes 24641536 | tf_op jit(solution)/shard_map/dot_general | solution.py:33
  1040.4 9.4 reduce.5
  1049.8 4.5 reshape.194
  1054.4 5.9 all-to-all-start.1
  1064.4 63.7 %reduce-scatter.27.cloned.1.call-done = bf16[128,1024]{1,0:T(8,128)(2,1)} async-done(((bf16[2048,1024]{1,0:T(8,128)(2,1)}), bf16[128,1024]{1,0:T(8,128)(2,1)}) %reduce-scatter.27.cloned.1.call-update) | async-done | bytes 262160 | tf_op jit(solution)/shard_map/reduce_scatter | solution.py:234
  1129.9 73.4 %reduce-scatter.25.cloned.1.call-done = bf16[128,1024]{1,0:T(8,128)(2,1)} async-done(((bf16[2048,1024]{1,0:T(8,128)(2,1)}), bf16[128,1024]{1,0:T(8,128)(2,1)}) %reduce-scatter.25.cloned.1.call-update) | async-done | bytes 262160 | tf_op jit(solution)/shard_map/reduce_scatter | solution.py:233
  1205.0 74.3 %reduce-scatter.23.cloned.1.call-done = bf16[128,1024]{1,0:T(8,128)(2,1)} async-done(((bf16[2048,1024]{1,0:T(8,128)(2,1)}), bf16[128,1024]{1,0:T(8,128)(2,1)}) %reduce-scatter.23.cloned.1.call-update) | async-done | bytes 262160 | tf_op jit(solution)/shard_map/reduce_scatter | solution.py:232
  1281.1 4.5 reshape.195
  1285.7 8.7 bitcast_reduce_fusion
  1299.9 161.2 %reduce-scatter.33.cloned.1.call-done = bf16[128,4096]{1,0:T(8,128)(2,1)} async-done(((bf16[2048,4096]{1,0:T(8,128)(2,1)}), bf16[128,4096]{1,0:T(8,128)(2,1)}) %reduce-scatter.33.cloned.1.call-update) | async-done | bytes 1048592
  1464.1 178.5 %reduce-scatter.29.cloned.1.call-done = bf16[128,4096]{1,0:T(8,128)(2,1)} async-done(((bf16[2048,4096]{1,0:T(8,128)(2,1)}), bf16[128,4096]{1,0:T(8,128)(2,1)}) %reduce-scatter.29.cloned.1.call-update) | async-done | bytes 1048592 | tf_op jit(solution)/shard_map/reduce_scatter | solution.py:236
  1645.3 129.5 %all-reduce.3.cloned.1.call-done = (f32[2048]{0:T(1024)}, f32[2048]{0:T(1024)}, f32[2048]{0:T(1024)}, f32[2048]{0:T(1024)}, f32[2048]{0:T(1024)}, /*index=5*/f32...) async-done(((f32[2048]{0:T(1024)}, f32[2048]{0:T(1024)}, f32[2048]{0:T(1024)}, f32[2048]{0:T(1024)}, f32[2048]{0:T(1024)}, /*index=5*/f32[8192]{0:T(1024)}, ...) | async-done | bytes 98320 | tf_op jit(solution)/shard_map/psum | solution.py:241
  (202 shorter events, 96.3 us)
Async XLA Ops:
  7.2 88.4 %all-gather.11.cloned.1.call-start = ((), (), s32[]{:S(2)}) async-start(), calls=%async_computation.12 | async-start | bytes 3932160 | tf_op jit(solution)/shard_map/all_gather | solution.py:105
  54.7 3.9 copy-start.36
  54.7 5.8 copy-start.30
  54.7 6.5 copy-start.37
  56.0 92.5 %all-gather.15.cloned.1.call-start = ((), (), s32[]{:S(2)}) async-start(), calls=%async_computation.14 | async-start | bytes 4456448 | tf_op jit(solution)/shard_map/all_gather | solution.py:91
  56.7 143.0 %all-gather.17.cloned.1.call-start = ((), (), s32[]{:S(2)}) async-start(), calls=%async_computation.15 | async-start | bytes 4456448 | tf_op jit(solution)/shard_map/all_gather | solution.py:92
  57.5 193.3 %all-gather.13.cloned.1.call-start = ((), (), s32[]{:S(2)}) async-start(), calls=%async_computation.13 | async-start | bytes 4456448 | tf_op jit(solution)/shard_map/all_gather | solution.py:93
  58.0 246.5 %all-gather.19.cloned.1.call-start = ((), (), s32[]{:S(2)}) async-start(), calls=%async_computation.16 | async-start | bytes 4456448 | tf_op jit(solution)/shard_map/all_gather | solution.py:94
  58.6 288.5 %reduce-scatter.15.cloned.1.call-start = ((), (), s32[]{:S(2)}) async-start(), calls=%async_computation.17 | async-start | bytes 3932160 | tf_op jit(solution)/shard_map/reduce_scatter | solution.py:128
  155.3 53.1 %copy-start.9 = (bf16[640,1024]{0,1:T(8,128)(2,1)}, bf16[640,1024]{0,1:T(8,128)(2,1)S(1)}, u32[]{:S(2)}) copy-start(bf16[640,1024]{0,1:T(8,128)(2,1)S(1)} %copy.89) | copy-start | bytes 3932164
  208.4 3.1 copy-start.5
  211.4 4.7 copy-start
  216.1 34.7 %dynamic-slice-start = ((f32[2048]{0:T(1024)}, s32[]{:T(128)}), f32[1024]{0:T(1024)S(1)}, s32[]{:S(2)}) async-start(f32[2048]{0:T(1024)} %param.26, s32[]{:T(128)} %select_n.41), calls=%async_computation.37 | async-start | bytes 8704 | tf_op jit(solution)/shard_map/dynamic_slice | solution.py:103
  250.8 7.1 copy-start.1
  261.3 43.3 %copy-start.38 = (bf16[8,128,640]{2,1,0:T(8,128)(2,1)}, bf16[8,128,640]{2,1,0:T(8,128)(2,1)S(1)}, u32[]{:S(2)}) copy-start(bf16[8,128,640]{2,1,0:T(8,128)(2,1)S(1)} %fusion.24) | copy-start | bytes 3932164
  311.1 36.0 %copy-start.2 = (bf16[320,2048]{1,0:T(8,128)(2,1)S(1)}, bf16[320,2048]{1,0:T(8,128)(2,1)}, u32[]{:S(2)}) copy-start(bf16[320,2048]{1,0:T(8,128)(2,1)} %reshape.155) | copy-start | bytes 3932164
  311.1 36.0 %copy-start.17 = (f32[2048]{0:T(1024)S(1)}, f32[2048]{0:T(1024)}, u32[]{:S(2)}) copy-start(f32[2048]{0:T(1024)} %param.28) | copy-start | bytes 24580
  311.2 38.6 %copy-start.18 = (f32[2048]{0:T(1024)S(1)}, f32[2048]{0:T(1024)}, u32[]{:S(2)}) copy-start(f32[2048]{0:T(1024)} %param.29) | copy-start | bytes 24580
  311.2 38.6 %copy-start.20 = (f32[2048]{0:T(1024)S(1)}, f32[2048]{0:T(1024)}, u32[]{:S(2)}) copy-start(f32[2048]{0:T(1024)} %param.30) | copy-start | bytes 24580
  311.2 79.6 %all-gather.21.cloned.1.call-start = ((), (), s32[]{:S(2)}) async-start(), calls=%async_computation.18 | async-start | bytes 3932160 | tf_op jit(solution)/shard_map/all_gather | solution.py:136
  351.6 168.5 %all-gather.23.cloned.1.call-start = ((), (), s32[]{:S(2)}) async-start(), calls=%async_computation.19 | async-start | bytes 17825792 | tf_op jit(solution)/shard_map/all_gather | solution.py:95
  352.4 298.7 %all-gather.25.cloned.1.call-start = ((), (), s32[]{:S(2)}) async-start(), calls=%async_computation.20 | async-start | bytes 17825792 | tf_op jit(solution)/shard_map/all_gather | solution.py:96
  353.1 354.9 %reduce-scatter.17.cloned.1.call-start = ((), (), s32[]{:S(2)}) async-start(), calls=%async_computation.21 | async-start | bytes 3932160 | tf_op jit(solution)/shard_map/reduce_scatter | solution.py:141
  672.1 35.9 %copy-start.25 = (f32[2048]{0:T(1024)S(1)}, f32[2048]{0:T(1024)}, u32[]{:S(2)}) copy-start(f32[2048]{0:T(1024)} %param.34) | copy-start | bytes 24580
  672.1 84.8 %all-gather.27.cloned.1.call-start = ((), (), s32[]{:S(2)}) async-start(), calls=%async_computation.22 | async-start | bytes 3932160 | tf_op jit(solution)/shard_map/all_gather | solution.py:165
  717.8 119.3 %reduce-scatter.19.cloned.1.call-start = ((), (), s32[]{:S(2)}) async-start(), calls=%async_computation.23 | async-start | bytes 3932160 | tf_op jit(solution)/shard_map/reduce_scatter | solution.py:173
  799.3 85.3 %all-gather.29.cloned.1.call-start = ((), (), s32[]{:S(2)}) async-start(), calls=%async_computation.24 | async-start | bytes 3932160 | tf_op jit(solution)/shard_map/all_gather | solution.py:181
  837.0 4.4 copy-start.4
  837.0 4.4 copy-start.12
  845.4 189.1 %reduce-scatter.21.cloned.1.call-start = ((), (), s32[]{:S(2)}) async-start(), calls=%async_computation.25 | async-start | bytes 3932160 | tf_op jit(solution)/shard_map/reduce_scatter | solution.py:225
  891.2 7.1 copy-start.14
  891.2 17.6 slice-start
  891.2 17.6 slice-start.1
  898.3 10.5 slice-start.2
  898.3 10.5 slice-start.3
  908.8 7.0 copy-start.6
  919.6 3.0 copy-start.15
  922.6 3.0 copy-start.33
  930.1 132.4 %reduce-scatter.31.cloned.1.call-start = ((), (), s32[]{:S(2)}) async-start(), calls=%async_computation.30 | async-start | bytes 4456448
  944.3 183.8 %reduce-scatter.27.cloned.1.call-start = ((), (), s32[]{:S(2)}) async-start(), calls=%async_computation.28 | async-start | bytes 4456448 | tf_op jit(solution)/shard_map/reduce_scatter | solution.py:234
  951.2 252.0 %reduce-scatter.25.cloned.1.call-start = ((), (), s32[]{:S(2)}) async-start(), calls=%async_computation.27 | async-start | bytes 4456448 | tf_op jit(solution)/shard_map/reduce_scatter | solution.py:233
  959.4 320.0 %reduce-scatter.23.cloned.1.call-start = ((), (), s32[]{:S(2)}) async-start(), calls=%async_computation.26 | async-start | bytes 4456448 | tf_op jit(solution)/shard_map/reduce_scatter | solution.py:232
  966.4 494.6 %reduce-scatter.33.cloned.1.call-start = ((), (), s32[]{:S(2)}) async-start(), calls=%async_computation.31 | async-start | bytes 17825792
  1013.8 628.8 %reduce-scatter.29.cloned.1.call-start = ((), (), s32[]{:S(2)}) async-start(), calls=%async_computation.29 | async-start | bytes 17825792 | tf_op jit(solution)/shard_map/reduce_scatter | solution.py:236
  1049.8 10.5 copy-start.8
  1054.3 6.8 copy-start.24
  1054.4 226.8 %all-to-all-start.1 = ((bf16[16,2,20480]{2,1,0:T(2,128)(2,1)}), bf16[16,2,20480]{2,1,0:T(2,128)(2,1)}, u32[]{:S(2)}, u32[]{:S(2)}) async-start(bf16[16,2,20480]{2,1,0:T(2,128)(2,1)} %reshape.194), calls=%async_computation.5 | async-start | bytes 2621440 | tf_op jit(solution)/shard_map/all_to_all | solution.py:229
  1060.3 714.5 %all-reduce.3.cloned.1.call-start = ((), (), s32[]{:S(2)}) async-start(), calls=%async_computation.32 | async-start | bytes 196608 | tf_op jit(solution)/shard_map/psum | solution.py:241
  (18 other events, 28.2 us)
Sparse Core Ops, SparseCore 0:
  56.1 39.4 all-gather.10
  97.7 50.6 all-gather.14
  150.6 49.0 all-gather.16
  201.7 49.0 all-gather.12
  252.8 51.7 all-gather.18
  311.3 35.7 reduce-scatter.14
  351.8 39.0 all-gather.20
  393.2 126.8 all-gather.22
  522.5 128.5 all-gather.24
  672.2 35.7 reduce-scatter.16
  717.9 39.0 all-gather.26
  799.4 37.5 reduce-scatter.18
  845.5 39.0 all-gather.28
  930.2 37.5 reduce-scatter.20
  971.5 72.7 reduce-scatter.30
  1048.5 79.5 reduce-scatter.26
  1131.8 71.4 reduce-scatter.24
  1207.4 71.8 reduce-scatter.22
  1283.5 177.5 reduce-scatter.32
  1465.0 177.5 reduce-scatter.28
  1650.7 124.0 all-reduce.2

commit v2 on v1

--- a/solution.py
+++ b/solution.py
@@ -3,6 +3,8 @@
 import jax
 import jax.numpy as jnp
 from jax import lax
+from jax.experimental import pallas as pl
+from jax.experimental.pallas import tpu as pltpu
 from jax.sharding import PartitionSpec as P
 
 HEAD_DIM = 128
@@ -53,6 +55,372 @@
     return lax.dynamic_update_slice_in_dim(
         jnp.zeros((full_size,), jnp.float32), local_sum, offset, 0
     )
+
+MESH = pl.DeviceIdType.MESH
+TILE = 1024
+
+
+def place():
+    dp, tensor = lax.axis_index("dp"), lax.axis_index("tensor")
+    return dp // 4, (dp // 2) % 2, dp % 2, tensor
+
+
+def device_of(plane, across, core, tensor):
+    return ((plane * 2 + across) * 2 + core, tensor)
+
+
+def enter(peers):
+    barrier = pltpu.get_barrier_semaphore()
+    for peer in peers:
+        pl.semaphore_signal(barrier, inc=1, device_id=peer, device_id_type=MESH)
+    pl.semaphore_wait(barrier, len(peers))
+
+
+def gather_kernel(planes, widths, *refs):
+    count = len(widths)
+    shard_refs, full_refs = refs[:count], refs[count : 2 * count]
+    local_sem, plane_send, plane_recv, x_send, x_recv, core_send, core_recv = refs[2 * count :]
+    plane, across, core, tensor = place()
+    far = [lax.rem(plane + k, planes) for k in range(planes)]
+    near = [lax.rem(plane + planes - k, planes) for k in range(planes)]
+    x_peer = device_of(plane, 1 - across, core, tensor)
+    core_peer = device_of(plane, across, 1 - core, tensor)
+    enter([device_of(far[k], across, core, tensor) for k in range(1, planes)] + [x_peer, core_peer])
+    tiles = [(i, start) for i, width in enumerate(widths) for start in range(0, width, TILE)]
+    total = len(tiles)
+
+    def view(c, *at):
+        i, start = tiles[c]
+        return full_refs[i].at[(*at, slice(None), pl.ds(start, TILE))]
+
+    def own(c):
+        i, start = tiles[c]
+        return shard_refs[i].at[:, pl.ds(start, TILE)]
+
+    def to_plane(c, k):
+        return pltpu.make_async_remote_copy(
+            own(c), view(c, plane, across, core), plane_send.at[c, k - 1], plane_recv.at[c, k - 1],
+            device_id=device_of(far[k], across, core, tensor), device_id_type=MESH,
+        )
+
+    def from_plane(c, k):
+        return pltpu.make_async_remote_copy(
+            own(c), view(c, near[k], across, core), plane_send.at[c, k - 1], plane_recv.at[c, k - 1],
+            device_id=device_of(far[k], across, core, tensor), device_id_type=MESH,
+        )
+
+    def keep(c):
+        return pltpu.make_async_copy(own(c), view(c, plane, across, core), local_sem.at[c])
+
+    def to_x(c, side):
+        part = view(c, slice(None), side, core)
+        return pltpu.make_async_remote_copy(
+            part, part, x_send.at[c], x_recv.at[c], device_id=x_peer, device_id_type=MESH
+        )
+
+    def to_core(c, side):
+        part = view(c, slice(None), slice(None), side)
+        return pltpu.make_async_remote_copy(
+            part, part, core_send.at[c], core_recv.at[c], device_id=core_peer, device_id_type=MESH
+        )
+
+    def begin(c):
+        keep(c).start()
+        for k in range(1, planes):
+            to_plane(c, k).start()
+
+    ahead = 3
+    for c in range(min(ahead, total)):
+        begin(c)
+    for c in range(total):
+        keep(c).wait()
+        for k in range(1, planes):
+            from_plane(c, k).wait_recv()
+        to_x(c, across).start()
+        if c + ahead < total:
+            begin(c + ahead)
+        if c > 0:
+            to_x(c - 1, 1 - across).wait_recv()
+            to_core(c - 1, core).start()
+    to_x(total - 1, 1 - across).wait_recv()
+    to_core(total - 1, core).start()
+    for c in range(total):
+        for k in range(1, planes):
+            to_plane(c, k).wait_send()
+        to_x(c, across).wait_send()
+        to_core(c, core).wait_send()
+        to_core(c, 1 - core).wait_recv()
+
+
+def gather_weights(shard_list):
+    planes = lax.axis_size("dp") // 4
+    widths = [shard.shape[1] for shard in shard_list]
+    total = sum(width // TILE for width in widths)
+    sem = pltpu.SemaphoreType.DMA
+    full = pl.pallas_call(
+        partial(gather_kernel, planes, widths),
+        out_shape=[
+            jax.ShapeDtypeStruct((planes, 2, 2, *shard.shape), jnp.bfloat16) for shard in shard_list
+        ],
+        in_specs=[pl.BlockSpec(memory_space=pl.ANY)] * len(shard_list),
+        out_specs=[pl.BlockSpec(memory_space=pl.ANY)] * len(shard_list),
+        scratch_shapes=[
+            sem((total,)), sem((total, planes - 1)), sem((total, planes - 1)),
+            sem((total,)), sem((total,)), sem((total,)), sem((total,)),
+        ],
+        compiler_params=pltpu.CompilerParams(collective_id=0, has_side_effects=True),
+        name="gather_weights",
+    )(*shard_list)
+    return [array.reshape(-1, array.shape[-1]) for array in full]
+
+
+def scatter_kernel(planes, jobs, widths, *refs):
+    lefts, rights = 4, len(widths)
+    left_ref, right_refs, small_ref = refs[0], refs[1 : 1 + rights], refs[1 + rights]
+    outs = refs[2 + rights :]
+    grad_refs, small_out = outs[:rights], outs[rights]
+    left_far, right_fars = outs[rights + 1], outs[rights + 2 : rights + 2 + rights]
+    (
+        left_buf, right_buf, stage, x_land, plane_land, out_buf, small_land,
+        left_sem, right_sem, out_sem, core_send, core_recv, left_send, left_recv,
+        x_send, x_recv, plane_send, plane_recv, small_send, small_recv,
+    ) = outs[2 * rights + 2 :]
+    plane, across, core, tensor = place()
+    tokens = left_ref.shape[-1]
+    far = [lax.rem(plane + k, planes) for k in range(planes)]
+    x_peer = device_of(plane, 1 - across, core, tensor)
+    core_peer = device_of(plane, across, 1 - core, tensor)
+    y_peer = device_of(plane, across, core, 1 - tensor)
+    plane_peers = [device_of(far[k], across, core, tensor) for k in range(1, planes)]
+    enter(plane_peers + [x_peer, core_peer, y_peer])
+    total = len(jobs)
+
+    def left_out(a):
+        return pltpu.make_async_remote_copy(
+            left_ref.at[a, :, :, 1 - core], left_far.at[a], left_send.at[a], left_recv.at[a],
+            device_id=core_peer, device_id_type=MESH,
+        )
+
+    def right_out(c):
+        _, i, start = jobs[c]
+        return pltpu.make_async_remote_copy(
+            right_refs[i].at[:, pl.ds(start, TILE)], right_fars[i].at[:, pl.ds(start, TILE)],
+            core_send.at[c], core_recv.at[c], device_id=core_peer, device_id_type=MESH,
+        )
+
+    def left_load(a, slot):
+        mine = [
+            pltpu.make_async_copy(
+                left_ref.at[a, :, side, core], left_buf.at[slot, side, :, :, pl.ds(0, tokens)],
+                left_sem.at[slot, 0, side],
+            )
+            for side in range(2)
+        ]
+        theirs = [
+            pltpu.make_async_copy(
+                left_far.at[a, :, side], left_buf.at[slot, side, :, :, pl.ds(tokens, tokens)],
+                left_sem.at[slot, 1, side],
+            )
+            for side in range(2)
+        ]
+        return mine + theirs
+
+    def right_load(c):
+        _, i, start = jobs[c]
+        slot = c % 2
+        cols = pl.ds(start, TILE)
+        return [
+            pltpu.make_async_copy(
+                right_refs[i].at[:, cols], right_buf.at[slot, pl.ds(0, tokens)], right_sem.at[slot, 0]
+            ),
+            pltpu.make_async_copy(
+                right_fars[i].at[:, cols], right_buf.at[slot, pl.ds(tokens, tokens)], right_sem.at[slot, 1]
+            ),
+        ]
+
+    def x_out(c):
+        return pltpu.make_async_remote_copy(
+            stage.at[c % 3, 1 - across], x_land.at[c], x_send.at[c], x_recv.at[c],
+            device_id=x_peer, device_id_type=MESH,
+        )
+
+    def plane_out(c, k):
+        return pltpu.make_async_remote_copy(
+            x_land.at[c, far[k]], plane_land.at[c, k - 1], plane_send.at[c, k - 1], plane_recv.at[c, k - 1],
+            device_id=plane_peers[k - 1], device_id_type=MESH,
+        )
+
+    def grad_out(c):
+        _, i, start = jobs[c]
+        return pltpu.make_async_copy(
+            out_buf.at[c % 2], grad_refs[i].at[:, pl.ds(start, TILE)], out_sem.at[c % 2]
+        )
+
+    order = []
+    for a, _, _ in jobs:
+        if a not in order:
+            order.append(a)
+    seen = set()
+    for c in range(total):
+        a = jobs[c][0]
+        if a not in seen:
+            seen.add(a)
+            left_out(a).start()
+        right_out(c).start()
+
+    def fetch(c):
+        a = jobs[c][0]
+        if c == 0 or jobs[c - 1][0] != a:
+            left_out(a).wait_recv()
+            for copy in left_load(a, order.index(a) % 2):
+                copy.start()
+        right_out(c).wait_recv()
+        for copy in right_load(c):
+            copy.start()
+
+    def multiply(c):
+        a = jobs[c][0]
+        slot = order.index(a) % 2
+        if c == 0 or jobs[c - 1][0] != a:
+            for copy in left_load(a, slot):
+                copy.wait()
+        for copy in right_load(c):
+            copy.wait()
+        if c + 1 < total:
+            fetch(c + 1)
+        if c >= 3:
+            x_out(c - 3).wait_send()
+
+        @pl.loop(0, TILE // 256)
+        def _(n):
+            cols = pl.ds(pl.multiple_of(n * 256, 256), 256)
+            left = left_buf[slot]
+            result = jnp.dot(
+                left.reshape(-1, left.shape[-1]), right_buf[c % 2, :, cols],
+                preferred_element_type=jnp.float32,
+            ).astype(jnp.bfloat16)
+            stage[c % 3, :, :, :, cols] = result.reshape(*left.shape[:-1], 256)
+
+        x_out(c).start()
+
+    def fold(c):
+        x_out(c).wait_recv()
+
+        @pl.loop(0, planes)
+        def _(p):
+            x_land[c, p] = (
+                x_land[c, p].astype(jnp.float32) + stage[c % 3, across, p].astype(jnp.float32)
+            ).astype(jnp.bfloat16)
+
+        for k in range(1, planes):
+            plane_out(c, k).start()
+
+    def finish(c):
+        for k in range(1, planes):
+            plane_out(c, k).wait_recv()
+        if c >= 2:
+            grad_out(c - 2).wait()
+        value = x_land[c, plane].astype(jnp.float32)
+        for k in range(1, planes):
+            value += plane_land[c, k - 1].astype(jnp.float32)
+        out_buf[c % 2] = value
+        grad_out(c).start()
+
+    def small_copy(step, peer, slot):
+        return pltpu.make_async_remote_copy(
+            small_land.at[0], small_land.at[slot], small_send.at[step], small_recv.at[step],
+            device_id=peer, device_id_type=MESH,
+        )
+
+    def small_begin(step):
+        if step < 3:
+            if step == 0:
+                pltpu.sync_copy(small_ref, small_land.at[0])
+            small_copy(step, (core_peer, x_peer, y_peer)[step], 1 + step).start()
+        else:
+            for k in range(1, planes):
+                small_copy(2 + k, plane_peers[k - 1], 3 + k).start()
+
+    def small_end(step):
+        if step < 3:
+            small_copy(step, core_peer, 1 + step).wait()
+            small_land[0] = small_land[0] + small_land[1 + step]
+        else:
+            for k in range(1, planes):
+                small_copy(2 + k, core_peer, 3 + k).wait()
+            value = jnp.zeros(small_land.shape[1:], jnp.float32)
+            for p in range(planes):
+                back = lax.rem(plane + planes - p, planes)
+                value += small_land[jnp.where(back == 0, 0, 3 + back)]
+            small_land[1] = value
+            pltpu.sync_copy(small_land.at[1], small_out)
+
+    fetch(0)
+    for c in range(total + 2):
+        if c < total:
+            multiply(c)
+        if 1 <= c <= total:
+            fold(c - 1)
+        if c >= 2:
+            finish(c - 2)
+        if c in (1, 2, 3, 4):
+            small_end(c - 1)
+        if c in (0, 1, 2, 3):
+            small_begin(c)
+    for a in order:
+        left_out(a).wait_send()
+    for c in range(total):
+        right_out(c).wait_send()
+        if c >= total - 3:
+            x_out(c).wait_send()
+        for k in range(1, planes):
+            plane_out(c, k).wait_send()
+    for c in range(total - 2, total):
+        grad_out(c).wait()
+
+
+def scatter_grads(lefts, rights, smalls):
+    size = lax.axis_size("dp")
+    planes = size // 4
+    tokens, features = lefts[0].shape
+    rows = features // size
+    left = jnp.stack([array.T for array in lefts]).reshape(4, planes, 2, 2, rows, tokens)
+    arrays = [array for array, _ in rights]
+    widths = [array.shape[1] for array in arrays]
+    jobs = [
+        (which, i, start)
+        for i, (array, which) in enumerate(rights)
+        for start in range(0, array.shape[1], TILE)
+    ]
+    total = len(jobs)
+    sem = pltpu.SemaphoreType.DMA
+    hbm = pl.BlockSpec(memory_space=pl.ANY)
+    results = pl.pallas_call(
+        partial(scatter_kernel, planes, jobs, widths),
+        out_shape=[jax.ShapeDtypeStruct((rows, width), jnp.float32) for width in widths]
+        + [jax.ShapeDtypeStruct(smalls.shape, jnp.float32)]
+        + [jax.ShapeDtypeStruct((4, planes, 2, rows, tokens), jnp.bfloat16)]
+        + [jax.ShapeDtypeStruct(array.shape, jnp.bfloat16) for array in arrays],
+        in_specs=[hbm] * (2 + len(arrays)),
+        out_specs=[hbm] * (2 + 2 * len(arrays)),
+        scratch_shapes=[
+            pltpu.VMEM((2, 2, planes, rows, 2 * tokens), jnp.bfloat16),
+            pltpu.VMEM((2, 2 * tokens, TILE), jnp.bfloat16),
+            pltpu.VMEM((3, 2, planes, rows, TILE), jnp.bfloat16),
+            pltpu.VMEM((total, planes, rows, TILE), jnp.bfloat16),
+            pltpu.VMEM((total, planes - 1, rows, TILE), jnp.bfloat16),
+            pltpu.VMEM((2, rows, TILE), jnp.float32),
+            pltpu.VMEM((3 + planes, *smalls.shape), jnp.float32),
+            sem((2, 2, 2)), sem((2, 2)), sem((2,)), sem((total,)), sem((total,)), sem((4,)), sem((4,)),
+            sem((total,)), sem((total,)), sem((total, planes - 1)), sem((total, planes - 1)),
+            sem((2 + planes,)), sem((2 + planes,)),
+        ],
+        compiler_params=pltpu.CompilerParams(
+            collective_id=1, has_side_effects=True, vmem_limit_bytes=60 * 2**20
+        ),
+        name="scatter_grads",
+    )(left, *arrays, smalls)
+    return results[: len(arrays)], results[len(arrays)]
 
 
 def shards(
@@ -87,15 +455,9 @@
     length = lengths[dealing[group_index]]
     key_valid = jnp.arange(seq_len) < length
     factor = HEAD_DIM ** (-0.5)
-    gathered = (
-        lax.all_gather(w_query, "dp", axis=0, tiled=True),
-        lax.all_gather(w_key, "dp", axis=0, tiled=True),
-        lax.all_gather(w_value, "dp", axis=0, tiled=True),
-        lax.all_gather(w_out, "dp", axis=1, tiled=True),
-        lax.all_gather(w_up, "dp", axis=0, tiled=True),
-        lax.all_gather(w_down, "dp", axis=1, tiled=True),
-    )
-    query_full, key_full, value_full, out_full, up_full, down_full = gathered
+    query_full, key_full, value_full, out_turned, up_full, down_turned = gather_weights(
+        [w_query, w_key, w_value, w_out.T, w_up, w_down.T]
+    )
     head_cols = query_full.shape[1]
     heads_local = head_cols // HEAD_DIM
     up_cols = up_full.shape[1]
@@ -123,7 +485,7 @@
         "hqk,khd->qhd", softmax_low, value_rows, preferred_element_type=jnp.float32
     )
     mixed_heads = mixed_heads.astype(jnp.bfloat16).reshape(seq_len, head_cols)
-    attn_part = jnp.dot(mixed_heads, out_full, preferred_element_type=jnp.float32)
+    attn_part = contract_cols(mixed_heads, out_turned)
     attended = (
         lax.psum_scatter(
             attn_part.astype(jnp.bfloat16), "tensor", scatter_dimension=0, tiled=True
@@ -136,7 +498,7 @@
     full_hidden = lax.all_gather(hidden.astype(jnp.bfloat16), "tensor", axis=0, tiled=True)
     upward = jnp.dot(full_hidden, up_full, preferred_element_type=jnp.float32) + up_bias
     active = jax.nn.gelu(upward, approximate=True).astype(jnp.bfloat16)
-    down_part = jnp.dot(active, down_full, preferred_element_type=jnp.float32)
+    down_part = contract_cols(active, down_turned)
     downward = (
         lax.psum_scatter(
             down_part.astype(jnp.bfloat16), "tensor", scatter_dimension=0, tiled=True
@@ -147,15 +509,6 @@
         hidden + downward, gain_second, shift_second
     )
     output = result.astype(jnp.bfloat16).reshape(cotangent.shape)
-    gathered = (
-        lax.all_gather(w_query, "dp", axis=0, tiled=True),
-        lax.all_gather(w_key, "dp", axis=0, tiled=True),
-        lax.all_gather(w_value, "dp", axis=0, tiled=True),
-        lax.all_gather(w_out, "dp", axis=1, tiled=True),
-        lax.all_gather(w_up, "dp", axis=0, tiled=True),
-        lax.all_gather(w_down, "dp", axis=1, tiled=True),
-    )
-    query_full, key_full, value_full, out_full, up_full, down_full = gathered
     grad_result = cotangent.reshape(half_rows, features).astype(jnp.float32)
     grad_second, grad_gain_second, grad_shift_second = norm_backward(
         grad_result, gain_second, normed_second, inverse_second
@@ -163,12 +516,10 @@
     grad_down = grad_second.astype(jnp.bfloat16)
     grad_b_down = jnp.sum(grad_down.astype(jnp.float32), axis=0)
     full_grad_down = lax.all_gather(grad_down, "tensor", axis=0, tiled=True)
-    grad_active = contract_cols(full_grad_down, down_full)
-    grad_w_down = contract_rows(active, full_grad_down)
+    grad_active = jnp.dot(full_grad_down, down_turned, preferred_element_type=jnp.float32)
     _, gelu_pull = jax.vjp(partial(jax.nn.gelu, approximate=True), upward)
     grad_up = gelu_pull(grad_active)[0].astype(jnp.bfloat16)
     grad_up_bias = jnp.sum(grad_up.astype(jnp.float32), axis=0)
-    grad_w_up = contract_rows(full_hidden, grad_up)
     hidden_part = contract_cols(grad_up, up_full)
     grad_hidden = grad_second + lax.psum_scatter(
         hidden_part.astype(jnp.bfloat16), "tensor", scatter_dimension=0, tiled=True
@@ -179,8 +530,9 @@
     grad_attended = grad_first.astype(jnp.bfloat16)
     grad_b_out = jnp.sum(grad_attended.astype(jnp.float32), axis=0)
     full_grad_attended = lax.all_gather(grad_attended, "tensor", axis=0, tiled=True)
-    grad_mixed = contract_cols(full_grad_attended, out_full).astype(jnp.bfloat16)
-    grad_w_out = contract_rows(mixed_heads, full_grad_attended)
+    grad_mixed = jnp.dot(
+        full_grad_attended, out_turned, preferred_element_type=jnp.float32
+    ).astype(jnp.bfloat16)
     grad_mixed = grad_mixed.reshape(seq_len, heads_local, HEAD_DIM)
     scores = attention_scores(query_rows, key_rows, key_valid, factor)
     softmax_again = jnp.exp(scores - log_norm)
@@ -212,9 +564,6 @@
         .reshape(seq_len, head_cols)
     )
     grad_values = grad_values.reshape(seq_len, head_cols)
-    grad_w_query = contract_rows(full_in, grad_queries)
-    grad_w_key = contract_rows(full_in, grad_keys)
-    grad_w_value = contract_rows(full_in, grad_values)
     grad_query_bias = jnp.sum(grad_queries.astype(jnp.float32), axis=0)
     grad_value_bias = jnp.sum(grad_values.astype(jnp.float32), axis=0)
     input_part = (
@@ -228,30 +577,30 @@
     grad_sent = grad_own.astype(jnp.bfloat16).reshape(1, 1, half_rows, features)
     returned = lax.all_to_all(grad_sent, "dp", split_axis=2, concat_axis=0, tiled=True)
     grad_inputs = jnp.zeros_like(returned).at[dealing].set(returned)
-    weight_sums = (
-        lax.psum_scatter(grad_w_query.astype(jnp.bfloat16), "dp", scatter_dimension=0, tiled=True).astype(jnp.float32),
-        lax.psum_scatter(grad_w_key.astype(jnp.bfloat16), "dp", scatter_dimension=0, tiled=True).astype(jnp.float32),
-        lax.psum_scatter(grad_w_value.astype(jnp.bfloat16), "dp", scatter_dimension=0, tiled=True).astype(jnp.float32),
-        lax.psum_scatter(grad_w_out.astype(jnp.bfloat16), "dp", scatter_dimension=1, tiled=True).astype(jnp.float32),
-        lax.psum_scatter(grad_w_up.astype(jnp.bfloat16), "dp", scatter_dimension=0, tiled=True).astype(jnp.float32),
-        lax.psum_scatter(grad_w_down.astype(jnp.bfloat16), "dp", scatter_dimension=1, tiled=True).astype(jnp.float32),
-    )
     full_cols = b_query.shape[0]
     full_up = b_up.shape[0]
-    small_sums = lax.psum(
-        (
-            place_slice(grad_query_bias, full_cols, tensor_index * head_cols),
-            place_slice(grad_value_bias, full_cols, tensor_index * head_cols),
-            grad_b_out,
-            place_slice(grad_up_bias, full_up, tensor_index * up_cols),
-            grad_b_down,
-            grad_gain_first,
-            grad_shift_first,
-            grad_gain_second,
-            grad_shift_second,
-        ),
-        ("dp", "tensor"),
-    )
+    smalls = (
+        place_slice(grad_query_bias, full_cols, tensor_index * head_cols),
+        place_slice(grad_value_bias, full_cols, tensor_index * head_cols),
+        grad_b_out,
+        place_slice(grad_up_bias, full_up, tensor_index * up_cols),
+        grad_b_down,
+        grad_gain_first,
+        grad_shift_first,
+        grad_gain_second,
+        grad_shift_second,
+    )
+    sums, small_total = scatter_grads(
+        [full_in, full_grad_attended, full_hidden, full_grad_down],
+        [(active, 3), (grad_up, 2), (mixed_heads, 1), (grad_queries, 0), (grad_keys, 0), (grad_values, 0)],
+        jnp.concatenate(smalls).reshape(-1, 128),
+    )
+    weight_sums = (sums[3], sums[4], sums[5], sums[2].T, sums[1], sums[0].T)
+    small_total = small_total.reshape(-1)
+    small_sums, at = [], 0
+    for small in smalls:
+        small_sums.append(small_total[at : at + small.shape[0]])
+        at += small.shape[0]
     return (
         output,
         grad_inputs,

time: 1800 us -> 1270 us (0.71)
  waiting for transfers between devices: 1360 us -> 279 us
  Pallas kernels: 0 us -> 639 us
  matrix products: 222 us -> 142 us
    pallas_call x0 -> x2, Pallas kernels: none -> 639 us  [the longest x1 321 us: gather_weights(): pl.pallas_call(partial(gather_kernel, planes, widths), out_shape=[jax.Sha...]
    all_gather x6 -> x0, waiting for transfers between devices: 416 us -> none  [the longest x1 129 us: shards(): lax.all_gather(w_up, 'dp', axis=0, tiled=True)]
    reduce_scatter x4 -> x0, waiting for transfers between devices: 390 us -> none  [the longest x1 178 us: shards(): lax.psum_scatter(grad_w_up.astype(jnp.bfloat16), 'dp', scatter_dimension=...]
    unnamed x23 -> x8, waiting for transfers between devices: 165 us -> 0.13 us
    psum x1 -> x0, waiting for transfers between devices: 129 us -> none  [shards(): lax.psum((place_slice(grad_query_bias, full_cols, tensor_index * head_col...]
    dot_general x8 -> x2, matrix products: 99.1 us -> 28.6 us  [the longest x1 22.8 us: shards(): jnp.dot(full_grad_down, down_turned, preferred_element_type=jnp.float32)]
    unnamed x104 -> x127, local copies, waits for them, and re-layouts: 68.9 us -> 33.6 us
    all_gather x1, waiting for transfers between devices: 33 us -> 0.02 us  [shards(): full_in = lax.all_gather(own_rows, 'tensor', axis=0, tiled=True)]
  transfers between devices with their start and end apart: 22 -> 9, of which waited for: 19 -> 7; matrix products, arithmetic and copies ran while one was open for 11% -> 3% of each run, Pallas kernels for 0% -> 51%
where the time goes in v2:
time: 1270 us; the launch traced here: 1260 us
  Pallas kernels  639 us (50%)
  waiting for transfers between devices  279 us (22%)
  matrix products  142 us (11%)
  local copies, waits for them, and re-layouts  80.3 us (6%)
  other arithmetic  50.8 us (4%)
  blocking collectives  43.2 us (3%)
  between operations  17.5 us (1%)
    pallas_call x1, Pallas kernels, gather_weights(): pl.pallas_call(partial(gather_kernel, planes, widths), out_shape=[jax.Sha...  321 us
    pallas_call x1, Pallas kernels, scatter_grads(): pl.pallas_call(partial(scatter_kernel, planes, jobs, widths), out_shape=[...  318 us
    reduce_scatter x1, waiting for transfers between devices, shards(): lax.psum_scatter(attn_part.astype(jnp.bfloat16), 'tensor', scatter_dimens...  65.4 us
    dot_general x6, matrix products, contract_cols(): lax.dot_general(left, right, (((1,), (1,)), ((), ())), preferred_element_...  46 us
    all_to_all x1, blocking collectives, shards(): lax.all_to_all(ordered, 'dp', split_axis=0, concat_axis=2, tiled=True)  43.2 us
    all_gather x1, waiting for transfers between devices, shards(): lax.all_gather(grad_attended, 'tensor', axis=0, tiled=True)  39.1 us
    all_gather x1, waiting for transfers between devices, shards(): full_grad_down = lax.all_gather(grad_down, 'tensor', axis=0, tiled=True)  39 us
    all_gather x1, waiting for transfers between devices, shards(): lax.all_gather(hidden.astype(jnp.bfloat16), 'tensor', axis=0, tiled=True)  38.6 us
  transfers between devices with their start and end apart: 9, of which 7 were waited for; matrix products, arithmetic and copies ran while one was open for 3% of the time, Pallas kernels for 51%

profile of v2, /device:TPU:0, one launch (start us, length us, event | category | flops | bytes accessed | tf_op | source)
XLA Modules:
  0.0 1258.6 jit_solution(348953053109166688)
XLA Ops:
  11.5 43.2 %all_to_all.21 = bf16[16,1,20,2048]{3,2,1,0:T(8,128)(2,1)S(1)} all-to-all(bf16[16,1,20,2048]{3,2,1,0:T(8,128)(2,1)S(1)} %fusion.28), channel_id=1, replica_groups=mesh['dp'=16,'tensor'=2] {'dp'}, dimensions={0} | all-to-all | bytes 2621440 | tf_op jit(solution)/shard_map/all_to_all | solution.py:450
  61.4 320.8 %gather_weights.1 = (bf16[4,2,2,128,1024]{4,3,2,1,0:T(8,128)(2,1)}, bf16[4,2,2,128,1024]{4,3,2,1,0:T(8,128)(2,1)}, bf16[4,2,2,128,1024]{4,3,2,1,0:T(8,128)(2,1)}...) custom-call(bf16[128,1024]{1,0:T(8,128)(2,1)} %refs_0_.1, ...), custom_call_target="tpu_custom_call" | custom-call | tf_op jit(solution)/shard_map/gather_weights/pallas_call | solution.py:160
  382.8 5.9 add_convert_fusion.3
  389.5 7.4 convolution_convert_fusion.4
  398.8 3.0 fusion.41
  405.6 6.9 fusion.29
  412.4 3.0 fusion.24
  416.5 4.2 convolution_convert_fusion
  420.9 65.4 %reduce-scatter.5.cloned.1.call-done = bf16[320,2048]{1,0:T(8,128)(2,1)} async-done(((bf16[640,2048]{1,0:T(8,128)(2,1)}), bf16[320,2048]{1,0:T(8,128)(2,1)}) %reduce-scatter.5.cloned.1.call-update) | async-done | bytes 1310736 | tf_op jit(solution)/shard_map/reduce_scatter | solution.py:490
  491.4 38.6 %all-gather.7.cloned.1.call-done = bf16[640,2048]{1,0:T(8,128)(2,1)} async-done(((bf16[320,2048]{1,0:T(8,128)(2,1)}), bf16[640,2048]{1,0:T(8,128)(2,1)}) %all-gather.7.cloned.1.call-update) | async-done | bytes 2621456 | tf_op jit(solution)/shard_map/all_gather | solution.py:498
  530.0 19.8 %multiply_convert_fusion.1 = (bf16[640,4096]{1,0:T(8,128)(2,1)S(1)}, f32[640,4096]{1,0:T(8,128)}) fusion(f32[4096]{0:T(1024)S(1)} %dynamic_slice.19, bf16[640,2048]{1,0:T(8,128)(2,1)} %all-gather.7.cloned.1.call-done, bf16[2048,4096]{1,0:T(8,128)(2,1)} %bitcast.173), kind=kOutput, calls=%fused_computation.20 | convolution fusion | flops 10763632640 | bytes 35143680 | tf_op jit(solution)/shard_map/dot_general | solution.py:499
  549.8 2.3 copy-done.18
  552.1 15.7 %convolution_convert_fusion.2 = bf16[640,2048]{1,0:T(8,128)(2,1)} fusion(bf16[640,4096]{1,0:T(8,128)(2,1)S(1)} %get-tuple-element.122.refs_1_, bf16[2048,4096]{1,0:T(8,128)(2,1)} %bitcast.175), kind=kOutput, calls=%fused_computation.35 | convolution fusion | flops 10738728960 | bytes 24641536 | tf_op jit(solution)/shard_map/dot_general | solution.py:41
  567.9 37.7 %reduce-scatter.7.cloned.1.call-done = bf16[320,2048]{1,0:T(8,128)(2,1)} async-done(((bf16[640,2048]{1,0:T(8,128)(2,1)}), bf16[320,2048]{1,0:T(8,128)(2,1)}) %reduce-scatter.7.cloned.1.call-update) | async-done | bytes 1310736 | tf_op jit(solution)/shard_map/reduce_scatter | solution.py:503
  605.6 2.5 fusion.40
  610.5 3.7 convert_reduce_fusion.2
  614.5 39.0 %all-gather.9.cloned.1.call-done = bf16[640,2048]{1,0:T(8,128)(2,1)} async-done(((bf16[320,2048]{1,0:T(8,128)(2,1)}), bf16[640,2048]{1,0:T(8,128)(2,1)}) %all-gather.9.cloned.1.call-update) | async-done | bytes 2621456 | tf_op jit(solution)/shard_map/all_gather | solution.py:518
  653.4 22.8 %convert_reduce_fusion = (f32[4096]{0:T(1024)S(1)}, bf16[640,4096]{1,0:T(8,128)(2,1)S(1)}) fusion(f32[640,4096]{1,0:T(8,128)} %get-tuple-element.123, f32[4096]{0:T(1024)S(1)} %dynamic_slice.19, bf16[640,2048]{1,0:T(8,128)(2,1)} %all-gather.9.cloned.1.call-done, bf16[2048,4096]{1,0:T(8,128)(2,1)} %bitcast.176), kind=kOutput, calls=%fused_computation.19 | convolution fusion | flops 10797707264 | bytes 35160064 | tf_op jit(solution)/shard_map/dot_general | solution.py:519
  676.2 2.2 copy-done.19
  678.4 15.7 %convolution_convert_fusion.1 = bf16[640,2048]{1,0:T(8,128)(2,1)} fusion(bf16[640,4096]{1,0:T(8,128)(2,1)S(1)} %get-tuple-element.105.refs_2_, bf16[2048,4096]{1,0:T(8,128)(2,1)} %bitcast.174), kind=kOutput, calls=%fused_computation.34 | convolution fusion | flops 10738728960 | bytes 24641536 | tf_op jit(solution)/shard_map/dot_general | solution.py:41
  694.5 37.5 %reduce-scatter.9.cloned.1.call-done = bf16[320,2048]{1,0:T(8,128)(2,1)} async-done(((bf16[640,2048]{1,0:T(8,128)(2,1)}), bf16[320,2048]{1,0:T(8,128)(2,1)}) %reduce-scatter.9.cloned.1.call-update) | async-done | bytes 1310736 | tf_op jit(solution)/shard_map/reduce_scatter | solution.py:524
  731.9 3.8 multiply_reduce_fusion.1
  735.8 3.4 convert_reduce_fusion.3
  739.2 39.1 %all-gather.11.cloned.1.call-done = bf16[640,2048]{1,0:T(8,128)(2,1)} async-done(((bf16[320,2048]{1,0:T(8,128)(2,1)}), bf16[640,2048]{1,0:T(8,128)(2,1)}) %all-gather.11.cloned.1.call-update) | async-done | bytes 2621456 | tf_op jit(solution)/shard_map/all_gather | solution.py:532
  778.3 5.9 convolution_convert_fusion.3
  785.0 7.1 convert_reduce_fusion.4
  792.1 11.0 multiply_reduce_fusion
  803.1 7.0 multiply_convert_fusion
  811.8 2.1 multiply_convert_fusion.2
  814.4 2.9 fusion.43
  817.4 3.0 fusion.42
  820.4 4.4 add_convert_fusion
  826.4 2.6 copy.120.refs_3_
  829.0 2.6 copy.109
  831.6 4.5 copy.111
  836.0 4.6 copy.112
  841.2 21.4 %reduce-scatter.11.cloned.1.call-done = bf16[320,2048]{1,0:T(8,128)(2,1)} async-done(((bf16[640,2048]{1,0:T(8,128)(2,1)}), bf16[320,2048]{1,0:T(8,128)(2,1)}) %reduce-scatter.11.cloned.1.call-update) | async-done | bytes 1310736 | tf_op jit(solution)/shard_map/reduce_scatter | solution.py:574
  866.9 9.4 reduce.5
  876.3 4.5 reshape.237
  880.8 5.9 all-to-all-start.1
  888.2 2.5 copy.122.refs_5_
  892.1 4.6 copy.110
  896.8 9.2 pad_maximum_fusion.refs_0_
  906.0 317.8 %scatter_grads.1 = (f32[128,4096]{1,0:T(8,128)}, f32[128,4096]{1,0:T(8,128)}, f32[128,1024]{1,0:T(8,128)}, f32[128,1024]{1,0:T(8,128)}, f32[128,1024]{1,0:T(8,12...) custom-call(bf16[4,4,2,2,128,640]{5,4,3,2,1,0:T(8,128)(2,1)} %pad_ma, ...), custom_call_target="tpu_custom_call" | custom-call | tf_op jit(solution)/shard_map/scatter_grads/pallas_call | solution.py:398
  1223.8 2.9 copy.115
  1229.0 4.5 reshape.238
  1233.5 8.7 bitcast_reduce_fusion
  1242.2 2.2 reshape.229
  (189 shorter events, 46.4 us)
Async XLA Ops:
  7.2 375.6 %all-gather.5.cloned.1.call-start = ((), (), s32[]{:S(2)}) async-start(), calls=%async_computation.6 | async-start | bytes 3932160 | tf_op jit(solution)/shard_map/all_gather | solution.py:467
  54.7 3.2 copy-start.26
  54.7 4.5 copy-start.32
  56.0 4.8 copy-start.48
  56.0 430.3 %reduce-scatter.5.cloned.1.call-start = ((), (), s32[]{:S(2)}) async-start(), calls=%async_computation.7 | async-start | bytes 3932160 | tf_op jit(solution)/shard_map/reduce_scatter | solution.py:490
  60.1 322.7 %dynamic-slice-start = ((f32[2048]{0:T(1024)}, s32[]{:T(128)}), f32[1024]{0:T(1024)S(1)}, s32[]{:S(2)}) async-start(f32[2048]{0:T(1024)} %param.25, s32[]{:T(128)} %select_n.41), calls=%async_computation.18 | async-start | bytes 8704 | tf_op jit(solution)/shard_map/dynamic_slice | solution.py:464
  389.5 9.3 copy-start.8
  398.8 3.1 copy-start.4
  401.9 10.6 copy-start
  401.9 3.7 copy-start.20
  401.9 3.7 dynamic-slice-start.1
  412.4 3.0 copy-start.23
  412.4 4.1 copy-start.46
  420.8 65.5 %copy-start.1 = (bf16[320,2048]{1,0:T(8,128)(2,1)S(1)}, bf16[320,2048]{1,0:T(8,128)(2,1)}, u32[]{:S(2)}) copy-start(bf16[320,2048]{1,0:T(8,128)(2,1)} %reshape.195) | copy-start | bytes 3932164
  420.8 65.5 %copy-start.31 = (f32[2048]{0:T(1024)S(1)}, f32[2048]{0:T(1024)}, u32[]{:S(2)}) copy-start(f32[2048]{0:T(1024)} %param.28) | copy-start | bytes 24580
  420.8 68.1 %copy-start.33 = (f32[2048]{0:T(1024)S(1)}, f32[2048]{0:T(1024)}, u32[]{:S(2)}) copy-start(f32[2048]{0:T(1024)} %param.29) | copy-start | bytes 24580
  420.8 68.1 %copy-start.36 = (f32[2048]{0:T(1024)S(1)}, f32[2048]{0:T(1024)}, u32[]{:S(2)}) copy-start(f32[2048]{0:T(1024)} %param.30) | copy-start | bytes 24580
  420.8 109.2 %all-gather.7.cloned.1.call-start = ((), (), s32[]{:S(2)}) async-start(), calls=%async_computation.8 | async-start | bytes 3932160 | tf_op jit(solution)/shard_map/all_gather | solution.py:498
  490.8 114.8 %reduce-scatter.7.cloned.1.call-start = ((), (), s32[]{:S(2)}) async-start(), calls=%async_computation.9 | async-start | bytes 3932160 | tf_op jit(solution)/shard_map/reduce_scatter | solution.py:503
  567.8 37.8 %copy-start.38 = (f32[2048]{0:T(1024)S(1)}, f32[2048]{0:T(1024)}, u32[]{:S(2)}) copy-start(f32[2048]{0:T(1024)} %param.34) | copy-start | bytes 24580
  567.9 85.6 %all-gather.9.cloned.1.call-start = ((), (), s32[]{:S(2)}) async-start(), calls=%async_computation.10 | async-start | bytes 3932160 | tf_op jit(solution)/shard_map/all_gather | solution.py:518
  614.2 117.7 %reduce-scatter.9.cloned.1.call-start = ((), (), s32[]{:S(2)}) async-start(), calls=%async_computation.11 | async-start | bytes 3932160 | tf_op jit(solution)/shard_map/reduce_scatter | solution.py:524
  694.2 84.2 %all-gather.11.cloned.1.call-start = ((), (), s32[]{:S(2)}) async-start(), calls=%async_computation.12 | async-start | bytes 3932160 | tf_op jit(solution)/shard_map/all_gather | solution.py:532
  731.9 3.8 copy-start.3
  731.9 3.8 copy-start.17
  739.2 123.5 %reduce-scatter.11.cloned.1.call-start = ((), (), s32[]{:S(2)}) async-start(), calls=%async_computation.13 | async-start | bytes 3932160 | tf_op jit(solution)/shard_map/reduce_scatter | solution.py:574
  784.9 7.1 copy-start.24
  784.9 18.1 %slice-start = ((s8[13107200]{0:T(1024)(128)(4,1)}), s8[4194304]{0:T(1024)(128)(4,1)S(1)}, s32[]{:S(2)}) async-start(s8[13107200]{0:T(1024)(128)(4,1)} %bitcast.141), calls=%async_computation.14 | async-start | bytes 8388608
  785.0 18.1 %slice-start.1 = ((s8[13107200]{0:T(1024)(128)(4,1)}), s8[524288]{0:T(1024)(128)(4,1)S(1)}, s32[]{:S(2)}) async-start(s8[13107200]{0:T(1024)(128)(4,1)} %bitcast.141), calls=%async_computation.15 | async-start | bytes 1048576
  792.0 28.4 %copy-start.14 = (bf16[8,128,640]{2,1,0:T(8,128)(2,1)}, bf16[8,128,640]{2,1,0:T(8,128)(2,1)S(1)}, u32[]{:S(2)}) copy-start(bf16[8,128,640]{2,1,0:T(8,128)(2,1)S(1)} %get-tuple-element.129) | copy-start | bytes 3932164
  792.1 11.0 slice-start.2
  792.1 11.0 slice-start.3
  803.1 7.0 copy-start.5
  811.8 5.6 copy-start.12
  811.8 2.7 copy-start.45
  813.9 3.5 copy-start.16
  814.4 3.0 copy-start.44
  817.4 3.0 copy-start.43
  836.0 26.6 %copy-start.10 = (f32[320,2048]{1,0:T(8,128)S(1)}, f32[320,2048]{1,0:T(8,128)}, u32[]{:S(2)}) copy-start(f32[320,2048]{1,0:T(8,128)} %get-tuple-element.108) | copy-start | bytes 7864324
  876.3 10.4 copy-start.15
  880.8 348.3 %all-to-all-start.1 = ((bf16[16,2,20480]{2,1,0:T(2,128)(2,1)}), bf16[16,2,20480]{2,1,0:T(2,128)(2,1)}, u32[]{:S(2)}, u32[]{:S(2)}) async-start(bf16[16,2,20480]{2,1,0:T(2,128)(2,1)} %reshape.237), calls=%async_computation.5 | async-start | bytes 2621440 | tf_op jit(solution)/shard_map/all_to_all | solution.py:578
  886.7 4.0 copy-start.13
  892.1 4.7 copy-start.11
  896.8 9.2 copy-start.34
  1223.8 3.0 copy-start.30
  1223.8 4.0 copy-start.35
  1245.8 3.4 copy-start.27
  1245.8 4.2 copy-start.22
  (16 other events, 28.9 us)
Sparse Core Ops, SparseCore 0:
  56.1 39.3 all-gather.4
  420.9 65.2 reduce-scatter.4
  490.9 39.0 all-gather.6
  568.0 37.5 reduce-scatter.6
  614.4 39.0 all-gather.8
  694.3 37.5 reduce-scatter.8
  739.3 39.0 all-gather.10
  825.0 37.5 reduce-scatter.10

commit v3 on v2

--- a/solution.py
+++ b/solution.py
@@ -58,6 +58,7 @@
 
 MESH = pl.DeviceIdType.MESH
 TILE = 1024
+SLOPE = 0.7978845608028654
 
 
 def place():
@@ -76,102 +77,449 @@
     pl.semaphore_wait(barrier, len(peers))
 
 
-def gather_kernel(planes, widths, *refs):
+def gather_tiles(widths):
+    return [(i, start) for i, width in enumerate(widths) for start in range(0, width, TILE)]
+
+
+def forward_kernel(planes, widths, *refs):
     count = len(widths)
-    shard_refs, full_refs = refs[:count], refs[count : 2 * count]
-    local_sem, plane_send, plane_recv, x_send, x_recv, core_send, core_recv = refs[2 * count :]
+    shard_refs = refs[:count]
+    own_ref, cot_ref, mask_ref, vec_ref = refs[count : count + 4]
+    outs = refs[count + 4 :]
+    full_refs = outs[:count]
+    (
+        x_full, cot_full, qkv_out, mixed_out, normed_out, inverse_out, hidden_out, active_out, slope_out,
+        result_out, down_out, second_out, sums_out,
+    ) = outs[count : count + 13]
+    (
+        w_buf, x_buf, qkv_buf, mixed_buf, attn_acc, attn_land, send_buf, hidden_buf, active_buf, slope_buf,
+        down_acc, down_land, inverse_buf, result_buf, sums_buf,
+        plane_send, plane_recv, x_send, x_recv, core_send, core_recv, w_sem, in_send, in_recv,
+        attn_send, attn_recv, down_send, down_recv, load_sem, store_sem,
+    ) = outs[count + 13 :]
     plane, across, core, tensor = place()
     far = [lax.rem(plane + k, planes) for k in range(planes)]
     near = [lax.rem(plane + planes - k, planes) for k in range(planes)]
     x_peer = device_of(plane, 1 - across, core, tensor)
     core_peer = device_of(plane, across, 1 - core, tensor)
-    enter([device_of(far[k], across, core, tensor) for k in range(1, planes)] + [x_peer, core_peer])
-    tiles = [(i, start) for i, width in enumerate(widths) for start in range(0, width, TILE)]
-    total = len(tiles)
-
-    def view(c, *at):
+    y_peer = device_of(plane, across, core, 1 - tensor)
+    plane_peers = [device_of(far[k], across, core, tensor) for k in range(planes)]
+    tiles = gather_tiles(widths)
+    half, features = own_ref.shape
+    tokens = 2 * half
+    block = features // planes
+    head_cols = mixed_buf.shape[1]
+    factor = HEAD_DIM ** (-0.5)
+    own_rows = pl.ds(pl.multiple_of(tensor * half, half), half)
+
+    vec_at = {}
+    at = 0
+    for key, size in (
+        ("b_query", head_cols), ("b_value", head_cols), ("b_out", features), ("gain_first", features),
+        ("shift_first", features), ("b_up", widths[4]), ("b_down", features), ("gain_second", features),
+        ("shift_second", features),
+    ):
+        vec_at[key] = at
+        at += size
+
+    def vector(key, start, size):
+        return vec_ref[:, pl.ds(vec_at[key] + start, size)]
+
+    first_down = len(tiles) - widths[5] // TILE
+    units = [(c, k) for c in range(first_down) for k in range(planes)]
+    units += [(c, k) for k in range(planes) for c in range(first_down, len(tiles))]
+    ahead, lag = 6, 2
+
+    def view(c, *where):
         i, start = tiles[c]
-        return full_refs[i].at[(*at, slice(None), pl.ds(start, TILE))]
+        return full_refs[i].at[(*where, slice(None), pl.ds(start, TILE))]
 
     def own(c):
         i, start = tiles[c]
         return shard_refs[i].at[:, pl.ds(start, TILE)]
 
-    def to_plane(c, k):
-        return pltpu.make_async_remote_copy(
-            own(c), view(c, plane, across, core), plane_send.at[c, k - 1], plane_recv.at[c, k - 1],
-            device_id=device_of(far[k], across, core, tensor), device_id_type=MESH,
-        )
-
-    def from_plane(c, k):
-        return pltpu.make_async_remote_copy(
-            own(c), view(c, near[k], across, core), plane_send.at[c, k - 1], plane_recv.at[c, k - 1],
-            device_id=device_of(far[k], across, core, tensor), device_id_type=MESH,
-        )
-
-    def keep(c):
-        return pltpu.make_async_copy(own(c), view(c, plane, across, core), local_sem.at[c])
-
-    def to_x(c, side):
-        part = view(c, slice(None), side, core)
-        return pltpu.make_async_remote_copy(
-            part, part, x_send.at[c], x_recv.at[c], device_id=x_peer, device_id_type=MESH
-        )
-
-    def to_core(c, side):
-        part = view(c, slice(None), slice(None), side)
-        return pltpu.make_async_remote_copy(
-            part, part, core_send.at[c], core_recv.at[c], device_id=core_peer, device_id_type=MESH
-        )
-
-    def begin(c):
-        keep(c).start()
-        for k in range(1, planes):
-            to_plane(c, k).start()
-
-    ahead = 3
-    for c in range(min(ahead, total)):
-        begin(c)
-    for c in range(total):
-        keep(c).wait()
-        for k in range(1, planes):
-            from_plane(c, k).wait_recv()
-        to_x(c, across).start()
-        if c + ahead < total:
-            begin(c + ahead)
-        if c > 0:
-            to_x(c - 1, 1 - across).wait_recv()
-            to_core(c - 1, core).start()
-    to_x(total - 1, 1 - across).wait_recv()
-    to_core(total - 1, core).start()
-    for c in range(total):
-        for k in range(1, planes):
-            to_plane(c, k).wait_send()
-        to_x(c, across).wait_send()
-        to_core(c, core).wait_send()
-        to_core(c, 1 - core).wait_recv()
-
-
-def gather_weights(shard_list):
+    def unit_z(u, source):
+        c, k = units[u]
+        if k == 0:
+            return pltpu.make_async_copy(own(c), view(c, plane, across, core), plane_recv.at[c, 0])
+        return pltpu.make_async_remote_copy(
+            own(c), view(c, source, across, core), plane_send.at[c, k], plane_recv.at[c, k],
+            device_id=plane_peers[k], device_id_type=MESH,
+        )
+
+    def unit_x(u, side):
+        c, k = units[u]
+        part = view(c, near[k], side, core)
+        return pltpu.make_async_remote_copy(
+            part, part, x_send.at[c, k], x_recv.at[c, k], device_id=x_peer, device_id_type=MESH
+        )
+
+    def unit_core(u, side):
+        c, k = units[u]
+        part = view(c, near[k], slice(None), side)
+        return pltpu.make_async_remote_copy(
+            part, part, core_send.at[c, k], core_recv.at[c, k], device_id=core_peer, device_id_type=MESH
+        )
+
+    def z_start(u):
+        unit_z(u, plane).start()
+
+    def z_wait(u):
+        c, k = units[u]
+        if k == 0:
+            unit_z(u, plane).wait()
+        else:
+            unit_z(u, near[k]).wait_recv()
+
+    def pump(n):
+        if n < len(units):
+            z_wait(n)
+            unit_x(n, across).start()
+            if n + ahead < len(units):
+                z_start(n + ahead)
+        if n >= lag:
+            unit_x(n - lag, 1 - across).wait_recv()
+            unit_core(n - lag, core).start()
+
+    def landed(u):
+        unit_core(u, 1 - core).wait_recv()
+
+    def tile_copies(c):
+        i, start = tiles[c]
+        return [
+            pltpu.make_async_copy(
+                full_refs[i].at[p, :, :, :, pl.ds(start, TILE)], w_buf.at[c % 2, p], w_sem.at[c % 2, p]
+            )
+            for p in range(planes)
+        ]
+
+    def load_tile(c):
+        for u, (tile, _) in enumerate(units):
+            if tile == c:
+                landed(u)
+        for copy in tile_copies(c):
+            copy.start()
+
+    def wait_tile(c):
+        for copy in tile_copies(c):
+            copy.wait()
+
+    def down_copy(k, j):
+        c = first_down + j
+        return pltpu.make_async_copy(
+            view(c, near[k], slice(None), slice(None)), w_buf.at[k % 2, j], w_sem.at[k % 2, j]
+        )
+
+    down_parts = widths[5] // TILE
+
+    def load_down(k):
+        for j in range(down_parts):
+            landed(units.index((first_down + j, k)))
+            down_copy(k, j).start()
+
+    def flat(value):
+        return value.reshape(-1, value.shape[-1])
+
+    def load_x():
+        exchange(0, own_ref, x_full).wait_recv()
+        keep(0, own_ref, x_full).wait()
+        copy = pltpu.make_async_copy(x_full, x_buf, load_sem.at[2])
+        copy.start()
+        copy.wait()
+
+    def exchange(which, source, target):
+        return pltpu.make_async_remote_copy(
+            source, target.at[own_rows], in_send.at[which], in_recv.at[which],
+            device_id=y_peer, device_id_type=MESH,
+        )
+
+    def keep(which, source, target):
+        return pltpu.make_async_copy(source, target.at[own_rows], load_sem.at[which])
+
+    def project(c, bias):
+        wait_tile(c)
+
+        @pl.loop(0, TILE // 512)
+        def _(n):
+            cols = pl.ds(pl.multiple_of(n * 512, 512), 512)
+            value = jnp.dot(
+                x_buf[...], flat(w_buf[c % 2, :, :, :, :, cols]), preferred_element_type=jnp.float32
+            )
+            if bias is not None:
+                value += vec_ref[:, pl.ds(pl.multiple_of(vec_at[bias] + n * 512, 128), 512)]
+            qkv_buf[:, pl.ds(pl.multiple_of(c * TILE + n * 512, 512), 512)] = value.astype(jnp.bfloat16)
+
+    def attend(first, last):
+        @pl.loop(first, last)
+        def _(h):
+            def cols(which):
+                return pl.ds(pl.multiple_of(which * head_cols + h * HEAD_DIM, HEAD_DIM), HEAD_DIM)
+
+            scores = contract_cols(qkv_buf[:, cols(0)], qkv_buf[:, cols(1)]) * factor
+            scores = jnp.where(mask_ref[0:1, :] > 0.0, scores, MASKED)
+            expanded = jnp.exp(scores - jnp.max(scores, axis=1, keepdims=True))
+            weight = (expanded / jnp.sum(expanded, axis=1, keepdims=True)).astype(jnp.bfloat16)
+            mixed_buf[:, cols(0)] = jnp.dot(
+                weight, qkv_buf[:, cols(2)], preferred_element_type=jnp.float32
+            ).astype(jnp.bfloat16)
+
+    def block_cols(p):
+        return pl.ds(pl.multiple_of(p * block, block), block)
+
+    def attn_share(p):
+        return pltpu.make_async_remote_copy(
+            send_buf.at[:, block_cols(p)], attn_land.at[:, block_cols(p)], attn_send.at[p], attn_recv.at[p],
+            device_id=y_peer, device_id_type=MESH,
+        )
+
+    def project_out():
+        wait_tile(3)
+
+        @pl.loop(0, planes)
+        def _(p):
+            value = contract_cols(mixed_buf[...], flat(w_buf[1, p]))
+            attn_acc[:, block_cols(p)] = value
+            send_buf[:, block_cols(p)] = value.astype(jnp.bfloat16)
+            attn_share(p).start()
+
+    def first_norm():
+        @pl.loop(0, planes)
+        def _(p):
+            attn_share(p).wait()
+
+        @pl.loop(0, tokens // 16)
+        def _(i):
+            rows = pl.ds(pl.multiple_of(i * 16, 16), 16)
+            value = (
+                x_buf[rows, :].astype(jnp.float32)
+                + (attn_acc[rows, :] + attn_land[rows, :].astype(jnp.float32))
+                + vector("b_out", 0, features)
+            )
+            hidden, normed, inverse = norm_forward(
+                value, vector("gain_first", 0, features), vector("shift_first", 0, features)
+            )
+            attn_acc[rows, :] = normed
+            inverse_buf[rows, :] = jnp.broadcast_to(inverse, (16, 128))
+            hidden_buf[rows, :] = hidden.astype(jnp.bfloat16)
+
+        store(0, attn_acc, normed_out).start()
+        store(1, inverse_buf, inverse_out).start()
+        store(2, hidden_buf, hidden_out).start()
+        exchange(1, cot_ref, cot_full).wait_recv()
+        keep(1, cot_ref, cot_full).wait()
+        pltpu.make_async_copy(cot_full, x_buf, load_sem.at[2]).start()
+
+    def store(which, source, target):
+        return pltpu.make_async_copy(source, target, store_sem.at[which])
+
+    def slope_store(j):
+        return pltpu.make_async_copy(
+            slope_buf.at[j % 2], slope_out.at[:, pl.ds(j * TILE, TILE)], store_sem.at[5 + j % 2]
+        )
+
+    def raise_up(j):
+        c = 4 + j
+        wait_tile(c)
+        if j >= 2:
+            slope_store(j - 2).wait()
+
+        @pl.loop(0, TILE // 256)
+        def _(n):
+            cols = pl.ds(pl.multiple_of(n * 256, 256), 256)
+            value = jnp.dot(
+                hidden_buf[...], flat(w_buf[c % 2, :, :, :, :, cols]), preferred_element_type=jnp.float32
+            )
+            value += vec_ref[:, pl.ds(pl.multiple_of(vec_at["b_up"] + j * TILE + n * 256, 128), 256)]
+            square = value * value
+            bend = jnp.tanh(SLOPE * value * (1.0 + 0.044715 * square))
+            rise = 0.5 * (1.0 + bend)
+            active_buf[:, pl.ds(pl.multiple_of(j * TILE + n * 256, 256), 256)] = (value * rise).astype(
+                jnp.bfloat16
+            )
+            slope_buf[j % 2, :, cols] = (
+                rise + 0.5 * value * (1.0 - bend * bend) * (SLOPE * (1.0 + 3.0 * 0.044715 * square))
+            ).astype(jnp.bfloat16)
+
+        slope_store(j).start()
+
+    def down_share(k):
+        cols = block_cols(near[k])
+        return pltpu.make_async_remote_copy(
+            send_buf.at[:, cols], down_land.at[:, cols], down_send.at[k], down_recv.at[k],
+            device_id=y_peer, device_id_type=MESH,
+        )
+
+    def lower(k):
+        cols = block_cols(near[k])
+        value = None
+        for j in range(down_parts):
+            down_copy(k, j).wait()
+            part = contract_cols(active_buf[:, j * TILE : (j + 1) * TILE], flat(w_buf[k % 2, j]))
+            value = part if value is None else value + part
+        down_acc[:, cols] = value
+        send_buf[:, cols] = value.astype(jnp.bfloat16)
+        down_share(k).start()
+
+    def second_norm():
+        for k in range(planes):
+            down_share(k).wait()
+        pltpu.make_async_copy(cot_full, x_buf, load_sem.at[2]).wait()
+        store(2, hidden_buf, hidden_out).wait()
+        sums_buf[...] = jnp.zeros_like(sums_buf)
+        gain = vector("gain_second", 0, features)
+
+        def rows_of(which, i):
+            base = tensor if which == 0 else 1 - tensor
+            return pl.ds(pl.multiple_of(base * half + i * 16, 16), 16)
+
+        for which in (0, 1):
+            @pl.loop(0, half // 16)
+            def _(i):
+                rows = rows_of(which, i)
+                hidden = attn_acc[rows, :] * vector("gain_first", 0, features) + vector(
+                    "shift_first", 0, features
+                )
+                value = (
+                    hidden
+                    + (down_acc[rows, :] + down_land[rows, :].astype(jnp.float32))
+                    + vector("b_down", 0, features)
+                )
+                result, normed, inverse = norm_forward(value, gain, vector("shift_second", 0, features))
+                grad_out = x_buf[rows, :].astype(jnp.float32)
+                scaled = grad_out * gain
+                grad = inverse * (
+                    scaled
+                    - jnp.mean(scaled, axis=-1, keepdims=True)
+                    - normed * jnp.mean(scaled * normed, axis=-1, keepdims=True)
+                )
+                down_acc[rows, :] = grad
+                low = grad.astype(jnp.bfloat16)
+                hidden_buf[rows, :] = low
+                if which == 0:
+                    result_buf[pl.ds(pl.multiple_of(i * 16, 16), 16), :] = result.astype(jnp.bfloat16)
+                    sums_buf[0] += grad_out * normed
+                    sums_buf[1] += grad_out
+                    sums_buf[2] += low.astype(jnp.float32)
+
+        for which, source, target in (
+            (2, hidden_buf, down_out), (3, down_acc, second_out), (4, result_buf, result_out), (9, sums_buf, sums_out),
+        ):
+            store(which, source, target).start()
+
+    enter(plane_peers[1:] + [x_peer, core_peer, y_peer])
+    for u in range(ahead):
+        z_start(u)
+    for which, source, target in ((0, own_ref, x_full), (1, cot_ref, cot_full)):
+        exchange(which, source, target).start()
+        keep(which, source, target).start()
+
+    plan = {}
+
+    def at_slot(n, step, *args):
+        plan.setdefault(n, []).append((step, args))
+
+    def ready(c):
+        return planes * (c + 1) + 2
+
+    heads = head_cols // HEAD_DIM
+    at_slot(ready(0), load_x)
+    for c in range(3):
+        at_slot(ready(c), load_tile, c)
+        at_slot(ready(c) + 1, project, c, ("b_query", None, "b_value")[c])
+    begin = ready(2) + 2
+    for q in range(4):
+        at_slot(begin + q, attend, q * heads // 4, (q + 1) * heads // 4)
+    at_slot(begin + 3, load_tile, 3)
+    at_slot(begin + 4, project_out)
+    norm_slot = begin + 4 + 10 * planes // 4
+    at_slot(norm_slot, first_norm)
+    at_slot(max(ready(4), begin), load_tile, 4)
+    at_slot(max(ready(5), begin + 4), load_tile, 5)
+    for j in range(4):
+        slot = max(norm_slot + 1 + j, ready(4 + j) + 1)
+        at_slot(slot, raise_up, j)
+        if j >= 2:
+            plan.setdefault(max(norm_slot + 1 + j - 2, ready(4 + j)), []).append((load_tile, (4 + j,)))
+    for k in range(planes):
+        slot = planes * first_down + down_parts * (k + 1) + 2
+        at_slot(slot, load_down, k)
+        at_slot(slot + 1, lower, k)
+    last = max(max(plan), len(units) + lag - 1)
+    for n in range(last + 1):
+        if n < len(units) + lag:
+            pump(n)
+        for step, args in plan.get(n, []):
+            step(*args)
+        if n == begin + 3:
+            store(7, qkv_buf, qkv_out).start()
+            store(8, mixed_buf, mixed_out).start()
+    store(10, active_buf, active_out).start()
+    second_norm()
+    for which, source, target in (
+        (0, attn_acc, normed_out), (1, inverse_buf, inverse_out), (2, hidden_buf, down_out),
+        (3, down_acc, second_out), (4, result_buf, result_out), (7, qkv_buf, qkv_out),
+        (8, mixed_buf, mixed_out), (9, sums_buf, sums_out), (10, active_buf, active_out),
+    ):
+        store(which, source, target).wait()
+    for j in range(2, 4):
+        slope_store(j).wait()
+    for which, source, target in ((0, own_ref, x_full), (1, cot_ref, cot_full)):
+        exchange(which, source, target).wait_send()
+    for u, (c, k) in enumerate(units):
+        if k > 0:
+            unit_z(u, plane).wait_send()
+        unit_x(u, across).wait_send()
+        unit_core(u, core).wait_send()
+
+
+def forward(shard_list, own, cot, mask, vectors):
     planes = lax.axis_size("dp") // 4
     widths = [shard.shape[1] for shard in shard_list]
     total = sum(width // TILE for width in widths)
-    sem = pltpu.SemaphoreType.DMA
-    full = pl.pallas_call(
-        partial(gather_kernel, planes, widths),
-        out_shape=[
-            jax.ShapeDtypeStruct((planes, 2, 2, *shard.shape), jnp.bfloat16) for shard in shard_list
+    half, features = own.shape
+    tokens, rows = 2 * half, shard_list[0].shape[0]
+    head_cols, up_cols = widths[0], widths[4]
+    sem, low, high = pltpu.SemaphoreType.DMA, jnp.bfloat16, jnp.float32
+    hbm, vmem = pl.BlockSpec(memory_space=pl.ANY), pl.BlockSpec(memory_space=pltpu.VMEM)
+    shapes = [((planes, 2, 2, *shard.shape), low) for shard in shard_list] + [
+        ((tokens, features), low), ((tokens, features), low), ((tokens, 3 * head_cols), low),
+        ((tokens, head_cols), low), ((tokens, features), high), ((tokens, 128), high),
+        ((tokens, features), low), ((tokens, up_cols), low), ((tokens, up_cols), low),
+        ((half, features), low), ((tokens, features), low), ((tokens, features), high),
+        ((3, 16, features), high),
+    ]
+    results = pl.pallas_call(
+        partial(forward_kernel, planes, widths),
+        out_shape=[jax.ShapeDtypeStruct(*shape) for shape in shapes],
+        in_specs=[hbm] * (len(shard_list) + 2) + [vmem] * 2,
+        out_specs=[hbm] * len(shapes),
+        scratch_shapes=[
+            pltpu.VMEM((2, planes, 2, 2, rows, TILE), low),
+            pltpu.VMEM((tokens, features), low),
+            pltpu.VMEM((tokens, 3 * head_cols), low),
+            pltpu.VMEM((tokens, head_cols), low),
+            pltpu.VMEM((tokens, features), high),
+            pltpu.VMEM((tokens, features), low),
+            pltpu.VMEM((tokens, features), low),
+            pltpu.VMEM((tokens, features), low),
+            pltpu.VMEM((tokens, up_cols), low),
+            pltpu.VMEM((2, tokens, TILE), low),
+            pltpu.VMEM((tokens, features), high),
+            pltpu.VMEM((tokens, features), low),
+            pltpu.VMEM((tokens, 128), high),
+            pltpu.VMEM((half, features), low),
+            pltpu.VMEM((3, 16, features), high),
+            *[sem((total, planes))] * 6,
+            sem((2, max(planes, 4))), sem((2,)), sem((2,)),
+            sem((planes,)), sem((planes,)), sem((planes,)), sem((planes,)), sem((3,)), sem((11,)),
         ],
-        in_specs=[pl.BlockSpec(memory_space=pl.ANY)] * len(shard_list),
-        out_specs=[pl.BlockSpec(memory_space=pl.ANY)] * len(shard_list),
-        scratch_shapes=[
-            sem((total,)), sem((total, planes - 1)), sem((total, planes - 1)),
-            sem((total,)), sem((total,)), sem((total,)), sem((total,)),
-        ],
-        compiler_params=pltpu.CompilerParams(collective_id=0, has_side_effects=True),
-        name="gather_weights",
-    )(*shard_list)
-    return [array.reshape(-1, array.shape[-1]) for array in full]
+        compiler_params=pltpu.CompilerParams(
+            collective_id=0, has_side_effects=True, vmem_limit_bytes=62 * 2**20
+        ),
+        name="forward_gather",
+    )(*shard_list, own, cot, mask, vectors)
+    weights = [array.reshape(-1, array.shape[-1]) for array in results[: len(shard_list)]]
+    return weights, results[len(shard_list) :]
 
 
 def scatter_kernel(planes, jobs, widths, *refs):
@@ -455,70 +803,37 @@
     length = lengths[dealing[group_index]]
     key_valid = jnp.arange(seq_len) < length
     factor = HEAD_DIM ** (-0.5)
-    query_full, key_full, value_full, out_turned, up_full, down_turned = gather_weights(
-        [w_query, w_key, w_value, w_out.T, w_up, w_down.T]
-    )
-    head_cols = query_full.shape[1]
+    head_cols = w_query.shape[1]
     heads_local = head_cols // HEAD_DIM
-    up_cols = up_full.shape[1]
+    up_cols = w_up.shape[1]
     query_bias = lax.dynamic_slice_in_dim(b_query, tensor_index * head_cols, head_cols)
     value_bias = lax.dynamic_slice_in_dim(b_value, tensor_index * head_cols, head_cols)
     up_bias = lax.dynamic_slice_in_dim(b_up, tensor_index * up_cols, up_cols)
-    full_in = lax.all_gather(own_rows, "tensor", axis=0, tiled=True)
-    query_rows = (
-        jnp.dot(full_in, query_full, preferred_element_type=jnp.float32) + query_bias
-    ).astype(jnp.bfloat16)
-    key_rows = jnp.dot(full_in, key_full, preferred_element_type=jnp.float32).astype(jnp.bfloat16)
-    value_rows = (
-        jnp.dot(full_in, value_full, preferred_element_type=jnp.float32) + value_bias
-    ).astype(jnp.bfloat16)
-    query_rows = query_rows.reshape(seq_len, heads_local, HEAD_DIM)
-    key_rows = key_rows.reshape(seq_len, heads_local, HEAD_DIM)
-    value_rows = value_rows.reshape(seq_len, heads_local, HEAD_DIM)
+    vectors = jnp.concatenate(
+        (query_bias, value_bias, b_out, gain_first, shift_first, up_bias, b_down, gain_second, shift_second)
+    ).reshape(1, -1)
+    mask = jnp.broadcast_to(key_valid.astype(jnp.float32), (8, seq_len))
+    weights, saved = forward(
+        [w_query, w_key, w_value, w_out.T, w_up, w_down.T],
+        own_rows, cotangent.reshape(half_rows, features), mask, vectors,
+    )
+    query_full, key_full, value_full, out_turned, up_full, down_turned = weights
+    (
+        full_in, _, qkv, mixed_heads, normed_full, inverse_full, full_hidden, active, slope,
+        result, full_grad_down, second_full, second_sums,
+    ) = saved
+    output = result.reshape(cotangent.shape)
+    own = partial(lax.dynamic_slice_in_dim, start_index=tensor_index * half_rows, slice_size=half_rows)
+    normed_first, inverse_first, grad_second = own(normed_full), own(inverse_full)[:, :1], own(second_full)
+    grad_gain_second, grad_shift_second, grad_b_down = jnp.sum(second_sums, axis=1)
+    query_rows, key_rows, value_rows = (
+        qkv[:, i * head_cols : (i + 1) * head_cols].reshape(seq_len, heads_local, HEAD_DIM) for i in range(3)
+    )
     scores = attention_scores(query_rows, key_rows, key_valid, factor)
     row_max = jnp.max(scores, axis=-1, keepdims=True)
-    expanded = jnp.exp(scores - row_max)
-    row_sum = jnp.sum(expanded, axis=-1, keepdims=True)
-    log_norm = row_max + jnp.log(row_sum)
-    softmax_low = (expanded / row_sum).astype(jnp.bfloat16)
-    mixed_heads = jnp.einsum(
-        "hqk,khd->qhd", softmax_low, value_rows, preferred_element_type=jnp.float32
-    )
-    mixed_heads = mixed_heads.astype(jnp.bfloat16).reshape(seq_len, head_cols)
-    attn_part = contract_cols(mixed_heads, out_turned)
-    attended = (
-        lax.psum_scatter(
-            attn_part.astype(jnp.bfloat16), "tensor", scatter_dimension=0, tiled=True
-        ).astype(jnp.float32)
-        + b_out
-    )
-    hidden, normed_first, inverse_first = norm_forward(
-        own_rows.astype(jnp.float32) + attended, gain_first, shift_first
-    )
-    full_hidden = lax.all_gather(hidden.astype(jnp.bfloat16), "tensor", axis=0, tiled=True)
-    upward = jnp.dot(full_hidden, up_full, preferred_element_type=jnp.float32) + up_bias
-    active = jax.nn.gelu(upward, approximate=True).astype(jnp.bfloat16)
-    down_part = contract_cols(active, down_turned)
-    downward = (
-        lax.psum_scatter(
-            down_part.astype(jnp.bfloat16), "tensor", scatter_dimension=0, tiled=True
-        ).astype(jnp.float32)
-        + b_down
-    )
-    result, normed_second, inverse_second = norm_forward(
-        hidden + downward, gain_second, shift_second
-    )
-    output = result.astype(jnp.bfloat16).reshape(cotangent.shape)
-    grad_result = cotangent.reshape(half_rows, features).astype(jnp.float32)
-    grad_second, grad_gain_second, grad_shift_second = norm_backward(
-        grad_result, gain_second, normed_second, inverse_second
-    )
-    grad_down = grad_second.astype(jnp.bfloat16)
-    grad_b_down = jnp.sum(grad_down.astype(jnp.float32), axis=0)
-    full_grad_down = lax.all_gather(grad_down, "tensor", axis=0, tiled=True)
+    log_norm = row_max + jnp.log(jnp.sum(jnp.exp(scores - row_max), axis=-1, keepdims=True))
     grad_active = jnp.dot(full_grad_down, down_turned, preferred_element_type=jnp.float32)
-    _, gelu_pull = jax.vjp(partial(jax.nn.gelu, approximate=True), upward)
-    grad_up = gelu_pull(grad_active)[0].astype(jnp.bfloat16)
+    grad_up = (grad_active * slope.astype(jnp.float32)).astype(jnp.bfloat16)
     grad_up_bias = jnp.sum(grad_up.astype(jnp.float32), axis=0)
     hidden_part = contract_cols(grad_up, up_full)
     grad_hidden = grad_second + lax.psum_scatter(

time: 1270 us -> 1080 us (0.85)
  waiting for transfers between devices: 279 us -> 124 us
  matrix products: 142 us -> 79.6 us
  Pallas kernels: 639 us -> 699 us
  blocking collectives: 43.2 us -> 0 us
    reduce_scatter x2 -> x0, waiting for transfers between devices: 103 us -> none  [the longest x1 65.4 us: shards(): lax.psum_scatter(attn_part.astype(jnp.bfloat16), 'tensor', scatter_dimens...]
    all_gather x3 -> x0, waiting for transfers between devices: 77.6 us -> none  [the longest x1 39 us: shards(): full_grad_down = lax.all_gather(grad_down, 'tensor', axis=0, tiled=True)]
    pallas_call x1, Pallas kernels: 321 us -> 381 us  [forward(): pl.pallas_call(partial(forward_kernel, planes, widths), out_shape=[jax.Sh...]
    all_to_all x1 -> x0, blocking collectives: 43.2 us -> none  [shards(): lax.all_to_all(ordered, 'dp', split_axis=0, concat_axis=2, tiled=True)]
    dot_general x5 -> x0, matrix products: 42.9 us -> none  [the longest x1 19.8 us: shards(): jnp.dot(full_hidden, up_full, preferred_element_type=jnp.float32) + up_bias]
    all_to_all x0 -> x1, waiting for transfers between devices: none -> 25.7 us  [shards(): lax.all_to_all(ordered, 'dp', split_axis=0, concat_axis=2, tiled=True)]
    all_gather x1, waiting for transfers between devices: 39.1 us -> 19.6 us  [shards(): lax.all_gather(grad_attended, 'tensor', axis=0, tiled=True)]
    reduce_scatter x1, waiting for transfers between devices: 37.5 us -> 55.2 us  [shards(): lax.psum_scatter(hidden_part.astype(jnp.bfloat16), 'tensor', scatter_dime...]
  transfers between devices with their start and end apart: 9 -> 5, of which waited for: 7 -> 4; matrix products, arithmetic and copies ran while one was open for 3% -> 6% of each run, Pallas kernels for 51% -> 30%
where the time goes in v3:
time: 1080 us; the launch traced here: 1060 us
  Pallas kernels  699 us (65%)
  waiting for transfers between devices  124 us (11%)
  local copies, waits for them, and re-layouts  85.9 us (8%)
  matrix products  79.6 us (7%)
  other arithmetic  43.4 us (4%)
  between operations  16.9 us (2%)
  starting transfers between devices  13.6 us (1%)
    pallas_call x1, Pallas kernels, forward(): pl.pallas_call(partial(forward_kernel, planes, widths), out_shape=[jax.Sh...  381 us
    pallas_call x1, Pallas kernels, scatter_grads(): pl.pallas_call(partial(scatter_kernel, planes, jobs, widths), out_shape=[...  318 us
    reduce_scatter x1, waiting for transfers between devices, shards(): lax.psum_scatter(hidden_part.astype(jnp.bfloat16), 'tensor', scatter_dime...  55.2 us
    dot_general x4, matrix products, contract_cols(): lax.dot_general(left, right, (((1,), (1,)), ((), ())), preferred_element_...  31.9 us
    unnamed x114, local copies, waits for them, and re-layouts  30.8 us
    all_to_all x1, waiting for transfers between devices, shards(): lax.all_to_all(ordered, 'dp', split_axis=0, concat_axis=2, tiled=True)  25.7 us
    reduce_scatter x1, waiting for transfers between devices, shards(): lax.psum_scatter(input_part.astype(jnp.bfloat16), 'tensor', scatter_dimen...  23.6 us
  transfers between devices with their start and end apart: 5, of which 4 were waited for; matrix products, arithmetic and copies ran while one was open for 6% of the time, Pallas kernels for 30%

profile of v3, /device:TPU:0, one launch (start us, length us, event | category | flops | bytes accessed | tf_op | source)
XLA Modules:
  0.0 1062.8 jit_solution(1378585766399628024)
XLA Ops:
  8.5 2.0 copy.126
  11.3 1.4 fusion.8
  12.7 7.5 all-to-all-start
  26.5 25.7 %all-to-all-done = bf16[16,1,20,2048]{3,2,1,0:T(8,128)(2,1)S(1)} async-done(((bf16[16,1,20,2048]{3,2,1,0:T(8,128)(2,1)}), bf16[16,1,20,2048]{3,2,1,0:T(8,128)(2,1)S(1)}, u32[]{:S(2)}, u32[]{:S(2)}) %all-to-all-start) | async-done | bytes 1310752 | tf_op jit(solution)/shard_map/all_to_all | solution.py:798
  54.0 381.3 %forward_gather.1 = (bf16[4,2,2,128,1024]{4,3,2,1,0:T(8,128)(2,1)}, bf16[4,2,2,128,1024]{4,3,2,1,0:T(8,128)(2,1)}, bf16[4,2,2,128,1024]{4,3,2,1,0:T(8,128)(2,1)}...) custom-call(bf16[128,1024]{1,0:T(8,128)(2,1)} %refs_0_.1, ...), custom_call_target="tpu_custom_call" | custom-call | tf_op jit(solution)/shard_map/forward_gather/pallas_call | solution.py:491
  435.3 16.1 %convert_reduce_fusion = (f32[4096]{0:T(1024)S(1)}, bf16[640,4096]{1,0:T(8,128)(2,1)S(1)}) fusion(bf16[640,4096]{1,0:T(8,128)(2,1)} %get-tuple-element.47, bf16[640,2048]{1,0:T(8,128)(2,1)} %get-tuple-element.45, bf16[2048,4096]{1,0:T(8,128)(2,1)} %bitcast.142), kind=kOutput, calls=%fused_computation.8 | convolution fusion | flops 10750521344 | bytes 29900800 | tf_op jit(solution)/shard_map/dot_general | solution.py:835
  451.5 2.3 copy-done.9
  453.8 15.7 %convolution_convert_fusion = bf16[640,2048]{1,0:T(8,128)(2,1)} fusion(bf16[640,4096]{1,0:T(8,128)(2,1)S(1)} %get-tuple-element.148.refs_2_, bf16[2048,4096]{1,0:T(8,128)(2,1)} %bitcast.141), kind=kOutput, calls=%fused_computation.15 | convolution fusion | flops 10738728960 | bytes 24641536 | tf_op jit(solution)/shard_map/dot_general | solution.py:41
  470.6 55.2 %reduce-scatter.3.cloned.1.call-done = bf16[320,2048]{1,0:T(8,128)(2,1)} async-done(((bf16[640,2048]{1,0:T(8,128)(2,1)}), bf16[320,2048]{1,0:T(8,128)(2,1)}) %reduce-scatter.3.cloned.1.call-update) | async-done | bytes 1310736 | tf_op jit(solution)/shard_map/reduce_scatter | solution.py:839
  525.8 4.2 multiply_reduce_fusion.1
  530.0 3.6 convert_reduce_fusion.1
  534.3 4.1 fusion.18
  538.5 2.7 copy.114
  541.1 2.5 copy.115
  543.6 4.8 fusion
  548.5 2.8 exponential_reduce_fusion
  551.2 1.9 copy-done
  553.2 19.6 %all-gather.2.cloned.1.call-done = bf16[640,2048]{1,0:T(8,128)(2,1)} async-done(((bf16[320,2048]{1,0:T(8,128)(2,1)}), bf16[640,2048]{1,0:T(8,128)(2,1)}) %all-gather.2.cloned.1.call-update) | async-done | bytes 2621456 | tf_op jit(solution)/shard_map/all_gather | solution.py:847
  572.8 6.9 convolution_convert_fusion.1
  579.7 2.4 copy.116
  582.1 8.7 convert_reduce_fusion.2
  591.7 7.5 multiply_reduce_fusion
  599.2 7.3 multiply_convert_fusion
  606.5 1.5 convert_reduce_fusion.3
  608.1 2.1 multiply_convert_fusion.2
  610.7 4.7 fusion.21
  615.4 4.6 fusion.20
  620.0 6.9 add_convert_fusion
  627.0 4.4 copy.103
  631.4 4.5 copy.100
  635.9 4.5 copy.102
  641.1 23.6 %reduce-scatter.5.cloned.1.call-done = bf16[320,2048]{1,0:T(8,128)(2,1)} async-done(((bf16[640,2048]{1,0:T(8,128)(2,1)}), bf16[320,2048]{1,0:T(8,128)(2,1)}) %reduce-scatter.5.cloned.1.call-update) | async-done | bytes 1310736 | tf_op jit(solution)/shard_map/reduce_scatter | solution.py:889
  664.8 2.9 fusion.9
  667.7 2.0 copy.127
  670.2 9.4 reduce.6
  679.6 4.4 reshape.199
  684.0 6.0 all-to-all-start.1
  690.0 2.6 copy.112.refs_6_
  692.7 1.5 copy.111.refs_5_
  694.1 1.5 copy.110.refs_4_
  695.6 4.6 copy.101
  700.2 9.2 pad_maximum_fusion.refs_0_
  709.4 317.8 %scatter_grads.1 = (f32[128,4096]{1,0:T(8,128)}, f32[128,4096]{1,0:T(8,128)}, f32[128,1024]{1,0:T(8,128)}, f32[128,1024]{1,0:T(8,128)}, f32[128,1024]{1,0:T(8,12...) custom-call(bf16[4,4,2,2,128,640]{5,4,3,2,1,0:T(8,128)(2,1)} %pad_ma, ...), custom_call_target="tpu_custom_call" | custom-call | tf_op jit(solution)/shard_map/scatter_grads/pallas_call | solution.py:746
  1027.3 2.9 copy.106
  1032.5 4.5 reshape.200
  1037.0 8.7 bitcast_reduce_fusion
  1045.7 2.2 reshape.190
  1049.2 1.8 copy.104
  (141 shorter events, 20.7 us)
Async XLA Ops:
  7.8 0.7 copy-start.33
  11.2 9.0 copy-start.40
  11.2 10.9 %copy-start.15 = (bf16[4096,128]{1,0:T(8,128)(2,1)S(1)}, bf16[4096,128]{1,0:T(8,128)(2,1)}, u32[]{:S(2)}) copy-start(bf16[4096,128]{1,0:T(8,128)(2,1)} %param.33) | copy-start | bytes 3145732
  12.6 10.9 %copy-start.21 = (bf16[1024,128]{1,0:T(8,128)(2,1)S(1)}, bf16[1024,128]{1,0:T(8,128)(2,1)}, u32[]{:S(2)}) copy-start(bf16[1024,128]{1,0:T(8,128)(2,1)} %param.27) | copy-start | bytes 786436
  12.6 12.4 %copy-start.41 = (s32[16]{0:T(128)S(1)}, s32[16]{0:T(128)}, u32[]{:S(2)}) copy-start(s32[16]{0:T(128)} %param.20) | copy-start | bytes 196
  12.6 13.6 %copy-start.35 = (f32[2048]{0:T(1024)S(1)}, f32[2048]{0:T(1024)}, u32[]{:S(2)}) copy-start(f32[2048]{0:T(1024)} %param.25) | copy-start | bytes 24580
  12.6 13.7 %copy-start.36 = (f32[2048]{0:T(1024)S(1)}, f32[2048]{0:T(1024)}, u32[]{:S(2)}) copy-start(f32[2048]{0:T(1024)} %param.26) | copy-start | bytes 24580
  12.6 13.7 %copy-start.28 = (f32[2048]{0:T(1024)S(1)}, f32[2048]{0:T(1024)}, u32[]{:S(2)}) copy-start(f32[2048]{0:T(1024)} %param.28) | copy-start | bytes 24580
  12.6 13.7 %copy-start.22 = (f32[2048]{0:T(1024)S(1)}, f32[2048]{0:T(1024)}, u32[]{:S(2)}) copy-start(f32[2048]{0:T(1024)} %param.29) | copy-start | bytes 24580
  12.7 13.7 %copy-start.29 = (f32[2048]{0:T(1024)S(1)}, f32[2048]{0:T(1024)}, u32[]{:S(2)}) copy-start(f32[2048]{0:T(1024)} %param.30) | copy-start | bytes 24580
  12.7 13.7 %copy-start.27 = (f32[8192]{0:T(1024)S(1)}, f32[8192]{0:T(1024)}, u32[]{:S(2)}) copy-start(f32[8192]{0:T(1024)} %param.32) | copy-start | bytes 98308
  12.7 13.7 %copy-start.30 = (f32[2048]{0:T(1024)S(1)}, f32[2048]{0:T(1024)}, u32[]{:S(2)}) copy-start(f32[2048]{0:T(1024)} %param.34) | copy-start | bytes 24580
  12.7 13.7 %copy-start.31 = (f32[2048]{0:T(1024)S(1)}, f32[2048]{0:T(1024)}, u32[]{:S(2)}) copy-start(f32[2048]{0:T(1024)} %param.35) | copy-start | bytes 24580
  12.7 13.7 %copy-start.32 = (f32[2048]{0:T(1024)S(1)}, f32[2048]{0:T(1024)}, u32[]{:S(2)}) copy-start(f32[2048]{0:T(1024)} %param.36) | copy-start | bytes 24580
  12.7 39.5 %all-to-all-start = ((bf16[16,1,20,2048]{3,2,1,0:T(8,128)(2,1)}), bf16[16,1,20,2048]{3,2,1,0:T(8,128)(2,1)S(1)}, u32[]{:S(2)}, u32[]{:S(2)}) async-start(bf16[16,1,20,2048]{3,2,1,0:T(8,128)(2,1)} %fusion.8), calls=%async_computation | async-start | bytes 3145728 | tf_op jit(solution)/shard_map/all_to_all | solution.py:798
  20.2 505.6 %reduce-scatter.3.cloned.1.call-start = ((), (), s32[]{:S(2)}) async-start(), calls=%async_computation.4 | async-start | bytes 3932160 | tf_op jit(solution)/shard_map/reduce_scatter | solution.py:839
  26.5 27.5 %copy-start.25 = (f32[18432]{0:T(1024)}, f32[18432]{0:T(1024)S(1)}, u32[]{:S(2)}) copy-start(f32[18432]{0:T(1024)S(1)} %constant_dynamic-update-slice_fusion) | copy-start | bytes 221188
  451.5 2.3 copy-start.9
  469.5 1.0 copy-start.26
  469.5 103.3 %all-gather.2.cloned.1.call-start = ((), (), s32[]{:S(2)}) async-start(), calls=%async_computation.5 | async-start | bytes 3932160 | tf_op jit(solution)/shard_map/all_gather | solution.py:847
  533.6 131.1 %reduce-scatter.5.cloned.1.call-start = ((), (), s32[]{:S(2)}) async-start(), calls=%async_computation.6 | async-start | bytes 3932160 | tf_op jit(solution)/shard_map/reduce_scatter | solution.py:889
  548.4 4.7 copy-start
  582.1 8.8 copy-start.1
  582.1 9.2 copy-start.10
  582.1 9.5 copy-start.11
  590.9 29.2 %copy-start.14 = (bf16[8,128,640]{2,1,0:T(8,128)(2,1)}, bf16[8,128,640]{2,1,0:T(8,128)(2,1)S(1)}, u32[]{:S(2)}) copy-start(bf16[8,128,640]{2,1,0:T(8,128)(2,1)S(1)} %get-tuple-element.146) | copy-start | bytes 3932164
  599.2 7.3 copy-start.2
  606.5 1.5 copy-start.3
  608.0 7.3 copy-start.5
  608.1 2.7 copy-start.39
  610.1 5.3 copy-start.7
  610.7 4.7 copy-start.38
  615.4 4.6 copy-start.37
  635.9 5.1 copy-start.20
  684.0 8.7 copy-start.8
  684.0 348.5 %all-to-all-start.1 = ((bf16[16,2,20480]{2,1,0:T(2,128)(2,1)}), bf16[16,2,20480]{2,1,0:T(2,128)(2,1)}, u32[]{:S(2)}, u32[]{:S(2)}) async-start(bf16[16,2,20480]{2,1,0:T(2,128)(2,1)} %reshape.199), calls=%async_computation.3 | async-start | bytes 2621440 | tf_op jit(solution)/shard_map/all_to_all | solution.py:893
  690.0 4.1 copy-start.6
  695.6 4.6 copy-start.4
  700.2 9.2 copy-start.23
  1027.3 3.0 copy-start.19
  1027.3 4.0 copy-start.24
  1045.7 2.4 copy-start.34
  1049.2 1.8 copy-start.13
  1049.2 2.9 copy-start.18
  1049.2 3.7 copy-start.17
  1051.0 2.7 copy-start.16
  1051.0 3.5 copy-start.12
Sparse Core Ops, SparseCore 0:
  469.6 56.1 reduce-scatter.2
  533.7 38.9 all-gather.1
  627.1 37.5 reduce-scatter.4

commit v4 on v3

--- a/solution.py
+++ b/solution.py
@@ -21,16 +21,6 @@
     return (normed * scale_gain + bias_shift, normed, inverse)
 
 
-def norm_backward(grad_out, scale_gain, normed, inverse):
-    scaled = grad_out * scale_gain
-    grad_in = inverse * (
-        scaled
-        - jnp.mean(scaled, axis=-1, keepdims=True)
-        - normed * jnp.mean(scaled * normed, axis=-1, keepdims=True)
-    )
-    return (grad_in, jnp.sum(grad_out * normed, axis=0), jnp.sum(grad_out, axis=0))
-
-
 def contract_rows(left, right):
     return lax.dot_general(
         left, right, (((0,), (0,)), ((), ())), preferred_element_type=jnp.float32
@@ -42,19 +32,6 @@
         left, right, (((1,), (1,)), ((), ())), preferred_element_type=jnp.float32
     )
 
-
-def attention_scores(query_rows, key_rows, key_valid, factor):
-    scores = (
-        jnp.einsum("qhd,khd->hqk", query_rows, key_rows, preferred_element_type=jnp.float32)
-        * factor
-    )
-    return jnp.where(key_valid[None, None, :], scores, MASKED)
-
-
-def place_slice(local_sum, full_size, offset):
-    return lax.dynamic_update_slice_in_dim(
-        jnp.zeros((full_size,), jnp.float32), local_sum, offset, 0
-    )
 
 MESH = pl.DeviceIdType.MESH
 TILE = 1024
@@ -518,109 +495,146 @@
         ),
         name="forward_gather",
     )(*shard_list, own, cot, mask, vectors)
-    weights = [array.reshape(-1, array.shape[-1]) for array in results[: len(shard_list)]]
-    return weights, results[len(shard_list) :]
-
-
-def scatter_kernel(planes, jobs, widths, *refs):
-    lefts, rights = 4, len(widths)
-    left_ref, right_refs, small_ref = refs[0], refs[1 : 1 + rights], refs[1 + rights]
-    outs = refs[2 + rights :]
-    grad_refs, small_out = outs[:rights], outs[rights]
-    left_far, right_fars = outs[rights + 1], outs[rights + 2 : rights + 2 + rights]
+    return results[: len(shard_list)], results[len(shard_list) :]
+
+
+JOB = 512
+
+
+def backward_kernel(planes, *refs):
     (
-        left_buf, right_buf, stage, x_land, plane_land, out_buf, small_land,
-        left_sem, right_sem, out_sem, core_send, core_recv, left_send, left_recv,
-        x_send, x_recv, plane_send, plane_recv, small_send, small_recv,
-    ) = outs[2 * rights + 2 :]
+        query_w, key_w, value_w, out_w, up_w, down_w,
+        x_in, qkv_in, mixed_in, normed_in, inverse_in, hidden_in, active_in, slope_in, down_in, second_in,
+        sums_in, mask_ref, gain_ref,
+    ) = refs[:19]
+    (
+        grad_query, grad_key, grad_value, grad_out_w, grad_up, grad_down, small_out, own_out,
+        left_own, left_far, active_far, rise_own, rise_far, mixed_far, qkv_own, qkv_far,
+    ) = refs[19:35]
+    (
+        left_buf, right_buf, stage, x_land, plane_land, out_buf, tile_buf, wide_buf, low_buf, rise_buf,
+        slope_buf, acc_buf, hidden_land, send_buf, qkv_buf, turn_buf, input_land, row_buf, inverse_buf,
+        sums_buf, small_land,
+        left_sem, right_sem, out_sem, core_send, core_recv, left_send, left_recv, x_send, x_recv,
+        plane_send, plane_recv, small_send, small_recv, tile_sem, wide_sem, slope_sem, load_sem, store_sem,
+        turn_sem, hidden_send, hidden_recv, input_send, input_recv, row_sem,
+    ) = refs[35:]
     plane, across, core, tensor = place()
-    tokens = left_ref.shape[-1]
     far = [lax.rem(plane + k, planes) for k in range(planes)]
     x_peer = device_of(plane, 1 - across, core, tensor)
     core_peer = device_of(plane, across, 1 - core, tensor)
     y_peer = device_of(plane, across, core, 1 - tensor)
-    plane_peers = [device_of(far[k], across, core, tensor) for k in range(1, planes)]
-    enter(plane_peers + [x_peer, core_peer, y_peer])
+    plane_peers = [device_of(far[k], across, core, tensor) for k in range(planes)]
+    tokens, features = low_buf.shape
+    half = tokens // 2
+    head_cols = mixed_in.shape[1]
+    heads = head_cols // HEAD_DIM
+    up_cols = active_in.shape[1]
+    block = features // planes
+    factor = HEAD_DIM ** (-0.5)
+    slots = x_land.shape[0]
+    thin = tile_buf.shape[-1]
+
+    jobs = [(0, active_in, active_far, s, grad_down, s) for s in range(0, up_cols, JOB)]
+    jobs += [(1, rise_own, rise_far, s, grad_up, s) for s in range(0, up_cols, JOB)]
+    jobs += [(2, mixed_in, mixed_far, s, grad_out_w, s) for s in range(0, head_cols, JOB)]
+    for which, result in enumerate((grad_query, grad_key, grad_value)):
+        jobs += [
+            (3, qkv_own, qkv_far, which * head_cols + s, result, s) for s in range(0, head_cols, JOB)
+        ]
     total = len(jobs)
+    up_first, out_first, qkv_first = (
+        [job[0] for job in jobs].index(a) for a in (1, 2, 3)
+    )
+
+    def local(source, target, sem):
+        return pltpu.make_async_copy(source, target, sem)
+
+    def remote(source, target, send, recv, peer):
+        return pltpu.make_async_remote_copy(
+            source, target, send, recv, device_id=peer, device_id_type=MESH
+        )
 
     def left_out(a):
-        return pltpu.make_async_remote_copy(
-            left_ref.at[a, :, :, 1 - core], left_far.at[a], left_send.at[a], left_recv.at[a],
-            device_id=core_peer, device_id_type=MESH,
-        )
-
-    def right_out(c):
-        _, i, start = jobs[c]
-        return pltpu.make_async_remote_copy(
-            right_refs[i].at[:, pl.ds(start, TILE)], right_fars[i].at[:, pl.ds(start, TILE)],
-            core_send.at[c], core_recv.at[c], device_id=core_peer, device_id_type=MESH,
-        )
-
-    def left_load(a, slot):
-        mine = [
-            pltpu.make_async_copy(
-                left_ref.at[a, :, side, core], left_buf.at[slot, side, :, :, pl.ds(0, tokens)],
-                left_sem.at[slot, 0, side],
+        return remote(
+            turn_buf.at[:, :, 1 - core], left_far.at[a], left_send.at[a], left_recv.at[a], core_peer
+        )
+
+    def left_keep(a):
+        return local(turn_buf.at[:, :, core], left_own.at[a], turn_sem.at[0])
+
+    kept = set()
+
+    def left_kept(a):
+        if a not in kept:
+            kept.add(a)
+            left_keep(a).wait()
+
+    def turn(a, source):
+        if a > 0:
+            left_out(a - 1).wait_send()
+            left_kept(a - 1)
+
+        @pl.loop(0, planes)
+        def _(p):
+            cols = pl.ds(pl.multiple_of(p * block, block), block)
+            turn_buf[p] = source[:, cols].T.reshape(turn_buf.shape[1:])
+
+        left_keep(a).start()
+        left_out(a).start()
+
+    def right_out(c, source=None):
+        _, own, other, start, _, _ = jobs[c]
+        cols = pl.ds(start, JOB)
+        return remote(
+            (own if source is None else source).at[:, cols], other.at[:, cols], core_send.at[c],
+            core_recv.at[c], core_peer,
+        )
+
+    def left_load(a):
+        slot = a % 2
+        copies = []
+        for side in range(2):
+            copies.append(
+                local(left_own.at[a, :, side], left_buf.at[slot, side, :, :, pl.ds(0, tokens)], left_sem.at[slot, 0, side])
             )
-            for side in range(2)
+            copies.append(
+                local(left_far.at[a, :, side], left_buf.at[slot, side, :, :, pl.ds(tokens, tokens)], left_sem.at[slot, 1, side])
+            )
+        return copies
+
+    def right_load(c):
+        _, own, other, start, _, _ = jobs[c]
+        slot, cols = c % 2, pl.ds(start, JOB)
+        return [
+            local(own.at[:, cols], right_buf.at[slot, pl.ds(0, tokens)], right_sem.at[slot, 0]),
+            local(other.at[:, cols], right_buf.at[slot, pl.ds(tokens, tokens)], right_sem.at[slot, 1]),
         ]
-        theirs = [
-            pltpu.make_async_copy(
-                left_far.at[a, :, side], left_buf.at[slot, side, :, :, pl.ds(tokens, tokens)],
-                left_sem.at[slot, 1, side],
-            )
-            for side in range(2)
-        ]
-        return mine + theirs
-
-    def right_load(c):
-        _, i, start = jobs[c]
-        slot = c % 2
-        cols = pl.ds(start, TILE)
-        return [
-            pltpu.make_async_copy(
-                right_refs[i].at[:, cols], right_buf.at[slot, pl.ds(0, tokens)], right_sem.at[slot, 0]
-            ),
-            pltpu.make_async_copy(
-                right_fars[i].at[:, cols], right_buf.at[slot, pl.ds(tokens, tokens)], right_sem.at[slot, 1]
-            ),
-        ]
 
     def x_out(c):
-        return pltpu.make_async_remote_copy(
-            stage.at[c % 3, 1 - across], x_land.at[c], x_send.at[c], x_recv.at[c],
-            device_id=x_peer, device_id_type=MESH,
+        return remote(
+            stage.at[c % 3, 1 - across], x_land.at[c % slots], x_send.at[c], x_recv.at[c], x_peer
         )
 
     def plane_out(c, k):
-        return pltpu.make_async_remote_copy(
-            x_land.at[c, far[k]], plane_land.at[c, k - 1], plane_send.at[c, k - 1], plane_recv.at[c, k - 1],
-            device_id=plane_peers[k - 1], device_id_type=MESH,
+        return remote(
+            x_land.at[c % slots, far[k]], plane_land.at[c % slots, k - 1], plane_send.at[c, k - 1],
+            plane_recv.at[c, k - 1], plane_peers[k],
         )
 
     def grad_out(c):
-        _, i, start = jobs[c]
-        return pltpu.make_async_copy(
-            out_buf.at[c % 2], grad_refs[i].at[:, pl.ds(start, TILE)], out_sem.at[c % 2]
-        )
-
-    order = []
-    for a, _, _ in jobs:
-        if a not in order:
-            order.append(a)
-    seen = set()
-    for c in range(total):
-        a = jobs[c][0]
-        if a not in seen:
-            seen.add(a)
-            left_out(a).start()
-        right_out(c).start()
+        _, _, _, _, result, start = jobs[c]
+        return local(out_buf.at[c % 2], result.at[:, pl.ds(start, JOB)], out_sem.at[c % 2])
+
+    def new_left(c):
+        return c == 0 or jobs[c - 1][0] != jobs[c][0]
 
     def fetch(c):
         a = jobs[c][0]
-        if c == 0 or jobs[c - 1][0] != a:
+        if new_left(c):
+            left_kept(a)
             left_out(a).wait_recv()
-            for copy in left_load(a, order.index(a) % 2):
+            for copy in left_load(a):
                 copy.start()
         right_out(c).wait_recv()
         for copy in right_load(c):
@@ -628,9 +642,8 @@
 
     def multiply(c):
         a = jobs[c][0]
-        slot = order.index(a) % 2
-        if c == 0 or jobs[c - 1][0] != a:
-            for copy in left_load(a, slot):
+        if new_left(c):
+            for copy in left_load(a):
                 copy.wait()
         for copy in right_load(c):
             copy.wait()
@@ -639,10 +652,10 @@
         if c >= 3:
             x_out(c - 3).wait_send()
 
-        @pl.loop(0, TILE // 256)
+        @pl.loop(0, JOB // 256)
         def _(n):
             cols = pl.ds(pl.multiple_of(n * 256, 256), 256)
-            left = left_buf[slot]
+            left = left_buf[a % 2]
             result = jnp.dot(
                 left.reshape(-1, left.shape[-1]), right_buf[c % 2, :, cols],
                 preferred_element_type=jnp.float32,
@@ -653,11 +666,12 @@
 
     def fold(c):
         x_out(c).wait_recv()
+        slot = c % slots
 
         @pl.loop(0, planes)
         def _(p):
-            x_land[c, p] = (
-                x_land[c, p].astype(jnp.float32) + stage[c % 3, across, p].astype(jnp.float32)
+            x_land[slot, p] = (
+                x_land[slot, p].astype(jnp.float32) + stage[c % 3, across, p].astype(jnp.float32)
             ).astype(jnp.bfloat16)
 
         for k in range(1, planes):
@@ -665,29 +679,26 @@
 
     def finish(c):
         for k in range(1, planes):
-            plane_out(c, k).wait_recv()
+            plane_out(c, k).wait()
         if c >= 2:
             grad_out(c - 2).wait()
-        value = x_land[c, plane].astype(jnp.float32)
+        value = x_land[c % slots, plane].astype(jnp.float32)
         for k in range(1, planes):
-            value += plane_land[c, k - 1].astype(jnp.float32)
+            value += plane_land[c % slots, k - 1].astype(jnp.float32)
         out_buf[c % 2] = value
         grad_out(c).start()
 
     def small_copy(step, peer, slot):
-        return pltpu.make_async_remote_copy(
-            small_land.at[0], small_land.at[slot], small_send.at[step], small_recv.at[step],
-            device_id=peer, device_id_type=MESH,
+        return remote(
+            small_land.at[0], small_land.at[slot], small_send.at[step], small_recv.at[step], peer
         )
 
     def small_begin(step):
         if step < 3:
-            if step == 0:
-                pltpu.sync_copy(small_ref, small_land.at[0])
             small_copy(step, (core_peer, x_peer, y_peer)[step], 1 + step).start()
         else:
             for k in range(1, planes):
-                small_copy(2 + k, plane_peers[k - 1], 3 + k).start()
+                small_copy(2 + k, plane_peers[k], 3 + k).start()
 
     def small_end(step):
         if step < 3:
@@ -701,74 +712,389 @@
                 back = lax.rem(plane + planes - p, planes)
                 value += small_land[jnp.where(back == 0, 0, 3 + back)]
             small_land[1] = value
-            pltpu.sync_copy(small_land.at[1], small_out)
-
+            local(small_land.at[1], small_out, load_sem.at[0]).start()
+
+    def total_row(value):
+        return jnp.sum(value, axis=0, keepdims=True)
+
+    def tile_copy(weight, start, slot):
+        return [
+            local(weight.at[p, :, :, :, pl.ds(start, thin)], tile_buf.at[slot, p], tile_sem.at[slot, p])
+            for p in range(planes)
+        ]
+
+    def slope_copy(start, slot):
+        return local(slope_in.at[:, pl.ds(start, thin)], slope_buf.at[slot], slope_sem.at[slot])
+
+    def flat(value):
+        return value.reshape(-1, value.shape[-1])
+
+    def rise_start(i):
+        for copy in tile_copy(down_w, i * thin, i % 2):
+            copy.start()
+        slope_copy(i * thin, i % 2).start()
+
+    def rise_store(g):
+        cols = pl.ds(g * 2 * JOB, 2 * JOB)
+        return local(rise_buf.at[:, cols], rise_own.at[:, cols], store_sem.at[g])
+
+    def rise(g):
+        per = 2 * JOB // thin
+        for i in range(g * per, (g + 1) * per):
+            for copy in tile_copy(down_w, i * thin, i % 2):
+                copy.wait()
+            slope_copy(i * thin, i % 2).wait()
+            value = jnp.dot(low_buf[...], flat(tile_buf[i % 2]), preferred_element_type=jnp.float32)
+            value = (value * slope_buf[i % 2].astype(jnp.float32)).astype(jnp.bfloat16)
+            rise_buf[:, i * thin : (i + 1) * thin] = value
+            if i + 2 < up_cols // thin:
+                rise_start(i + 2)
+            row = 3 + tensor * (up_cols // features) + (i * thin) // features
+            col = (i * thin) % features
+            small_land[0, pl.ds(row, 1), col : col + thin] = total_row(value.astype(jnp.float32))
+        rise_store(g).start()
+        for c in (up_first + 2 * g, up_first + 2 * g + 1):
+            right_out(c, rise_buf).start()
+
+    def block_cols(p):
+        return pl.ds(pl.multiple_of(p * block, block), block)
+
+    def wide_copy(p, side):
+        return local(
+            up_w.at[p, :, :, :, pl.ds(side * features, features)], wide_buf.at[side], wide_sem.at[side, 0]
+        )
+
+    def hidden_share(p):
+        return remote(
+            send_buf.at[:, block_cols(p)], hidden_land.at[:, block_cols(p)], hidden_send.at[p],
+            hidden_recv.at[p], y_peer,
+        )
+
+    def hidden_start():
+        for side in range(2):
+            wide_copy(0, side).start()
+
+    def hidden_back(first, last):
+        @pl.loop(first, last)
+        def _(p):
+            value = None
+            for side in range(2):
+                wide_copy(p, side).wait()
+                part = contract_cols(
+                    rise_buf[:, side * features : (side + 1) * features], flat(wide_buf[side])
+                )
+                value = part if value is None else value + part
+
+                @pl.when(p + 1 < planes)
+                def _():
+                    wide_copy(p + 1, side).start()
+
+            acc_buf[:, block_cols(p)] = value
+            send_buf[:, block_cols(p)] = value.astype(jnp.bfloat16)
+            hidden_share(p).start()
+
+    strip = row_buf.shape[2]
+
+    def row_start(which, i):
+        base = tensor if which == 0 else 1 - tensor
+        return pl.multiple_of(base * half + i * strip, strip)
+
+    def row_copies(which, i):
+        rows = pl.ds(row_start(which, i), strip)
+        slot = (which * (half // strip) + i) % 2
+        return [
+            local(normed_in.at[rows], row_buf.at[slot, 0], row_sem.at[slot, 0]),
+            local(second_in.at[rows], row_buf.at[slot, 1], row_sem.at[slot, 1]),
+        ]
+
+    strips = [(which, i) for which in range(2) for i in range(half // strip)]
+
+    def norm_start():
+        for pair in strips[:2]:
+            for copy in row_copies(*pair):
+                copy.start()
+        local(inverse_in, inverse_buf, load_sem.at[1]).start()
+
+    def norm_back():
+        @pl.loop(0, planes)
+        def _(p):
+            hidden_share(p).wait()
+
+        local(inverse_in, inverse_buf, load_sem.at[1]).wait()
+        sums_buf[...] = jnp.zeros_like(sums_buf)
+        for at, (which, i) in enumerate(strips):
+            for copy in row_copies(which, i):
+                copy.wait()
+
+            @pl.loop(0, strip // 16)
+            def _(r):
+                local_rows = pl.ds(pl.multiple_of(r * 16, 16), 16)
+                rows = pl.ds(pl.multiple_of(row_start(which, i) + r * 16, 16), 16)
+                normed = row_buf[at % 2, 0, local_rows, :]
+                grad_hidden = row_buf[at % 2, 1, local_rows, :] + (
+                    acc_buf[rows, :] + hidden_land[rows, :].astype(jnp.float32)
+                )
+                scaled = grad_hidden * gain_ref[...]
+                grad = inverse_buf[rows, 0:1] * (
+                    scaled
+                    - jnp.mean(scaled, axis=-1, keepdims=True)
+                    - normed * jnp.mean(scaled * normed, axis=-1, keepdims=True)
+                )
+                acc_buf[rows, :] = grad
+                low = grad.astype(jnp.bfloat16)
+                low_buf[rows, :] = low
+                if which == 0:
+                    sums_buf[0] += grad_hidden * normed
+                    sums_buf[1] += grad_hidden
+                    sums_buf[2] += low.astype(jnp.float32)
+
+            if at + 2 < len(strips):
+                for copy in row_copies(*strips[at + 2]):
+                    copy.start()
+        small_land[0, 8:9, :] = total_row(sums_buf[0])
+        small_land[0, 9:10, :] = total_row(sums_buf[1])
+        small_land[0, 2:3, :] = total_row(sums_buf[2])
+
+    def mixed_start():
+        for i in range(2):
+            for copy in tile_copy(out_w, i * thin, i):
+                copy.start()
+        for g in range(up_cols // (2 * JOB)):
+            for c in (up_first + 2 * g, up_first + 2 * g + 1):
+                right_out(c, rise_buf).wait_send()
+        local(qkv_in, rise_buf.at[:, pl.ds(0, 3 * head_cols)], load_sem.at[2]).start()
+
+    def mixed_back():
+        for i in range(head_cols // thin):
+            for copy in tile_copy(out_w, i * thin, i % 2):
+                copy.wait()
+            value = jnp.dot(low_buf[...], flat(tile_buf[i % 2]), preferred_element_type=jnp.float32)
+            start = 3 * head_cols + i * thin
+            rise_buf[:, start : start + thin] = value.astype(jnp.bfloat16)
+            if i + 2 < head_cols // thin:
+                for copy in tile_copy(out_w, (i + 2) * thin, i % 2):
+                    copy.start()
+
+    def attend_back(first, last):
+        @pl.loop(first, last)
+        def _(h):
+            def cols(which):
+                return pl.ds(pl.multiple_of(which * head_cols + h * HEAD_DIM, HEAD_DIM), HEAD_DIM)
+
+            key, value = rise_buf[:, cols(1)], rise_buf[:, cols(2)]
+            key_sum = value_sum = None
+            query_total = jnp.zeros((1, HEAD_DIM), jnp.float32)
+            for part in range(2):
+                rows = slice(part * half, (part + 1) * half)
+                query, grad_mixed = rise_buf[rows, cols(0)], rise_buf[rows, cols(3)]
+                scores = contract_cols(query, key) * factor
+                scores = jnp.where(mask_ref[0:1, :] > 0.0, scores, MASKED)
+                expanded = jnp.exp(scores - jnp.max(scores, axis=1, keepdims=True))
+                weight = expanded / jnp.sum(expanded, axis=1, keepdims=True)
+                grad_weight = contract_cols(grad_mixed, value)
+                inner = jnp.sum(weight * grad_weight, axis=1, keepdims=True)
+                grad_scores = (weight * (grad_weight - inner)).astype(jnp.bfloat16)
+                grad_value = contract_rows(weight.astype(jnp.bfloat16), grad_mixed)
+                grad_key = contract_rows(grad_scores, query)
+                grad_query = (
+                    jnp.dot(grad_scores, key, preferred_element_type=jnp.float32) * factor
+                ).astype(jnp.bfloat16)
+                qkv_buf[rows, cols(0)] = grad_query
+                query_total += total_row(grad_query.astype(jnp.float32))
+                key_sum = grad_key if key_sum is None else key_sum + grad_key
+                value_sum = grad_value if value_sum is None else value_sum + grad_value
+            qkv_buf[:, cols(1)] = (key_sum * factor).astype(jnp.bfloat16)
+            value_low = value_sum.astype(jnp.bfloat16)
+            qkv_buf[:, cols(2)] = value_low
+            at = pl.ds(pl.multiple_of(tensor * head_cols + h * HEAD_DIM, HEAD_DIM), HEAD_DIM)
+            small_land[0, 0:1, at] = query_total
+            small_land[0, 1:2, at] = total_row(value_low.astype(jnp.float32))
+
+    def attend_done():
+        local(qkv_buf, qkv_own, store_sem.at[4]).start()
+        for c in range(qkv_first, total):
+            right_out(c, qkv_buf).start()
+        input_start(0)
+
+    def input_copies(p):
+        return [
+            local(query_w.at[p], wide_buf.at[0, :, :, :, pl.ds(0, head_cols)], wide_sem.at[0, 0]),
+            local(key_w.at[p], wide_buf.at[0, :, :, :, pl.ds(head_cols, head_cols)], wide_sem.at[0, 1]),
+            local(value_w.at[p], wide_buf.at[1, :, :, :, pl.ds(0, head_cols)], wide_sem.at[1, 0]),
+        ]
+
+    def input_start(p):
+        for copy in input_copies(p):
+            copy.start()
+
+    own_rows = pl.ds(pl.multiple_of(tensor * half, half), half)
+    other_rows = pl.ds(pl.multiple_of((1 - tensor) * half, half), half)
+
+    def input_share(p):
+        return remote(
+            send_buf.at[pl.ds(0, half), block_cols(p)], input_land.at[:, block_cols(p)], input_send.at[p],
+            input_recv.at[p], y_peer,
+        )
+
+    def input_back(first, last):
+        @pl.loop(first, last)
+        def _(p):
+            for copy in input_copies(p):
+                copy.wait()
+            pair = flat(wide_buf[0])
+            single = flat(wide_buf[1, :, :, :, 0:head_cols])
+
+            def share(rows):
+                return contract_cols(qkv_buf[rows, 0 : 2 * head_cols], pair) + contract_cols(
+                    qkv_buf[rows, 2 * head_cols : 3 * head_cols], single
+                )
+
+            send_buf[0:half, block_cols(p)] = share(other_rows).astype(jnp.bfloat16)
+            input_share(p).start()
+            acc_buf[own_rows, block_cols(p)] += share(own_rows)
+
+            @pl.when(p + 1 < planes)
+            def _():
+                input_start(p + 1)
+
+    def input_done():
+        @pl.loop(0, planes)
+        def _(p):
+            input_share(p).wait()
+
+        @pl.loop(0, half // 16)
+        def _(i):
+            rows = pl.ds(pl.multiple_of(tensor * half + i * 16, 16), 16)
+            land = pl.ds(pl.multiple_of(i * 16, 16), 16)
+            send_buf[pl.ds(pl.multiple_of(half + i * 16, 16), 16), :] = (
+                acc_buf[rows, :] + input_land[land, :].astype(jnp.float32)
+            ).astype(jnp.bfloat16)
+
+        local(send_buf.at[pl.ds(half, half)], own_out, load_sem.at[3]).start()
+
+    local(down_in, low_buf, load_sem.at[0]).start()
+    local(hidden_in, send_buf, load_sem.at[1]).start()
+    local(sums_in, sums_buf, load_sem.at[2]).start()
+    rise_start(0)
+    rise_start(1)
+    enter(plane_peers[1:] + [x_peer, core_peer, y_peer])
+    for c in range(up_first):
+        right_out(c).start()
+    local(down_in, low_buf, load_sem.at[0]).wait()
+    turn(0, low_buf)
+    small_land[0] = jnp.zeros(small_land.shape[1:], jnp.float32)
+    local(sums_in, sums_buf, load_sem.at[2]).wait()
+    for i, row in enumerate((10, 11, 7)):
+        small_land[0, row : row + 1, :] = total_row(sums_buf[i])
     fetch(0)
-    for c in range(total + 2):
-        if c < total:
-            multiply(c)
-        if 1 <= c <= total:
-            fold(c - 1)
-        if c >= 2:
-            finish(c - 2)
-        if c in (1, 2, 3, 4):
-            small_end(c - 1)
-        if c in (0, 1, 2, 3):
-            small_begin(c)
-    for a in order:
-        left_out(a).wait_send()
+
+    def turn_hidden():
+        local(hidden_in, send_buf, load_sem.at[1]).wait()
+        turn(1, send_buf)
+
+    def stored():
+        for g in range(up_cols // (2 * JOB)):
+            rise_store(g).wait()
+
+    def load_input():
+        local(x_in, low_buf, load_sem.at[1]).start()
+
+    def turn_input():
+        local(x_in, low_buf, load_sem.at[1]).wait()
+        turn(3, low_buf)
+
+    def start_out():
+        for c in range(out_first, qkv_first):
+            right_out(c).start()
+
+    def wait_qkv():
+        local(qkv_in, rise_buf.at[:, pl.ds(0, 3 * head_cols)], load_sem.at[2]).wait()
+
+    def store_qkv_wait():
+        local(qkv_buf, qkv_own, store_sem.at[4]).wait()
+
+    plan = {
+        0: [(rise, 0)],
+        1: [(rise, 1)],
+        2: [(rise, 2)],
+        3: [(rise, 3), (turn_hidden,), (hidden_start,)],
+        4: [(hidden_back, 0, planes // 2)],
+        5: [(hidden_back, planes // 2, planes), (norm_start,), (start_out,), (stored,)],
+        10: [(norm_back,), (mixed_start,)],
+        11: [(turn, 2, low_buf), (mixed_back,), (load_input,)],
+        12: [(wait_qkv,), (attend_back, 0, heads // 4), (turn_input,)],
+        13: [(attend_back, heads // 4, heads // 2)],
+        14: [(attend_back, heads // 2, 3 * heads // 4)],
+        15: [(attend_back, 3 * heads // 4, heads), (attend_done,)],
+        16: [(input_back, 0, planes // 2), (small_begin, 0), (store_qkv_wait,)],
+        17: [(input_back, planes // 2, planes), (small_end, 0), (small_begin, 1)],
+        18: [(small_end, 1), (small_begin, 2)],
+        19: [(small_end, 2), (small_begin, 3)],
+        20: [(input_done,), (small_end, 3)],
+    }
+    for n in range(total + 4):
+        if n < total:
+            multiply(n)
+        for step in plan.get(n, []):
+            step[0](*step[1:])
+        if 2 <= n < total + 2:
+            fold(n - 2)
+        if n >= 4:
+            finish(n - 4)
+    local(small_land.at[1], small_out, load_sem.at[0]).wait()
+    local(send_buf.at[pl.ds(half, half)], own_out, load_sem.at[3]).wait()
+    left_out(3).wait_send()
     for c in range(total):
-        right_out(c).wait_send()
+        if not up_first <= c < out_first:
+            right_out(c).wait_send()
         if c >= total - 3:
             x_out(c).wait_send()
-        for k in range(1, planes):
-            plane_out(c, k).wait_send()
     for c in range(total - 2, total):
         grad_out(c).wait()
 
 
-def scatter_grads(lefts, rights, smalls):
-    size = lax.axis_size("dp")
-    planes = size // 4
-    tokens, features = lefts[0].shape
-    rows = features // size
-    left = jnp.stack([array.T for array in lefts]).reshape(4, planes, 2, 2, rows, tokens)
-    arrays = [array for array, _ in rights]
-    widths = [array.shape[1] for array in arrays]
-    jobs = [
-        (which, i, start)
-        for i, (array, which) in enumerate(rights)
-        for start in range(0, array.shape[1], TILE)
+def backward(weights, saved, mask, gain):
+    planes, _, _, rows, head_cols = weights[0].shape
+    up_cols = weights[4].shape[-1]
+    tokens, features = saved[0].shape
+    total = (2 * up_cols + 4 * head_cols) // JOB
+    slots = 8
+    thin, strip = 256, 64
+    sem, low, high = pltpu.SemaphoreType.DMA, jnp.bfloat16, jnp.float32
+    hbm, vmem = pl.BlockSpec(memory_space=pl.ANY), pl.BlockSpec(memory_space=pltpu.VMEM)
+    small_rows = 16
+    shapes = (
+        [((rows, head_cols), high)] * 4 + [((rows, up_cols), high)] * 2
+        + [((small_rows, features), high), ((tokens // 2, features), low)]
+        + [((4, planes, 2, rows, tokens), low)] * 2
+        + [((tokens, up_cols), low)] * 3 + [((tokens, head_cols), low)] + [((tokens, 3 * head_cols), low)] * 2
+    )
+    scratch = [
+        ((2, 2, planes, rows, 2 * tokens), low), ((2, 2 * tokens, JOB), low), ((3, 2, planes, rows, JOB), low),
+        ((slots, planes, rows, JOB), low), ((slots, planes - 1, rows, JOB), low), ((2, rows, JOB), high),
+        ((2, planes, 2, 2, rows, thin), low), ((2, 2, 2, rows, features), low), ((tokens, features), low),
+        ((tokens, up_cols), low), ((2, tokens, thin), low), ((tokens, features), high),
+        ((tokens, features), low), ((tokens, features), low), ((tokens, 3 * head_cols), low),
+        ((planes, 2, 2, rows, tokens), low), ((tokens // 2, features), low), ((2, 2, strip, features), high),
+        ((tokens, 128), high), ((3, 16, features), high), ((3 + planes, small_rows, features), high),
     ]
-    total = len(jobs)
-    sem = pltpu.SemaphoreType.DMA
-    hbm = pl.BlockSpec(memory_space=pl.ANY)
+    sems = [
+        (2, 2, 2), (2, 2), (2,), (total,), (total,), (4,), (4,), (total,), (total,),
+        (total, planes - 1), (total, planes - 1), (2 + planes,), (2 + planes,), (2, planes), (2, 2), (2,),
+        (4,), (5,), (1,), (planes,), (planes,), (planes,), (planes,), (2, 2),
+    ]
     results = pl.pallas_call(
-        partial(scatter_kernel, planes, jobs, widths),
-        out_shape=[jax.ShapeDtypeStruct((rows, width), jnp.float32) for width in widths]
-        + [jax.ShapeDtypeStruct(smalls.shape, jnp.float32)]
-        + [jax.ShapeDtypeStruct((4, planes, 2, rows, tokens), jnp.bfloat16)]
-        + [jax.ShapeDtypeStruct(array.shape, jnp.bfloat16) for array in arrays],
-        in_specs=[hbm] * (2 + len(arrays)),
-        out_specs=[hbm] * (2 + 2 * len(arrays)),
-        scratch_shapes=[
-            pltpu.VMEM((2, 2, planes, rows, 2 * tokens), jnp.bfloat16),
-            pltpu.VMEM((2, 2 * tokens, TILE), jnp.bfloat16),
-            pltpu.VMEM((3, 2, planes, rows, TILE), jnp.bfloat16),
-            pltpu.VMEM((total, planes, rows, TILE), jnp.bfloat16),
-            pltpu.VMEM((total, planes - 1, rows, TILE), jnp.bfloat16),
-            pltpu.VMEM((2, rows, TILE), jnp.float32),
-            pltpu.VMEM((3 + planes, *smalls.shape), jnp.float32),
-            sem((2, 2, 2)), sem((2, 2)), sem((2,)), sem((total,)), sem((total,)), sem((4,)), sem((4,)),
-            sem((total,)), sem((total,)), sem((total, planes - 1)), sem((total, planes - 1)),
-            sem((2 + planes,)), sem((2 + planes,)),
-        ],
+        partial(backward_kernel, planes),
+        out_shape=[jax.ShapeDtypeStruct(*shape) for shape in shapes],
+        in_specs=[hbm] * 17 + [vmem] * 2,
+        out_specs=[hbm] * len(shapes),
+        scratch_shapes=[pltpu.VMEM(*shape) for shape in scratch] + [sem(shape) for shape in sems],
         compiler_params=pltpu.CompilerParams(
-            collective_id=1, has_side_effects=True, vmem_limit_bytes=60 * 2**20
+            collective_id=1, has_side_effects=True, vmem_limit_bytes=62 * 2**20
         ),
-        name="scatter_grads",
-    )(left, *arrays, smalls)
-    return results[: len(arrays)], results[len(arrays)]
+        name="backward_scatter",
+    )(*weights, *saved, mask, gain)
+    return results[:6], results[6], results[7]
 
 
 def shards(
@@ -802,9 +1128,7 @@
     seq_len = half_rows * lax.axis_size("tensor")
     length = lengths[dealing[group_index]]
     key_valid = jnp.arange(seq_len) < length
-    factor = HEAD_DIM ** (-0.5)
     head_cols = w_query.shape[1]
-    heads_local = head_cols // HEAD_DIM
     up_cols = w_up.shape[1]
     query_bias = lax.dynamic_slice_in_dim(b_query, tensor_index * head_cols, head_cols)
     value_bias = lax.dynamic_slice_in_dim(b_value, tensor_index * head_cols, head_cols)
@@ -817,105 +1141,28 @@
         [w_query, w_key, w_value, w_out.T, w_up, w_down.T],
         own_rows, cotangent.reshape(half_rows, features), mask, vectors,
     )
-    query_full, key_full, value_full, out_turned, up_full, down_turned = weights
     (
         full_in, _, qkv, mixed_heads, normed_full, inverse_full, full_hidden, active, slope,
         result, full_grad_down, second_full, second_sums,
     ) = saved
     output = result.reshape(cotangent.shape)
-    own = partial(lax.dynamic_slice_in_dim, start_index=tensor_index * half_rows, slice_size=half_rows)
-    normed_first, inverse_first, grad_second = own(normed_full), own(inverse_full)[:, :1], own(second_full)
-    grad_gain_second, grad_shift_second, grad_b_down = jnp.sum(second_sums, axis=1)
-    query_rows, key_rows, value_rows = (
-        qkv[:, i * head_cols : (i + 1) * head_cols].reshape(seq_len, heads_local, HEAD_DIM) for i in range(3)
+    grads, small_total, grad_own = backward(
+        weights,
+        [
+            full_in, qkv, mixed_heads, normed_full, inverse_full, full_hidden, active, slope,
+            full_grad_down, second_full, second_sums,
+        ],
+        mask, gain_first.reshape(1, -1),
     )
-    scores = attention_scores(query_rows, key_rows, key_valid, factor)
-    row_max = jnp.max(scores, axis=-1, keepdims=True)
-    log_norm = row_max + jnp.log(jnp.sum(jnp.exp(scores - row_max), axis=-1, keepdims=True))
-    grad_active = jnp.dot(full_grad_down, down_turned, preferred_element_type=jnp.float32)
-    grad_up = (grad_active * slope.astype(jnp.float32)).astype(jnp.bfloat16)
-    grad_up_bias = jnp.sum(grad_up.astype(jnp.float32), axis=0)
-    hidden_part = contract_cols(grad_up, up_full)
-    grad_hidden = grad_second + lax.psum_scatter(
-        hidden_part.astype(jnp.bfloat16), "tensor", scatter_dimension=0, tiled=True
-    ).astype(jnp.float32)
-    grad_first, grad_gain_first, grad_shift_first = norm_backward(
-        grad_hidden, gain_first, normed_first, inverse_first
-    )
-    grad_attended = grad_first.astype(jnp.bfloat16)
-    grad_b_out = jnp.sum(grad_attended.astype(jnp.float32), axis=0)
-    full_grad_attended = lax.all_gather(grad_attended, "tensor", axis=0, tiled=True)
-    grad_mixed = jnp.dot(
-        full_grad_attended, out_turned, preferred_element_type=jnp.float32
-    ).astype(jnp.bfloat16)
-    grad_mixed = grad_mixed.reshape(seq_len, heads_local, HEAD_DIM)
-    scores = attention_scores(query_rows, key_rows, key_valid, factor)
-    softmax_again = jnp.exp(scores - log_norm)
-    grad_values = jnp.einsum(
-        "hqk,qhd->khd",
-        softmax_again.astype(jnp.bfloat16),
-        grad_mixed,
-        preferred_element_type=jnp.float32,
-    ).astype(jnp.bfloat16)
-    grad_softmax = jnp.einsum(
-        "qhd,khd->hqk", grad_mixed, value_rows, preferred_element_type=jnp.float32
-    )
-    row_inner = jnp.sum(softmax_again * grad_softmax, axis=-1, keepdims=True)
-    grad_scores = (softmax_again * (grad_softmax - row_inner)).astype(jnp.bfloat16)
-    grad_queries = (
-        (
-            jnp.einsum("hqk,khd->qhd", grad_scores, key_rows, preferred_element_type=jnp.float32)
-            * factor
-        )
-        .astype(jnp.bfloat16)
-        .reshape(seq_len, head_cols)
-    )
-    grad_keys = (
-        (
-            jnp.einsum("hqk,qhd->khd", grad_scores, query_rows, preferred_element_type=jnp.float32)
-            * factor
-        )
-        .astype(jnp.bfloat16)
-        .reshape(seq_len, head_cols)
-    )
-    grad_values = grad_values.reshape(seq_len, head_cols)
-    grad_query_bias = jnp.sum(grad_queries.astype(jnp.float32), axis=0)
-    grad_value_bias = jnp.sum(grad_values.astype(jnp.float32), axis=0)
-    input_part = (
-        contract_cols(grad_queries, query_full)
-        + contract_cols(grad_keys, key_full)
-        + contract_cols(grad_values, value_full)
-    )
-    grad_own = grad_first + lax.psum_scatter(
-        input_part.astype(jnp.bfloat16), "tensor", scatter_dimension=0, tiled=True
-    ).astype(jnp.float32)
-    grad_sent = grad_own.astype(jnp.bfloat16).reshape(1, 1, half_rows, features)
+    grad_sent = grad_own.reshape(1, 1, half_rows, features)
     returned = lax.all_to_all(grad_sent, "dp", split_axis=2, concat_axis=0, tiled=True)
     grad_inputs = jnp.zeros_like(returned).at[dealing].set(returned)
-    full_cols = b_query.shape[0]
-    full_up = b_up.shape[0]
-    smalls = (
-        place_slice(grad_query_bias, full_cols, tensor_index * head_cols),
-        place_slice(grad_value_bias, full_cols, tensor_index * head_cols),
-        grad_b_out,
-        place_slice(grad_up_bias, full_up, tensor_index * up_cols),
-        grad_b_down,
-        grad_gain_first,
-        grad_shift_first,
-        grad_gain_second,
-        grad_shift_second,
+    weight_sums = (grads[0], grads[1], grads[2], grads[3].T, grads[4], grads[5].T)
+    up_rows = b_up.shape[0] // features
+    small_sums = (
+        small_total[0], small_total[1], small_total[2], small_total[3 : 3 + up_rows].reshape(-1),
+        small_total[7], small_total[8], small_total[9], small_total[10], small_total[11],
     )
-    sums, small_total = scatter_grads(
-        [full_in, full_grad_attended, full_hidden, full_grad_down],
-        [(active, 3), (grad_up, 2), (mixed_heads, 1), (grad_queries, 0), (grad_keys, 0), (grad_values, 0)],
-        jnp.concatenate(smalls).reshape(-1, 128),
-    )
-    weight_sums = (sums[3], sums[4], sums[5], sums[2].T, sums[1], sums[0].T)
-    small_total = small_total.reshape(-1)
-    small_sums, at = [], 0
-    for small in smalls:
-        small_sums.append(small_total[at : at + small.shape[0]])
-        at += small.shape[0]
     return (
         output,
         grad_inputs,

time: 1080 us -> 860 us (0.80)
  matrix products: 79.6 us -> 0 us
  waiting for transfers between devices: 124 us -> 49 us
  local copies, waits for them, and re-layouts: 85.9 us -> 44.1 us
  other arithmetic: 43.4 us -> 12.7 us
  Pallas kernels: 699 us -> 725 us
  between operations: 16.9 us -> 3.46 us
    dot_general x11 -> x0, matrix products: 79.6 us -> none  [the longest x4 31.9 us: contract_cols(): lax.dot_general(left, right, (((1,), (1,)), ((), ())), preferred_element_...]
    reduce_scatter x2 -> x0, waiting for transfers between devices: 78.8 us -> none  [the longest x1 55.2 us: shards(): lax.psum_scatter(hidden_part.astype(jnp.bfloat16), 'tensor', scatter_dime...]
    pallas_call x1, Pallas kernels: 318 us -> 343 us  [backward(): pl.pallas_call(partial(backward_kernel, planes), out_shape=[jax.ShapeDtyp...]
    all_to_all x1, waiting for transfers between devices: 0.01 us -> 23.4 us  [shards(): lax.all_to_all(grad_sent, 'dp', split_axis=2, concat_axis=0, tiled=True)]
    all_gather x1 -> x0, waiting for transfers between devices: 19.6 us -> none  [shards(): lax.all_gather(grad_attended, 'tensor', axis=0, tiled=True)]
    transpose x4 -> x0, local copies, waits for them, and re-layouts: 18 us -> none  [scatter_grads(): left = jnp.stack([array.T for array in lefts]).reshape(4, planes, 2, 2, r...]
    reshape x7 -> x1, local copies, waits for them, and re-layouts: 15.2 us -> 3.34 us  [shards(): grad_sent = grad_own.reshape(1, 1, half_rows, features)]
    unnamed x114 -> x68, local copies, waits for them, and re-layouts: 30.8 us -> 24.3 us
  transfers between devices with their start and end apart: 5 -> 2, of which waited for: 4 -> 2; matrix products, arithmetic and copies ran while one was open for 6% -> 1% of each run, Pallas kernels for 30% -> 0%
where the time goes in v4:
time: 860 us; the launch traced here: 848 us
  Pallas kernels  725 us (84%)
  waiting for transfers between devices  49 us (6%)
  local copies, waits for them, and re-layouts  44.1 us (5%)
  starting transfers between devices  13.6 us (2%)
  other arithmetic  12.7 us (1%)
    pallas_call x1, Pallas kernels, forward(): pl.pallas_call(partial(forward_kernel, planes, widths), out_shape=[jax.Sh...  382 us
    pallas_call x1, Pallas kernels, backward(): pl.pallas_call(partial(backward_kernel, planes), out_shape=[jax.ShapeDtyp...  343 us
    all_to_all x1, waiting for transfers between devices, shards(): lax.all_to_all(ordered, 'dp', split_axis=0, concat_axis=2, tiled=True)  25.6 us
    unnamed x68, local copies, waits for them, and re-layouts  24.3 us
    all_to_all x1, waiting for transfers between devices, shards(): lax.all_to_all(grad_sent, 'dp', split_axis=2, concat_axis=0, tiled=True)  23.4 us
  transfers between devices with their start and end apart: 2, of which 2 were waited for; matrix products, arithmetic and copies ran while one was open for 1% of the time, Pallas kernels for 0%

profile of v4, /device:TPU:0, one launch (start us, length us, event | category | flops | bytes accessed | tf_op | source)
XLA Modules:
  0.0 847.6 jit_solution(4298710967855190180)
XLA Ops:
  0.7 0.7 compare_select_fusion
  1.3 0.7 compare_and_fusion
  2.0 2.0 copy.60
  4.0 0.6 gather_fusion
  4.7 1.4 fusion
  6.1 7.5 all-to-all-start
  13.6 0.0 copy-start.8
  13.6 0.0 copy-start.21
  13.6 0.0 copy-start.18
  13.6 0.0 copy-start.19
  13.6 0.0 copy-start.13
  13.6 0.0 copy-start.11
  13.6 0.0 copy-start.14
  13.7 0.0 copy-start.15
  13.7 0.0 copy-start.16
  13.7 0.6 dynamic_slice.15
  15.6 1.3 copy.49
  16.9 0.8 copy.48
  18.4 0.6 dynamic_slice.16
  19.0 0.6 fusion.1
  19.9 0.0 copy-start.9
  19.9 25.6 %all-to-all-done = bf16[16,1,20,2048]{3,2,1,0:T(8,128)(2,1)S(1)} async-done(((bf16[16,1,20,2048]{3,2,1,0:T(8,128)(2,1)}), bf16[16,1,20,2048]{3,2,1,0:T(8,128)(2,1)S(1)}, u32[]{:S(2)}, u32[]{:S(2)}) %all-to-all-start) | async-done | bytes 1310752 | tf_op jit(solution)/shard_map/all_to_all | solution.py:1124
  45.5 1.2 reshape.75.refs_6_
  46.7 0.6 broadcast_in_dim.22.refs_8_.refs_17_
  47.3 381.5 %forward_gather.1 = (bf16[4,2,2,128,1024]{4,3,2,1,0:T(8,128)(2,1)}, bf16[4,2,2,128,1024]{4,3,2,1,0:T(8,128)(2,1)}, bf16[4,2,2,128,1024]{4,3,2,1,0:T(8,128)(2,1)}...) custom-call(bf16[128,1024]{1,0:T(8,128)(2,1)} %refs_0_.1, ...), custom_call_target="tpu_custom_call" | custom-call | tf_op jit(solution)/shard_map/forward_gather/pallas_call | solution.py:468
  428.9 343.2 %backward_scatter.1 = (f32[128,1024]{1,0:T(8,128)}, f32[128,1024]{1,0:T(8,128)}, f32[128,1024]{1,0:T(8,128)}, f32[128,1024]{1,0:T(8,128)}, f32[128,4096]{1,0:T(8...) custom-call(bf16[4,2,2,128,1024]{4,3,2,1,0:T(8,128)(2,1)} %get-tuple, ...), custom_call_target="tpu_custom_call" | custom-call | tf_op jit(solution)/shard_map/backward_scatter/pallas_call | solution.py:1086
  772.1 3.3 copy.61
  775.4 0.5 broadcast.36
  776.0 9.4 %reduce.2 = bf16[320,2048]{1,0:T(8,128)(2,1)} reduce(bf16[320,1,1,2048]{3,2,1,0:T(2,128)(2,1)S(1)} %bitcast.38, bf16[]{:T(256)} %broadcast.36), dimensions={1,2}, to_apply=%bitcast.36.reduce_sub_computation | reduce | bytes 2621442
  785.3 4.6 reshape.106
  790.0 6.1 all-to-all-start.1
  796.1 1.8 copy.55
  798.0 1.0 copy.54
  799.0 0.6 copy.57
  799.6 0.6 fusion.2
  800.2 23.4 %all-to-all-done.1 = bf16[16,2,20480]{2,1,0:T(2,128)(2,1)} async-done(((bf16[16,2,20480]{2,1,0:T(2,128)(2,1)}), bf16[16,2,20480]{2,1,0:T(2,128)(2,1)}, u32[]{:S(2)}, u32[]{:S(2)}) %all-to-all-start.1) | async-done | bytes 1310752 | tf_op jit(solution)/shard_map/all_to_all | solution.py:1158
  823.6 4.5 reshape.107
  828.1 8.7 %bitcast_reduce_fusion = bf16[320,2048]{1,0:T(8,128)(2,1)} fusion(bf16[320,1,1,2048]{3,2,1,0:T(2,128)(2,1)S(1)} %reshape.107), kind=kLoop, calls=%fused_computation.21 | loop fusion | bytes 2621440 | tf_op jit(solution)/shard_map/all_to_all | solution.py:1158
  836.8 2.2 reshape.98
  839.0 0.2 broadcast.29
  839.2 1.1 scatter_fusion
  840.3 1.8 copy.53
  842.1 1.1 copy.76
  843.2 0.3 copy-done.6
  843.4 0.8 copy.77
  844.2 0.8 copy.78
  845.0 0.8 copy.79
  845.8 1.3 copy.80
  (44 shorter events, 0.1 us)
Async XLA Ops:
  6.1 7.6 copy-start.20
  6.1 9.5 %copy-start.3 = (bf16[4096,128]{1,0:T(8,128)(2,1)S(1)}, bf16[4096,128]{1,0:T(8,128)(2,1)}, u32[]{:S(2)}) copy-start(bf16[4096,128]{1,0:T(8,128)(2,1)} %param.33) | copy-start | bytes 3145732
  6.1 39.5 %all-to-all-start = ((bf16[16,1,20,2048]{3,2,1,0:T(8,128)(2,1)}), bf16[16,1,20,2048]{3,2,1,0:T(8,128)(2,1)S(1)}, u32[]{:S(2)}, u32[]{:S(2)}) async-start(bf16[16,1,20,2048]{3,2,1,0:T(8,128)(2,1)} %fusion), calls=%async_computation | async-start | bytes 3145728 | tf_op jit(solution)/shard_map/all_to_all | solution.py:1124
  13.6 3.4 copy-start.8
  13.6 4.9 copy-start.21
  13.6 6.1 copy-start.18
  13.6 6.1 copy-start.19
  13.6 6.1 copy-start.13
  13.6 6.1 copy-start.11
  13.6 6.1 copy-start.14
  13.6 6.2 copy-start.12
  13.7 6.2 copy-start.15
  13.7 6.2 copy-start.16
  13.7 6.2 copy-start.17
  19.9 27.4 %copy-start.9 = (f32[18432]{0:T(1024)}, f32[18432]{0:T(1024)S(1)}, u32[]{:S(2)}) copy-start(f32[18432]{0:T(1024)S(1)} %constant_dynamic-update-slice_fusion) | copy-start | bytes 221188
  790.0 6.1 copy-start.1
  790.0 33.6 %all-to-all-start.1 = ((bf16[16,2,20480]{2,1,0:T(2,128)(2,1)}), bf16[16,2,20480]{2,1,0:T(2,128)(2,1)}, u32[]{:S(2)}, u32[]{:S(2)}) async-start(bf16[16,2,20480]{2,1,0:T(2,128)(2,1)} %reshape.106), calls=%async_computation.1 | async-start | bytes 2621440 | tf_op jit(solution)/shard_map/all_to_all | solution.py:1158
  796.1 1.8 copy-start.7
  796.1 2.8 copy-start.10
  840.3 1.8 copy-start.2
  842.1 1.3 copy-start.6
  842.1 2.1 copy-start.5
  842.1 2.9 copy-start.4
  843.4 2.4 copy-start

commit v5 on v4

--- a/solution.py
+++ b/solution.py
@@ -54,6 +54,15 @@
     pl.semaphore_wait(barrier, len(peers))
 
 
+LAG, EARLY, X_FIRST, DEALT = 3, 3, (7,), 7
+
+
+def rest_shape(count):
+    whole = count // 16 * 16
+    rest = count - whole
+    padded = 4 if rest <= 4 else 8 if rest <= 8 else 16
+    return whole, rest, padded, 16 // padded
+
 def gather_tiles(widths):
     return [(i, start) for i, width in enumerate(widths) for start in range(0, width, TILE)]
 
@@ -61,8 +70,9 @@
 def forward_kernel(planes, widths, *refs):
     count = len(widths)
     shard_refs = refs[:count]
-    own_ref, cot_ref, mask_ref, vec_ref = refs[count : count + 4]
-    outs = refs[count + 4 :]
+    deal_refs = refs[count : count + 2]
+    cot_ref, mask_ref, vec_ref = refs[count + 2 : count + 5]
+    outs = refs[count + 5 :]
     full_refs = outs[:count]
     (
         x_full, cot_full, qkv_out, mixed_out, normed_out, inverse_out, hidden_out, active_out, slope_out,
@@ -70,19 +80,19 @@
     ) = outs[count : count + 13]
     (
         w_buf, x_buf, qkv_buf, mixed_buf, attn_acc, attn_land, send_buf, hidden_buf, active_buf, slope_buf,
-        down_acc, down_land, inverse_buf, result_buf, sums_buf,
+        down_acc, down_land, inverse_buf, result_buf, sums_buf, whole_land, rest_land,
         plane_send, plane_recv, x_send, x_recv, core_send, core_recv, w_sem, in_send, in_recv,
         attn_send, attn_recv, down_send, down_recv, load_sem, store_sem,
+        deal_send, deal_recv,
     ) = outs[count + 13 :]
     plane, across, core, tensor = place()
     far = [lax.rem(plane + k, planes) for k in range(planes)]
-    near = [lax.rem(plane + planes - k, planes) for k in range(planes)]
     x_peer = device_of(plane, 1 - across, core, tensor)
     core_peer = device_of(plane, across, 1 - core, tensor)
     y_peer = device_of(plane, across, core, 1 - tensor)
     plane_peers = [device_of(far[k], across, core, tensor) for k in range(planes)]
     tiles = gather_tiles(widths)
-    half, features = own_ref.shape
+    half, features = cot_ref.shape
     tokens = 2 * half
     block = features // planes
     head_cols = mixed_buf.shape[1]
@@ -103,9 +113,15 @@
         return vec_ref[:, pl.ds(vec_at[key] + start, size)]
 
     first_down = len(tiles) - widths[5] // TILE
-    units = [(c, k) for c in range(first_down) for k in range(planes)]
-    units += [(c, k) for k in range(planes) for c in range(first_down, len(tiles))]
-    ahead, lag = 6, 2
+    units = [(c, j) for c in range(first_down) for j in range(planes)]
+    units += [(c, j) for j in range(planes) for c in range(first_down, len(tiles))]
+    lag, early = LAG, EARLY
+    relayed = planes == 4
+    across_first = X_FIRST if relayed else ()
+    low_side = plane < planes // 2
+    origins = [
+        jnp.where(low_side, lax.rem(plane + j, planes), lax.rem(plane + planes - j, planes)) for j in range(planes)
+    ]
 
     def view(c, *where):
         i, start = tiles[c]
@@ -115,47 +131,96 @@
         i, start = tiles[c]
         return shard_refs[i].at[:, pl.ds(start, TILE)]
 
-    def unit_z(u, source):
-        c, k = units[u]
-        if k == 0:
-            return pltpu.make_async_copy(own(c), view(c, plane, across, core), plane_recv.at[c, 0])
+    def own_load(c):
+        return pltpu.make_async_copy(own(c), w_buf.at[1, c // 4, (c // 2) % 2, c % 2], plane_recv.at[c, 0])
+
+    def own_store(c):
+        return pltpu.make_async_copy(
+            w_buf.at[1, c // 4, (c // 2) % 2, c % 2], view(c, plane, across, core), plane_recv.at[c, 0]
+        )
+
+    def both(c):
+        return slice(None) if c in across_first else across
+
+    def z_copy(c, origin, target, send):
+        part = view(c, origin, both(c), core)
+        if c not in across_first and send > 0:
+            part = own(c)
+        place_there = jnp.where(
+            target < planes // 2, lax.rem(origin + planes - target, planes), lax.rem(target + planes - origin, planes)
+        )
         return pltpu.make_async_remote_copy(
-            own(c), view(c, source, across, core), plane_send.at[c, k], plane_recv.at[c, k],
-            device_id=plane_peers[k], device_id_type=MESH,
-        )
-
-    def unit_x(u, side):
-        c, k = units[u]
-        part = view(c, near[k], side, core)
+            part, view(c, origin, both(c), core), plane_send.at[c, send], plane_recv.at[c, place_there],
+            device_id=device_of(target, across, core, tensor), device_id_type=MESH,
+        )
+
+    def z_each(c, offsets, act):
+        for k in offsets:
+            copy = z_copy(c, plane, far[k], k)
+            if relayed and k != 2:
+                @pl.when((plane < planes - 1) if k == 1 else (plane > 0))
+                def _():
+                    act(copy)
+            else:
+                act(copy)
+
+    def z_relay(c, act):
+        if relayed:
+            @pl.when(jnp.logical_and(plane > 0, plane < planes - 1))
+            def _():
+                act(z_copy(c, origins[2], jnp.where(plane == 1, 0, planes - 1), 0))
+
+    def z_arrival(c, j):
+        part = view(c, origins[j], both(c), core)
         return pltpu.make_async_remote_copy(
-            part, part, x_send.at[c, k], x_recv.at[c, k], device_id=x_peer, device_id_type=MESH
+            part, part, plane_send.at[c, j], plane_recv.at[c, j], device_id=x_peer, device_id_type=MESH
+        )
+
+    def x_copy(c, j, side):
+        part = view(c, origins[j], side, core)
+        return pltpu.make_async_remote_copy(
+            own(c) if j == 0 else part, part, x_send.at[c, j], x_recv.at[c, j], device_id=x_peer,
+            device_id_type=MESH,
         )
 
     def unit_core(u, side):
-        c, k = units[u]
-        part = view(c, near[k], slice(None), side)
+        c, j = units[u]
+        part = view(c, origins[j], slice(None), side)
         return pltpu.make_async_remote_copy(
-            part, part, core_send.at[c, k], core_recv.at[c, k], device_id=core_peer, device_id_type=MESH
-        )
-
-    def z_start(u):
-        unit_z(u, plane).start()
-
-    def z_wait(u):
-        c, k = units[u]
-        if k == 0:
-            unit_z(u, plane).wait()
-        else:
-            unit_z(u, near[k]).wait_recv()
+            part, part, core_send.at[c, j], core_recv.at[c, j], device_id=core_peer, device_id_type=MESH
+        )
+
+    z_items = [(planes * max(c - early, 0), c, range(1, planes)) for c in range(first_down)]
+    near_by = [k for k in range(1, planes) if k in (1, planes - 1)]
+    at = planes * (first_down - early)
+    for offsets in (near_by, [k for k in range(1, planes) if k not in near_by]):
+        for c in range(first_down, len(tiles)):
+            z_items.append((at, c, offsets))
+            at += 2
+    z_items.sort(key=lambda item: item[0])
+
+    def z_begin(n):
+        for when, c, offsets in z_items:
+            if when == n:
+                if c in across_first:
+                    x_copy(c, 0, 1 - across).wait_recv()
+                z_each(c, offsets, lambda copy: copy.start())
 
     def pump(n):
         if n < len(units):
-            z_wait(n)
-            unit_x(n, across).start()
-            if n + ahead < len(units):
-                z_start(n + ahead)
+            if n > 0:
+                z_begin(n)
+            c, j = units[n]
+            if j > 0:
+                z_arrival(c, j).wait_recv()
+            if j == 2:
+                z_relay(c, lambda copy: copy.start())
+            if c not in across_first:
+                x_copy(c, j, across).start()
         if n >= lag:
-            unit_x(n - lag, 1 - across).wait_recv()
+            c, j = units[n - lag]
+            if c not in across_first:
+                x_copy(c, j, 1 - across).wait_recv()
             unit_core(n - lag, core).start()
 
     def landed(u):
@@ -184,7 +249,7 @@
     def down_copy(k, j):
         c = first_down + j
         return pltpu.make_async_copy(
-            view(c, near[k], slice(None), slice(None)), w_buf.at[k % 2, j], w_sem.at[k % 2, j]
+            view(c, origins[k], slice(None), slice(None)), w_buf.at[k % 2, j], w_sem.at[k % 2, j]
         )
 
     down_parts = widths[5] // TILE
@@ -197,12 +262,55 @@
     def flat(value):
         return value.reshape(-1, value.shape[-1])
 
+    groups = planes * 4
+    index = (plane * 2 + across) * 2 + core
+    group = half // groups
+    whole, rest, padded, chunks = rest_shape(group)
+    rest_width = features // chunks
+    deal_parts = ((0, whole_land), (1, rest_land)) if whole else ((1, rest_land),)
+
+    def deal(which, land, k):
+        target = lax.rem(index + k, groups)
+        return pltpu.make_async_remote_copy(
+            deal_refs[which].at[target], land.at[index], deal_send.at[which, k], deal_recv.at[which, k],
+            device_id=(target, tensor), device_id_type=MESH,
+        )
+
+    def deal_own(which, land):
+        return pltpu.make_async_copy(deal_refs[which].at[index], land.at[index], deal_recv.at[which, 0])
+
+    def dealt():
+        for which, land in deal_parts:
+            deal_own(which, land).wait()
+            for k in range(1, groups):
+                deal(which, land, k).wait_recv()
+        for s in range(groups):
+            start = s * group
+            if whole:
+                attn_acc[start : start + whole, :] = whole_land[s].astype(jnp.float32)
+            tail = rest_land[s].astype(jnp.float32)
+            for q in range(chunks):
+                attn_acc[start + whole : start + group, q * rest_width : (q + 1) * rest_width] = tail[
+                    q * padded : q * padded + rest, :
+                ]
+
+        @pl.loop(0, half // 16)
+        def _(i):
+            rows = pl.ds(pl.multiple_of(tensor * half + i * 16, 16), 16)
+            x_buf[rows, :] = attn_acc[pl.ds(pl.multiple_of(i * 16, 16), 16), :].astype(jnp.bfloat16)
+
+        exchange(0, x_buf.at[own_rows], x_buf).start()
+
     def load_x():
-        exchange(0, own_ref, x_full).wait_recv()
-        keep(0, own_ref, x_full).wait()
-        copy = pltpu.make_async_copy(x_full, x_buf, load_sem.at[2])
-        copy.start()
-        copy.wait()
+        exchange(0, x_buf.at[own_rows], x_buf).wait_recv()
+        store(11, x_buf, x_full).start()
+
+    def cot_load():
+        other_rows = pl.ds(pl.multiple_of((1 - tensor) * half, half), half)
+        return [
+            pltpu.make_async_copy(cot_ref, x_buf.at[own_rows], load_sem.at[1]),
+            pltpu.make_async_copy(cot_full.at[other_rows], x_buf.at[other_rows], load_sem.at[2]),
+        ]
 
     def exchange(which, source, target):
         return pltpu.make_async_remote_copy(
@@ -210,8 +318,8 @@
             device_id=y_peer, device_id_type=MESH,
         )
 
-    def keep(which, source, target):
-        return pltpu.make_async_copy(source, target.at[own_rows], load_sem.at[which])
+    def start_cot():
+        exchange(1, cot_ref, cot_full).start()
 
     def project(c, bias):
         wait_tile(c)
@@ -283,8 +391,10 @@
         store(1, inverse_buf, inverse_out).start()
         store(2, hidden_buf, hidden_out).start()
         exchange(1, cot_ref, cot_full).wait_recv()
-        keep(1, cot_ref, cot_full).wait()
-        pltpu.make_async_copy(cot_full, x_buf, load_sem.at[2]).start()
+        store(11, x_buf, x_full).wait()
+        exchange(0, x_buf.at[own_rows], x_buf).wait_send()
+        for copy in cot_load():
+            copy.start()
 
     def store(which, source, target):
         return pltpu.make_async_copy(source, target, store_sem.at[which])
@@ -320,14 +430,14 @@
         slope_store(j).start()
 
     def down_share(k):
-        cols = block_cols(near[k])
+        cols = block_cols(origins[k])
         return pltpu.make_async_remote_copy(
             send_buf.at[:, cols], down_land.at[:, cols], down_send.at[k], down_recv.at[k],
             device_id=y_peer, device_id_type=MESH,
         )
 
     def lower(k):
-        cols = block_cols(near[k])
+        cols = block_cols(origins[k])
         value = None
         for j in range(down_parts):
             down_copy(k, j).wait()
@@ -340,7 +450,8 @@
     def second_norm():
         for k in range(planes):
             down_share(k).wait()
-        pltpu.make_async_copy(cot_full, x_buf, load_sem.at[2]).wait()
+        for copy in cot_load():
+            copy.wait()
         store(2, hidden_buf, hidden_out).wait()
         sums_buf[...] = jnp.zeros_like(sums_buf)
         gain = vector("gain_second", 0, features)
@@ -383,12 +494,22 @@
         ):
             store(which, source, target).start()
 
-    enter(plane_peers[1:] + [x_peer, core_peer, y_peer])
-    for u in range(ahead):
-        z_start(u)
-    for which, source, target in ((0, own_ref, x_full), (1, cot_ref, cot_full)):
-        exchange(which, source, target).start()
-        keep(which, source, target).start()
+    for c in range(len(tiles)):
+        own_load(c).start()
+    for which, land in deal_parts:
+        deal_own(which, land).start()
+    enter([(lax.rem(index + k, groups), tensor) for k in range(1, groups)] + [y_peer])
+    for k in range(1, groups):
+        for which, land in deal_parts:
+            deal(which, land, k).start()
+    for c in across_first:
+        x_copy(c, 0, across).start()
+    z_begin(0)
+    for c in range(len(tiles)):
+        own_load(c).wait()
+        own_store(c).start()
+    for c in range(len(tiles)):
+        own_store(c).wait()
 
     plan = {}
 
@@ -396,13 +517,18 @@
         plan.setdefault(n, []).append((step, args))
 
     def ready(c):
-        return planes * (c + 1) + 2
+        return planes * (c + 1) + lag
 
     heads = head_cols // HEAD_DIM
-    at_slot(ready(0), load_x)
-    for c in range(3):
-        at_slot(ready(c), load_tile, c)
-        at_slot(ready(c) + 1, project, c, ("b_query", None, "b_value")[c])
+    at_slot(DEALT, dealt)
+    at_slot(ready(0), load_tile, 0)
+    at_slot(ready(1), load_tile, 1)
+    at_slot(ready(2) - 2, load_x)
+    at_slot(ready(2) - 2, project, 0, "b_query")
+    at_slot(ready(2) - 2, start_cot)
+    at_slot(ready(2) - 1, project, 1, None)
+    at_slot(ready(2), load_tile, 2)
+    at_slot(ready(2) + 1, project, 2, "b_value")
     begin = ready(2) + 2
     for q in range(4):
         at_slot(begin + q, attend, q * heads // 4, (q + 1) * heads // 4)
@@ -418,7 +544,7 @@
         if j >= 2:
             plan.setdefault(max(norm_slot + 1 + j - 2, ready(4 + j)), []).append((load_tile, (4 + j,)))
     for k in range(planes):
-        slot = planes * first_down + down_parts * (k + 1) + 2
+        slot = planes * first_down + down_parts * (k + 1) + lag
         at_slot(slot, load_down, k)
         at_slot(slot + 1, lower, k)
     last = max(max(plan), len(units) + lag - 1)
@@ -440,22 +566,32 @@
         store(which, source, target).wait()
     for j in range(2, 4):
         slope_store(j).wait()
-    for which, source, target in ((0, own_ref, x_full), (1, cot_ref, cot_full)):
-        exchange(which, source, target).wait_send()
-    for u, (c, k) in enumerate(units):
-        if k > 0:
-            unit_z(u, plane).wait_send()
-        unit_x(u, across).wait_send()
+    exchange(1, cot_ref, cot_full).wait_send()
+    for which, land in deal_parts:
+        for k in range(1, groups):
+            deal(which, land, k).wait_send()
+    for c in range(len(tiles)):
+        z_each(c, range(1, planes), lambda copy: copy.wait_send())
+        z_relay(c, lambda copy: copy.wait_send())
+    for u, (c, j) in enumerate(units):
+        if c not in across_first or j == 0:
+            x_copy(c, j, across).wait_send()
         unit_core(u, core).wait_send()
 
 
-def forward(shard_list, own, cot, mask, vectors):
+def forward(shard_list, dealt_rows, cot, mask, vectors):
     planes = lax.axis_size("dp") // 4
     widths = [shard.shape[1] for shard in shard_list]
     total = sum(width // TILE for width in widths)
-    half, features = own.shape
+    half, features = cot.shape
     tokens, rows = 2 * half, shard_list[0].shape[0]
     head_cols, up_cols = widths[0], widths[4]
+    groups = planes * 4
+    whole, rest, padded, chunks = rest_shape(half // groups)
+    whole_rows = dealt_rows[:, : max(whole, 16)] if whole else jnp.zeros((groups, 16, 128), jnp.bfloat16)
+    rest_rows = jnp.pad(dealt_rows[:, whole:], ((0, 0), (0, padded - rest), (0, 0)))
+    rest_rows = rest_rows.reshape(groups, padded, chunks, features // chunks)
+    rest_rows = rest_rows.transpose(0, 2, 1, 3).reshape(groups, 16, features // chunks)
     sem, low, high = pltpu.SemaphoreType.DMA, jnp.bfloat16, jnp.float32
     hbm, vmem = pl.BlockSpec(memory_space=pl.ANY), pl.BlockSpec(memory_space=pltpu.VMEM)
     shapes = [((planes, 2, 2, *shard.shape), low) for shard in shard_list] + [
@@ -468,7 +604,7 @@
     results = pl.pallas_call(
         partial(forward_kernel, planes, widths),
         out_shape=[jax.ShapeDtypeStruct(*shape) for shape in shapes],
-        in_specs=[hbm] * (len(shard_list) + 2) + [vmem] * 2,
+        in_specs=[hbm] * (len(shard_list) + 3) + [vmem] * 2,
         out_specs=[hbm] * len(shapes),
         scratch_shapes=[
             pltpu.VMEM((2, planes, 2, 2, rows, TILE), low),
@@ -486,15 +622,18 @@
             pltpu.VMEM((tokens, 128), high),
             pltpu.VMEM((half, features), low),
             pltpu.VMEM((3, 16, features), high),
+            pltpu.VMEM(whole_rows.shape, low),
+            pltpu.VMEM(rest_rows.shape, low),
             *[sem((total, planes))] * 6,
             sem((2, max(planes, 4))), sem((2,)), sem((2,)),
-            sem((planes,)), sem((planes,)), sem((planes,)), sem((planes,)), sem((3,)), sem((11,)),
+            sem((planes,)), sem((planes,)), sem((planes,)), sem((planes,)), sem((3,)), sem((12,)),
+            sem((2, groups)), sem((2, groups)),
         ],
         compiler_params=pltpu.CompilerParams(
             collective_id=0, has_side_effects=True, vmem_limit_bytes=62 * 2**20
         ),
         name="forward_gather",
-    )(*shard_list, own, cot, mask, vectors)
+    )(*shard_list, whole_rows, rest_rows, cot, mask, vectors)
     return results[: len(shard_list)], results[len(shard_list) :]
 
 
@@ -508,17 +647,17 @@
         sums_in, mask_ref, gain_ref,
     ) = refs[:19]
     (
-        grad_query, grad_key, grad_value, grad_out_w, grad_up, grad_down, small_out, own_out,
+        grad_query, grad_key, grad_value, grad_out_w, grad_up, grad_down, small_out, whole_out, rest_out,
         left_own, left_far, active_far, rise_own, rise_far, mixed_far, qkv_own, qkv_far,
-    ) = refs[19:35]
+    ) = refs[19:36]
     (
         left_buf, right_buf, stage, x_land, plane_land, out_buf, tile_buf, wide_buf, low_buf, rise_buf,
         slope_buf, acc_buf, hidden_land, send_buf, qkv_buf, turn_buf, input_land, row_buf, inverse_buf,
-        sums_buf, small_land,
+        sums_buf, small_land, whole_buf, rest_buf, rest_wide,
         left_sem, right_sem, out_sem, core_send, core_recv, left_send, left_recv, x_send, x_recv,
         plane_send, plane_recv, small_send, small_recv, tile_sem, wide_sem, slope_sem, load_sem, store_sem,
-        turn_sem, hidden_send, hidden_recv, input_send, input_recv, row_sem,
-    ) = refs[35:]
+        turn_sem, hidden_send, hidden_recv, input_send, input_recv, row_sem, back_send, back_recv,
+    ) = refs[36:]
     plane, across, core, tensor = place()
     far = [lax.rem(plane + k, planes) for k in range(planes)]
     x_peer = device_of(plane, 1 - across, core, tensor)
@@ -966,18 +1105,52 @@
         def _(i):
             rows = pl.ds(pl.multiple_of(tensor * half + i * 16, 16), 16)
             land = pl.ds(pl.multiple_of(i * 16, 16), 16)
-            send_buf[pl.ds(pl.multiple_of(half + i * 16, 16), 16), :] = (
-                acc_buf[rows, :] + input_land[land, :].astype(jnp.float32)
-            ).astype(jnp.bfloat16)
-
-        local(send_buf.at[pl.ds(half, half)], own_out, load_sem.at[3]).start()
+            acc_buf[land, :] = acc_buf[rows, :] + input_land[land, :].astype(jnp.float32)
+
+    groups = planes * 4
+    index = (plane * 2 + across) * 2 + core
+    group = half // groups
+    whole, rest, padded, chunks = rest_shape(group)
+    rest_width = features // chunks
+    back_parts = ((0, whole_buf, whole_out), (1, rest_buf, rest_out))[0 if whole else 1 :]
+
+    def back(which, source, target, k):
+        peer = lax.rem(index + k, groups)
+        return remote(
+            source.at[peer], target.at[index], back_send.at[which, k], back_recv.at[which, k], (peer, tensor)
+        )
+
+    def back_own(which, source, target):
+        return local(source.at[index], target.at[index], back_recv.at[which, 0])
+
+    def send_back():
+        rest_wide[...] = jnp.zeros_like(rest_wide)
+        for s in range(groups):
+            start = s * group
+            if whole:
+                whole_buf[s] = acc_buf[start : start + whole, :].astype(jnp.bfloat16)
+            for q in range(chunks):
+                rest_wide[q * padded : q * padded + rest, :] = acc_buf[
+                    start + whole : start + group, q * rest_width : (q + 1) * rest_width
+                ]
+            rest_buf[s] = rest_wide[...].astype(jnp.bfloat16)
+        for part in back_parts:
+            back_own(*part).start()
+            for k in range(1, groups):
+                back(*part, k).start()
+
+    def back_wait():
+        for part in back_parts:
+            back_own(*part).wait()
+            for k in range(1, groups):
+                back(*part, k).wait()
 
     local(down_in, low_buf, load_sem.at[0]).start()
     local(hidden_in, send_buf, load_sem.at[1]).start()
     local(sums_in, sums_buf, load_sem.at[2]).start()
     rise_start(0)
     rise_start(1)
-    enter(plane_peers[1:] + [x_peer, core_peer, y_peer])
+    enter([(lax.rem(index + k, groups), tensor) for k in range(1, groups)] + [y_peer])
     for c in range(up_first):
         right_out(c).start()
     local(down_in, low_buf, load_sem.at[0]).wait()
@@ -1030,7 +1203,7 @@
         17: [(input_back, planes // 2, planes), (small_end, 0), (small_begin, 1)],
         18: [(small_end, 1), (small_begin, 2)],
         19: [(small_end, 2), (small_begin, 3)],
-        20: [(input_done,), (small_end, 3)],
+        20: [(input_done,), (send_back,), (small_end, 3)],
     }
     for n in range(total + 4):
         if n < total:
@@ -1042,7 +1215,7 @@
         if n >= 4:
             finish(n - 4)
     local(small_land.at[1], small_out, load_sem.at[0]).wait()
-    local(send_buf.at[pl.ds(half, half)], own_out, load_sem.at[3]).wait()
+    back_wait()
     left_out(3).wait_send()
     for c in range(total):
         if not up_first <= c < out_first:
@@ -1063,9 +1236,13 @@
     sem, low, high = pltpu.SemaphoreType.DMA, jnp.bfloat16, jnp.float32
     hbm, vmem = pl.BlockSpec(memory_space=pl.ANY), pl.BlockSpec(memory_space=pltpu.VMEM)
     small_rows = 16
+    groups = planes * 4
+    whole, rest, padded, chunks = rest_shape(tokens // 2 // groups)
+    whole_shape = ((groups, whole, features) if whole else (groups, 16, 128), low)
+    rest_rows = ((groups, 16, features // chunks), low)
     shapes = (
         [((rows, head_cols), high)] * 4 + [((rows, up_cols), high)] * 2
-        + [((small_rows, features), high), ((tokens // 2, features), low)]
+        + [((small_rows, features), high), whole_shape, rest_rows]
         + [((4, planes, 2, rows, tokens), low)] * 2
         + [((tokens, up_cols), low)] * 3 + [((tokens, head_cols), low)] + [((tokens, 3 * head_cols), low)] * 2
     )
@@ -1077,11 +1254,12 @@
         ((tokens, features), low), ((tokens, features), low), ((tokens, 3 * head_cols), low),
         ((planes, 2, 2, rows, tokens), low), ((tokens // 2, features), low), ((2, 2, strip, features), high),
         ((tokens, 128), high), ((3, 16, features), high), ((3 + planes, small_rows, features), high),
+        whole_shape, rest_rows, ((16, features // chunks), high),
     ]
     sems = [
         (2, 2, 2), (2, 2), (2,), (total,), (total,), (4,), (4,), (total,), (total,),
         (total, planes - 1), (total, planes - 1), (2 + planes,), (2 + planes,), (2, planes), (2, 2), (2,),
-        (4,), (5,), (1,), (planes,), (planes,), (planes,), (planes,), (2, 2),
+        (4,), (5,), (1,), (planes,), (planes,), (planes,), (planes,), (2, 2), (2, groups), (2, groups),
     ]
     results = pl.pallas_call(
         partial(backward_kernel, planes),
@@ -1094,7 +1272,12 @@
         ),
         name="backward_scatter",
     )(*weights, *saved, mask, gain)
-    return results[:6], results[6], results[7]
+    whole_rows, rest_rows = results[7], results[8]
+    rest_rows = rest_rows.reshape(groups, chunks, padded, features // chunks).transpose(0, 2, 1, 3)
+    returned = rest_rows.reshape(groups, padded, features)[:, :rest]
+    if whole:
+        returned = jnp.concatenate((whole_rows, returned), axis=1)
+    return results[:6], results[6], returned
 
 
 def shards(
@@ -1121,10 +1304,8 @@
     group_index = lax.axis_index("dp")
     tensor_index = lax.axis_index("tensor")
     ordered = jnp.take(inputs, dealing, axis=0)
-    arrived = lax.all_to_all(ordered, "dp", split_axis=0, concat_axis=2, tiled=True)
-    features = arrived.shape[3]
-    half_rows = arrived.shape[2]
-    own_rows = arrived.reshape(half_rows, features)
+    features = cotangent.shape[-1]
+    half_rows = cotangent.shape[1]
     seq_len = half_rows * lax.axis_size("tensor")
     length = lengths[dealing[group_index]]
     key_valid = jnp.arange(seq_len) < length
@@ -1139,7 +1320,7 @@
     mask = jnp.broadcast_to(key_valid.astype(jnp.float32), (8, seq_len))
     weights, saved = forward(
         [w_query, w_key, w_value, w_out.T, w_up, w_down.T],
-        own_rows, cotangent.reshape(half_rows, features), mask, vectors,
+        ordered.reshape(ordered.shape[0], -1, features), cotangent.reshape(half_rows, features), mask, vectors,
     )
     (
         full_in, _, qkv, mixed_heads, normed_full, inverse_full, full_hidden, active, slope,
@@ -1154,8 +1335,7 @@
         ],
         mask, gain_first.reshape(1, -1),
     )
-    grad_sent = grad_own.reshape(1, 1, half_rows, features)
-    returned = lax.all_to_all(grad_sent, "dp", split_axis=2, concat_axis=0, tiled=True)
+    returned = grad_own.reshape(inputs.shape)
     grad_inputs = jnp.zeros_like(returned).at[dealing].set(returned)
     weight_sums = (grads[0], grads[1], grads[2], grads[3].T, grads[4], grads[5].T)
     up_rows = b_up.shape[0] // features

time: 860 us -> 788 us (0.916)
  waiting for transfers between devices: 49 us -> 0 us
  Pallas kernels: 725 us -> 741 us
  local copies, waits for them, and re-layouts: 44.1 us -> 30.3 us
  starting transfers between devices: 13.6 us -> 0 us
  other arithmetic: 12.7 us -> 2.96 us
    all_to_all x2 -> x0, waiting for transfers between devices: 49 us -> none  [the longest x1 25.6 us: shards(): lax.all_to_all(ordered, 'dp', split_axis=0, concat_axis=2, tiled=True)]
    all_to_all x2 -> x0, starting transfers between devices: 13.6 us -> none  [the longest x1 7.49 us: shards(): lax.all_to_all(ordered, 'dp', split_axis=0, concat_axis=2, tiled=True)]
    all_to_all x2 -> x0, local copies, waits for them, and re-layouts: 10.9 us -> none  [shards(): lax.all_to_all(grad_sent, 'dp', split_axis=2, concat_axis=0, tiled=True)]
    pallas_call x1, Pallas kernels: 343 us -> 353 us  [backward(): pl.pallas_call(partial(backward_kernel, planes), out_shape=[jax.ShapeDtyp...]
    unnamed x1 -> x0, other arithmetic: 9.38 us -> none
    unnamed x68 -> x43, local copies, waits for them, and re-layouts: 24.3 us -> 21 us
  transfers between devices with their start and end apart: 2 -> 0, of which waited for: 2 -> 0; matrix products, arithmetic and copies ran while one was open for 1% -> 0% of each run, Pallas kernels for 0% -> 0%
where the time goes in v5:
time: 788 us; the launch traced here: 777 us
  Pallas kernels  741 us (94%)
  local copies, waits for them, and re-layouts  30.3 us (4%)
    pallas_call x1, Pallas kernels, forward(): pl.pallas_call(partial(forward_kernel, planes, widths), out_shape=[jax.Sh...  388 us
    pallas_call x1, Pallas kernels, backward(): pl.pallas_call(partial(backward_kernel, planes), out_shape=[jax.ShapeDtyp...  353 us
    unnamed x43, local copies, waits for them, and re-layouts  21 us

profile of v5, /device:TPU:0, one launch (start us, length us, event | category | flops | bytes accessed | tf_op | source)
XLA Modules:
  0.0 777.4 jit_solution(15186209291168028162)
XLA Ops:
  0.7 0.7 dynamic-slice_dynamic-update-slice_fusion.1
  1.4 0.7 constant_dynamic-update-slice_fusion.6
  2.0 0.7 constant_dynamic-update-slice_fusion.5
  2.7 0.7 constant_dynamic-update-slice_fusion.4
  3.4 0.7 constant_dynamic-update-slice_fusion.3
  4.1 0.7 dynamic-slice_dynamic-update-slice_fusion
  4.9 0.7 constant_dynamic-update-slice_fusion.2
  5.6 0.7 constant_dynamic-update-slice_fusion.1
  6.2 0.7 constant_dynamic-update-slice_fusion
  6.9 1.2 dynamic_slice.15
  10.1 1.2 dynamic_slice.16
  11.4 0.6 fusion
  12.0 0.6 broadcast_in_dim.22.refs_9_.refs_17_
  12.6 0.7 compare_select_fusion
  13.3 2.0 copy.50
  15.4 0.0 copy-start.10
  15.4 0.6 gather_fusion
  16.0 0.0 copy-done.8
  16.0 0.0 copy-done.10
  16.1 0.2 broadcast_select_fusion
  16.3 0.0 copy-start.2
  16.3 1.0 slice.46.refs_6_
  17.3 0.1 slice.47
  17.4 0.8 reshape.74.refs_7_
  18.2 0.0 copy-done.2
  18.2 1.3 copy.42
  19.5 0.0 copy-done.7
  19.5 0.8 copy.41
  20.4 387.8 %forward_gather.1 = (bf16[4,2,2,128,1024]{4,3,2,1,0:T(8,128)(2,1)}, bf16[4,2,2,128,1024]{4,3,2,1,0:T(8,128)(2,1)}, bf16[4,2,2,128,1024]{4,3,2,1,0:T(8,128)(2,1)}...) custom-call(bf16[128,1024]{1,0:T(8,128)(2,1)} %refs_0_.1, ...), custom_call_target="tpu_custom_call" | custom-call | tf_op jit(solution)/shard_map/forward_gather/pallas_call | solution.py:604
  408.2 353.5 %backward_scatter.1 = (f32[128,1024]{1,0:T(8,128)}, f32[128,1024]{1,0:T(8,128)}, f32[128,1024]{1,0:T(8,128)}, f32[128,1024]{1,0:T(8,128)}, f32[128,4096]{1,0:T(8...) custom-call(bf16[4,2,2,128,1024]{4,3,2,1,0:T(8,128)(2,1)} %get-tuple, ...), custom_call_target="tpu_custom_call" | custom-call | tf_op jit(solution)/shard_map/backward_scatter/pallas_call | solution.py:1264
  761.6 1.0 reshape.79
  762.7 1.4 pad_maximum_fusion
  764.1 0.2 broadcast.19
  764.3 1.1 scatter_fusion
  765.4 1.8 copy.45
  767.2 3.0 copy.47
  770.2 0.0 copy-done.6
  770.2 1.0 copy.46
  771.2 0.0 copy-done.9
  771.2 0.6 fusion.1
  771.9 0.6 copy.48
  772.5 0.0 copy-done.1
  772.5 1.1 copy.65
  773.5 0.8 copy.66
  774.3 0.8 copy.67
  775.1 0.8 copy.68
  775.9 0.0 copy-done
  775.9 1.3 copy.69
  (15 shorter events, 0.0 us)
Async XLA Ops:
  6.9 9.1 %copy-start.8 = (f32[18432]{0:T(1024)}, f32[18432]{0:T(1024)S(1)}, u32[]{:S(2)}) copy-start(f32[18432]{0:T(1024)S(1)} %constant_dynamic-update-slice_fusion) | copy-start | bytes 221188
  15.4 0.7 copy-start.10
  16.3 1.9 copy-start.2
  17.3 2.2 copy-start.7
  767.2 3.0 copy-start.6
  767.2 4.0 copy-start.9
  767.2 5.3 copy-start.1
  770.2 3.3 copy-start.5
  771.2 3.1 copy-start.4
  772.5 2.7 copy-start.3
  773.5 2.4 copy-start

commit v6 on v5

--- a/solution.py
+++ b/solution.py
@@ -54,7 +54,7 @@
     pl.semaphore_wait(barrier, len(peers))
 
 
-LAG, EARLY, X_FIRST, DEALT = 3, 3, (7,), 7
+LAG, LEAD, X_FIRST, DEALT, X_LEAD, NORM = 4, (3, 2, 1), (3, 7), 7, 6, 14
 
 
 def rest_shape(count):
@@ -115,7 +115,7 @@
     first_down = len(tiles) - widths[5] // TILE
     units = [(c, j) for c in range(first_down) for j in range(planes)]
     units += [(c, j) for j in range(planes) for c in range(first_down, len(tiles))]
-    lag, early = LAG, EARLY
+    lag = LAG
     relayed = planes == 4
     across_first = X_FIRST if relayed else ()
     low_side = plane < planes // 2
@@ -144,7 +144,7 @@
 
     def z_copy(c, origin, target, send):
         part = view(c, origin, both(c), core)
-        if c not in across_first and send > 0:
+        if c not in across_first and send <= 3:
             part = own(c)
         place_there = jnp.where(
             target < planes // 2, lax.rem(origin + planes - target, planes), lax.rem(target + planes - origin, planes)
@@ -154,21 +154,20 @@
             device_id=device_of(target, across, core, tensor), device_id_type=MESH,
         )
 
-    def z_each(c, offsets, act):
-        for k in offsets:
-            copy = z_copy(c, plane, far[k], k)
-            if relayed and k != 2:
+    middle = jnp.logical_and(plane > 0, plane < planes - 1)
+
+    def z_each(c, act):
+        for k in range(1, planes):
+            if not relayed:
+                act(z_copy(c, plane, far[k], k))
+            elif k != 2:
                 @pl.when((plane < planes - 1) if k == 1 else (plane > 0))
                 def _():
-                    act(copy)
-            else:
-                act(copy)
-
-    def z_relay(c, act):
-        if relayed:
-            @pl.when(jnp.logical_and(plane > 0, plane < planes - 1))
-            def _():
-                act(z_copy(c, origins[2], jnp.where(plane == 1, 0, planes - 1), 0))
+                    act(z_copy(c, plane, far[k], k))
+
+    def z_pass(c, j):
+        near_end, far_side = jnp.where(plane == 1, 0, planes - 1), jnp.where(plane == 1, 2, 1)
+        return z_copy(c, origins[j], far_side if j == 3 else near_end, 3 + j)
 
     def z_arrival(c, j):
         part = view(c, origins[j], both(c), core)
@@ -190,33 +189,44 @@
             part, part, core_send.at[c, j], core_recv.at[c, j], device_id=core_peer, device_id_type=MESH
         )
 
-    z_items = [(planes * max(c - early, 0), c, range(1, planes)) for c in range(first_down)]
-    near_by = [k for k in range(1, planes) if k in (1, planes - 1)]
-    at = planes * (first_down - early)
-    for offsets in (near_by, [k for k in range(1, planes) if k not in near_by]):
-        for c in range(first_down, len(tiles)):
-            z_items.append((at, c, offsets))
-            at += 2
-    z_items.sort(key=lambda item: item[0])
+    lead_own, lead_first, lead_second = LEAD
+    z_at, first_at, second_at = {}, {}, {}
+    for c in range(len(tiles)):
+        for lead, table, ramp in ((lead_own, z_at, c - 1), (lead_first, first_at, c + 1), (lead_second, second_at, c + 2)):
+            table.setdefault(max(planes * (c - lead), ramp), []).append(c)
 
     def z_begin(n):
-        for when, c, offsets in z_items:
-            if when == n:
-                if c in across_first:
-                    x_copy(c, 0, 1 - across).wait_recv()
-                z_each(c, offsets, lambda copy: copy.start())
+        for c in z_at.get(n, []):
+            if c in across_first:
+                x_copy(c, 0, 1 - across).wait_recv()
+            z_each(c, lambda copy: copy.start())
+
+    def z_forward(n):
+        steps = [(c, (1, 3)) for c in first_at.get(n, [])] + [(c, (2,)) for c in second_at.get(n, [])]
+        if relayed and steps:
+            @pl.when(middle)
+            def _():
+                for c, positions in steps:
+                    for j in positions:
+                        z_arrival(c, j).wait_recv()
+                        z_pass(c, j).start()
 
     def pump(n):
         if n < len(units):
             if n > 0:
                 z_begin(n)
             c, j = units[n]
+            z_forward(n)
             if j > 0:
-                z_arrival(c, j).wait_recv()
-            if j == 2:
-                z_relay(c, lambda copy: copy.start())
+                if relayed:
+                    pl.when(jnp.logical_not(middle))(z_arrival(c, j).wait_recv)
+                else:
+                    z_arrival(c, j).wait_recv()
             if c not in across_first:
-                x_copy(c, j, across).start()
+                if j > 0:
+                    x_copy(c, j, across).start()
+            if j == 0 and c + X_LEAD < len(tiles) and c + X_LEAD not in across_first:
+                x_copy(c + X_LEAD, 0, across).start()
         if n >= lag:
             c, j = units[n - lag]
             if c not in across_first:
@@ -318,8 +328,10 @@
             device_id=y_peer, device_id_type=MESH,
         )
 
-    def start_cot():
-        exchange(1, cot_ref, cot_full).start()
+    def load_cot():
+        exchange(1, cot_ref, cot_full).wait_recv()
+        for copy in cot_load():
+            copy.start()
 
     def project(c, bias):
         wait_tile(c)
@@ -372,7 +384,7 @@
         def _(p):
             attn_share(p).wait()
 
-        @pl.loop(0, tokens // 16)
+        @pl.loop(0, tokens // 16, unroll=2)
         def _(i):
             rows = pl.ds(pl.multiple_of(i * 16, 16), 16)
             value = (
@@ -390,11 +402,9 @@
         store(0, attn_acc, normed_out).start()
         store(1, inverse_buf, inverse_out).start()
         store(2, hidden_buf, hidden_out).start()
-        exchange(1, cot_ref, cot_full).wait_recv()
         store(11, x_buf, x_full).wait()
         exchange(0, x_buf.at[own_rows], x_buf).wait_send()
-        for copy in cot_load():
-            copy.start()
+        exchange(1, cot_ref, cot_full).start()
 
     def store(which, source, target):
         return pltpu.make_async_copy(source, target, store_sem.at[which])
@@ -461,7 +471,7 @@
             return pl.ds(pl.multiple_of(base * half + i * 16, 16), 16)
 
         for which in (0, 1):
-            @pl.loop(0, half // 16)
+            @pl.loop(0, half // 16, unroll=2)
             def _(i):
                 rows = rows_of(which, i)
                 hidden = attn_acc[rows, :] * vector("gain_first", 0, features) + vector(
@@ -499,11 +509,12 @@
     for which, land in deal_parts:
         deal_own(which, land).start()
     enter([(lax.rem(index + k, groups), tensor) for k in range(1, groups)] + [y_peer])
+    z_begin(-1)
+    for c in sorted({*range(X_LEAD), *across_first}):
+        x_copy(c, 0, across).start()
     for k in range(1, groups):
         for which, land in deal_parts:
             deal(which, land, k).start()
-    for c in across_first:
-        x_copy(c, 0, across).start()
     z_begin(0)
     for c in range(len(tiles)):
         own_load(c).wait()
@@ -525,7 +536,6 @@
     at_slot(ready(1), load_tile, 1)
     at_slot(ready(2) - 2, load_x)
     at_slot(ready(2) - 2, project, 0, "b_query")
-    at_slot(ready(2) - 2, start_cot)
     at_slot(ready(2) - 1, project, 1, None)
     at_slot(ready(2), load_tile, 2)
     at_slot(ready(2) + 1, project, 2, "b_value")
@@ -534,7 +544,7 @@
         at_slot(begin + q, attend, q * heads // 4, (q + 1) * heads // 4)
     at_slot(begin + 3, load_tile, 3)
     at_slot(begin + 4, project_out)
-    norm_slot = begin + 4 + 10 * planes // 4
+    norm_slot = begin + 4 + NORM * planes // 4
     at_slot(norm_slot, first_norm)
     at_slot(max(ready(4), begin), load_tile, 4)
     at_slot(max(ready(5), begin + 4), load_tile, 5)
@@ -543,10 +553,13 @@
         at_slot(slot, raise_up, j)
         if j >= 2:
             plan.setdefault(max(norm_slot + 1 + j - 2, ready(4 + j)), []).append((load_tile, (4 + j,)))
+    raised = max(norm_slot + 4, ready(7) + 1)
     for k in range(planes):
         slot = planes * first_down + down_parts * (k + 1) + lag
         at_slot(slot, load_down, k)
-        at_slot(slot + 1, lower, k)
+        at_slot(max(slot + 1, raised), lower, k)
+        if k == planes // 2:
+            at_slot(slot, load_cot)
     last = max(max(plan), len(units) + lag - 1)
     for n in range(last + 1):
         if n < len(units) + lag:
@@ -571,8 +584,12 @@
         for k in range(1, groups):
             deal(which, land, k).wait_send()
     for c in range(len(tiles)):
-        z_each(c, range(1, planes), lambda copy: copy.wait_send())
-        z_relay(c, lambda copy: copy.wait_send())
+        z_each(c, lambda copy: copy.wait_send())
+        if relayed:
+            @pl.when(middle)
+            def _():
+                for j in range(1, planes):
+                    z_pass(c, j).wait_send()
     for u, (c, j) in enumerate(units):
         if c not in across_first or j == 0:
             x_copy(c, j, across).wait_send()
@@ -624,7 +641,7 @@
             pltpu.VMEM((3, 16, features), high),
             pltpu.VMEM(whole_rows.shape, low),
             pltpu.VMEM(rest_rows.shape, low),
-            *[sem((total, planes))] * 6,
+            sem((total, max(planes, 7))), *[sem((total, planes))] * 5,
             sem((2, max(planes, 4))), sem((2,)), sem((2,)),
             sem((planes,)), sem((planes,)), sem((planes,)), sem((planes,)), sem((3,)), sem((12,)),
             sem((2, groups)), sem((2, groups)),
@@ -755,11 +772,36 @@
             stage.at[c % 3, 1 - across], x_land.at[c % slots], x_send.at[c], x_recv.at[c], x_peer
         )
 
+    relayed = planes == 4
+    middle = jnp.logical_and(plane > 0, plane < planes - 1)
+
     def plane_out(c, k):
+        target, block_at, land = far[k], far[k], k - 1
+        if relayed and k == 1:
+            end = plane == planes - 1
+            target, block_at, land = jnp.where(end, plane - 1, plane + 1), jnp.where(end, 0, plane + 1), jnp.where(end, 3, 0)
+        if relayed and k == 3:
+            end = plane == 0
+            target, block_at, land = jnp.where(end, 1, plane - 1), jnp.where(end, planes - 1, plane - 1), jnp.where(end, 3, 2)
         return remote(
-            x_land.at[c % slots, far[k]], plane_land.at[c % slots, k - 1], plane_send.at[c, k - 1],
-            plane_recv.at[c, k - 1], plane_peers[k],
-        )
+            x_land.at[c % slots, block_at], plane_land.at[c % slots, land], plane_send.at[c, k - 1],
+            plane_recv.at[c, land], device_of(target, across, core, tensor),
+        )
+
+    def plane_in(c, land):
+        return remote(
+            x_land.at[c % slots, plane], plane_land.at[c % slots, land], plane_send.at[c, 0],
+            plane_recv.at[c, land], x_peer,
+        )
+
+    def relay(c):
+        @pl.when(middle)
+        def _():
+            plane_in(c, 3).wait_recv()
+            x_land[c % slots, far[2]] = (
+                x_land[c % slots, far[2]].astype(jnp.float32) + plane_land[c % slots, 3].astype(jnp.float32)
+            ).astype(jnp.bfloat16)
+            plane_out(c, 2).start()
 
     def grad_out(c):
         _, _, _, _, result, start = jobs[c]
@@ -814,17 +856,28 @@
             ).astype(jnp.bfloat16)
 
         for k in range(1, planes):
-            plane_out(c, k).start()
+            if relayed and k == 2:
+                @pl.when(jnp.logical_not(middle))
+                def _():
+                    plane_out(c, 2).start()
+            else:
+                plane_out(c, k).start()
 
     def finish(c):
         for k in range(1, planes):
-            plane_out(c, k).wait()
+            plane_out(c, k).wait_send()
         if c >= 2:
             grad_out(c - 2).wait()
-        value = x_land[c % slots, plane].astype(jnp.float32)
-        for k in range(1, planes):
-            value += plane_land[c % slots, k - 1].astype(jnp.float32)
-        out_buf[c % 2] = value
+        out_buf[c % 2] = x_land[c % slots, plane].astype(jnp.float32)
+        for land in range(planes - 1):
+            def add():
+                plane_in(c, land).wait_recv()
+                out_buf[c % 2] = out_buf[c % 2] + plane_land[c % slots, land].astype(jnp.float32)
+
+            if relayed and land != 1:
+                pl.when((plane > 0) if land == 0 else (plane < planes - 1))(add)
+            else:
+                add()
         grad_out(c).start()
 
     def small_copy(step, peer, slot):
@@ -965,7 +1018,7 @@
             for copy in row_copies(which, i):
                 copy.wait()
 
-            @pl.loop(0, strip // 16)
+            @pl.loop(0, strip // 16, unroll=2)
             def _(r):
                 local_rows = pl.ds(pl.multiple_of(r * 16, 16), 16)
                 rows = pl.ds(pl.multiple_of(row_start(which, i) + r * 16, 16), 16)
@@ -1212,6 +1265,8 @@
             step[0](*step[1:])
         if 2 <= n < total + 2:
             fold(n - 2)
+        if relayed and 3 <= n < total + 3:
+            relay(n - 3)
         if n >= 4:
             finish(n - 4)
     local(small_land.at[1], small_out, load_sem.at[0]).wait()
@@ -1231,7 +1286,7 @@
     up_cols = weights[4].shape[-1]
     tokens, features = saved[0].shape
     total = (2 * up_cols + 4 * head_cols) // JOB
-    slots = 8
+    slots, lands = 8, max(planes - 1, 4)
     thin, strip = 256, 64
     sem, low, high = pltpu.SemaphoreType.DMA, jnp.bfloat16, jnp.float32
     hbm, vmem = pl.BlockSpec(memory_space=pl.ANY), pl.BlockSpec(memory_space=pltpu.VMEM)
@@ -1248,7 +1303,7 @@
     )
     scratch = [
         ((2, 2, planes, rows, 2 * tokens), low), ((2, 2 * tokens, JOB), low), ((3, 2, planes, rows, JOB), low),
-        ((slots, planes, rows, JOB), low), ((slots, planes - 1, rows, JOB), low), ((2, rows, JOB), high),
+        ((slots, planes, rows, JOB), low), ((slots, lands, rows, JOB), low), ((2, rows, JOB), high),
         ((2, planes, 2, 2, rows, thin), low), ((2, 2, 2, rows, features), low), ((tokens, features), low),
         ((tokens, up_cols), low), ((2, tokens, thin), low), ((tokens, features), high),
         ((tokens, features), low), ((tokens, features), low), ((tokens, 3 * head_cols), low),
@@ -1258,7 +1313,7 @@
     ]
     sems = [
         (2, 2, 2), (2, 2), (2,), (total,), (total,), (4,), (4,), (total,), (total,),
-        (total, planes - 1), (total, planes - 1), (2 + planes,), (2 + planes,), (2, planes), (2, 2), (2,),
+        (total, planes - 1), (total, lands), (2 + planes,), (2 + planes,), (2, planes), (2, 2), (2,),
         (4,), (5,), (1,), (planes,), (planes,), (planes,), (planes,), (2, 2), (2, groups), (2, groups),
     ]
     results = pl.pallas_call(

time: 788 us -> 725 us (0.920)
  Pallas kernels: 741 us -> 685 us
    pallas_call x1, Pallas kernels: 388 us -> 343 us  [forward(): pl.pallas_call(partial(forward_kernel, planes, widths), out_shape=[jax.Sh...]
    pallas_call x1, Pallas kernels: 353 us -> 342 us  [backward(): pl.pallas_call(partial(backward_kernel, planes), out_shape=[jax.ShapeDtyp...]
where the time goes in v6:
time: 725 us; the launch traced here: 721 us
  Pallas kernels  685 us (94%)
  local copies, waits for them, and re-layouts  30.3 us (4%)
    pallas_call x1, Pallas kernels, forward(): pl.pallas_call(partial(forward_kernel, planes, widths), out_shape=[jax.Sh...  343 us
    pallas_call x1, Pallas kernels, backward(): pl.pallas_call(partial(backward_kernel, planes), out_shape=[jax.ShapeDtyp...  342 us
    unnamed x43, local copies, waits for them, and re-layouts  21 us

profile of v6, /device:TPU:0, one launch (start us, length us, event | category | flops | bytes accessed | tf_op | source)
XLA Modules:
  0.0 720.7 jit_solution(2785491267724315887)
XLA Ops:
  0.7 0.7 dynamic-slice_dynamic-update-slice_fusion.1
  1.4 0.7 constant_dynamic-update-slice_fusion.6
  2.0 0.7 constant_dynamic-update-slice_fusion.5
  2.7 0.7 constant_dynamic-update-slice_fusion.4
  3.4 0.7 constant_dynamic-update-slice_fusion.3
  4.1 0.7 dynamic-slice_dynamic-update-slice_fusion
  4.9 0.7 constant_dynamic-update-slice_fusion.2
  5.6 0.7 constant_dynamic-update-slice_fusion.1
  6.2 0.7 constant_dynamic-update-slice_fusion
  6.9 1.2 dynamic_slice.15
  10.1 1.2 dynamic_slice.16
  11.4 0.6 fusion
  12.0 0.6 broadcast_in_dim.22.refs_9_.refs_17_
  12.6 0.7 compare_select_fusion
  13.3 2.0 copy.50
  15.4 0.0 copy-start.10
  15.4 0.6 gather_fusion
  16.0 0.0 copy-done.8
  16.0 0.0 copy-done.10
  16.1 0.2 broadcast_select_fusion
  16.3 0.0 copy-start.2
  16.3 1.0 slice.46.refs_6_
  17.3 0.1 slice.47
  17.4 0.8 reshape.74.refs_7_
  18.2 0.0 copy-done.2
  18.2 1.3 copy.42
  19.5 0.0 copy-done.7
  19.5 0.8 copy.41
  20.4 342.6 %forward_gather.1 = (bf16[4,2,2,128,1024]{4,3,2,1,0:T(8,128)(2,1)}, bf16[4,2,2,128,1024]{4,3,2,1,0:T(8,128)(2,1)}, bf16[4,2,2,128,1024]{4,3,2,1,0:T(8,128)(2,1)}...) custom-call(bf16[128,1024]{1,0:T(8,128)(2,1)} %refs_0_.1, ...), custom_call_target="tpu_custom_call" | custom-call | tf_op jit(solution)/shard_map/forward_gather/pallas_call | solution.py:621
  363.0 342.0 %backward_scatter.1 = (f32[128,1024]{1,0:T(8,128)}, f32[128,1024]{1,0:T(8,128)}, f32[128,1024]{1,0:T(8,128)}, f32[128,1024]{1,0:T(8,128)}, f32[128,4096]{1,0:T(8...) custom-call(bf16[4,2,2,128,1024]{4,3,2,1,0:T(8,128)(2,1)} %get-tuple, ...), custom_call_target="tpu_custom_call" | custom-call | tf_op jit(solution)/shard_map/backward_scatter/pallas_call | solution.py:1319
  704.9 1.0 reshape.79
  705.9 1.4 pad_maximum_fusion
  707.4 0.2 broadcast.19
  707.6 1.1 scatter_fusion
  708.7 1.8 copy.45
  710.5 3.0 copy.47
  713.5 0.0 copy-done.6
  713.5 1.0 copy.46
  714.5 0.0 copy-done.9
  714.5 0.6 fusion.1
  715.1 0.6 copy.48
  715.8 0.0 copy-done.1
  715.8 1.1 copy.65
  716.8 0.8 copy.66
  717.6 0.8 copy.67
  718.4 0.8 copy.68
  719.2 0.0 copy-done
  719.2 1.3 copy.69
  (15 shorter events, 0.0 us)
Async XLA Ops:
  6.9 9.1 %copy-start.8 = (f32[18432]{0:T(1024)}, f32[18432]{0:T(1024)S(1)}, u32[]{:S(2)}) copy-start(f32[18432]{0:T(1024)S(1)} %constant_dynamic-update-slice_fusion) | copy-start | bytes 221188
  15.4 0.7 copy-start.10
  16.3 1.9 copy-start.2
  17.3 2.2 copy-start.7
  710.5 3.0 copy-start.6
  710.5 4.0 copy-start.9
  710.5 5.3 copy-start.1
  713.5 3.3 copy-start.5
  714.5 3.1 copy-start.4
  715.8 2.7 copy-start.3
  716.8 2.4 copy-start

commit v7 on v6

--- a/solution.py
+++ b/solution.py
@@ -71,8 +71,9 @@
     count = len(widths)
     shard_refs = refs[:count]
     deal_refs = refs[count : count + 2]
-    cot_ref, mask_ref, vec_ref = refs[count + 2 : count + 5]
-    outs = refs[count + 5 :]
+    cot_ref, lengths_ref, dealing_ref = refs[count + 2 : count + 5]
+    vector_refs = refs[count + 5 : count + 14]
+    outs = refs[count + 14 :]
     full_refs = outs[:count]
     (
         x_full, cot_full, qkv_out, mixed_out, normed_out, inverse_out, hidden_out, active_out, slope_out,
@@ -80,10 +81,10 @@
     ) = outs[count : count + 13]
     (
         w_buf, x_buf, qkv_buf, mixed_buf, attn_acc, attn_land, send_buf, hidden_buf, active_buf, slope_buf,
-        down_acc, down_land, inverse_buf, result_buf, sums_buf, whole_land, rest_land,
+        down_acc, down_land, inverse_buf, result_buf, sums_buf, whole_land, rest_land, vec_buf, mask_buf,
         plane_send, plane_recv, x_send, x_recv, core_send, core_recv, w_sem, in_send, in_recv,
         attn_send, attn_recv, down_send, down_recv, load_sem, store_sem,
-        deal_send, deal_recv,
+        deal_send, deal_recv, vec_sem,
     ) = outs[count + 13 :]
     plane, across, core, tensor = place()
     far = [lax.rem(plane + k, planes) for k in range(planes)]
@@ -99,18 +100,25 @@
     factor = HEAD_DIM ** (-0.5)
     own_rows = pl.ds(pl.multiple_of(tensor * half, half), half)
 
-    vec_at = {}
+    vec_at, vec_copies = {}, []
     at = 0
-    for key, size in (
-        ("b_query", head_cols), ("b_value", head_cols), ("b_out", features), ("gain_first", features),
-        ("shift_first", features), ("b_up", widths[4]), ("b_down", features), ("gain_second", features),
-        ("shift_second", features),
+    for key, size, part in (
+        ("b_query", head_cols, True), ("b_value", head_cols, True), ("b_out", features, False),
+        ("gain_first", features, False), ("shift_first", features, False), ("b_up", widths[4], True),
+        ("b_down", features, False), ("gain_second", features, False), ("shift_second", features, False),
     ):
         vec_at[key] = at
+        start = pl.multiple_of(tensor * size, size) if part else 0
+        vec_copies.append(
+            pltpu.make_async_copy(
+                vector_refs[len(vec_copies)].at[:, pl.ds(start, size)], vec_buf.at[:, pl.ds(at, size)],
+                vec_sem.at[len(vec_copies)],
+            )
+        )
         at += size
 
     def vector(key, start, size):
-        return vec_ref[:, pl.ds(vec_at[key] + start, size)]
+        return vec_buf[:, pl.ds(vec_at[key] + start, size)]
 
     first_down = len(tiles) - widths[5] // TILE
     units = [(c, j) for c in range(first_down) for j in range(planes)]
@@ -343,7 +351,7 @@
                 x_buf[...], flat(w_buf[c % 2, :, :, :, :, cols]), preferred_element_type=jnp.float32
             )
             if bias is not None:
-                value += vec_ref[:, pl.ds(pl.multiple_of(vec_at[bias] + n * 512, 128), 512)]
+                value += vec_buf[:, pl.ds(pl.multiple_of(vec_at[bias] + n * 512, 128), 512)]
             qkv_buf[:, pl.ds(pl.multiple_of(c * TILE + n * 512, 512), 512)] = value.astype(jnp.bfloat16)
 
     def attend(first, last):
@@ -353,7 +361,7 @@
                 return pl.ds(pl.multiple_of(which * head_cols + h * HEAD_DIM, HEAD_DIM), HEAD_DIM)
 
             scores = contract_cols(qkv_buf[:, cols(0)], qkv_buf[:, cols(1)]) * factor
-            scores = jnp.where(mask_ref[0:1, :] > 0.0, scores, MASKED)
+            scores = jnp.where(mask_buf[0:1, :] > 0.0, scores, MASKED)
             expanded = jnp.exp(scores - jnp.max(scores, axis=1, keepdims=True))
             weight = (expanded / jnp.sum(expanded, axis=1, keepdims=True)).astype(jnp.bfloat16)
             mixed_buf[:, cols(0)] = jnp.dot(
@@ -384,7 +392,7 @@
         def _(p):
             attn_share(p).wait()
 
-        @pl.loop(0, tokens // 16, unroll=2)
+        @pl.loop(0, tokens // 16, unroll=4)
         def _(i):
             rows = pl.ds(pl.multiple_of(i * 16, 16), 16)
             value = (
@@ -426,7 +434,7 @@
             value = jnp.dot(
                 hidden_buf[...], flat(w_buf[c % 2, :, :, :, :, cols]), preferred_element_type=jnp.float32
             )
-            value += vec_ref[:, pl.ds(pl.multiple_of(vec_at["b_up"] + j * TILE + n * 256, 128), 256)]
+            value += vec_buf[:, pl.ds(pl.multiple_of(vec_at["b_up"] + j * TILE + n * 256, 128), 256)]
             square = value * value
             bend = jnp.tanh(SLOPE * value * (1.0 + 0.044715 * square))
             rise = 0.5 * (1.0 + bend)
@@ -471,7 +479,7 @@
             return pl.ds(pl.multiple_of(base * half + i * 16, 16), 16)
 
         for which in (0, 1):
-            @pl.loop(0, half // 16, unroll=2)
+            @pl.loop(0, half // 16, unroll=4)
             def _(i):
                 rows = rows_of(which, i)
                 hidden = attn_acc[rows, :] * vector("gain_first", 0, features) + vector(
@@ -506,6 +514,8 @@
 
     for c in range(len(tiles)):
         own_load(c).start()
+    for copy in vec_copies:
+        copy.start()
     for which, land in deal_parts:
         deal_own(which, land).start()
     enter([(lax.rem(index + k, groups), tensor) for k in range(1, groups)] + [y_peer])
@@ -521,6 +531,11 @@
         own_store(c).start()
     for c in range(len(tiles)):
         own_store(c).wait()
+    for copy in vec_copies:
+        copy.wait()
+    mask_buf[...] = (
+        lax.broadcasted_iota(jnp.int32, mask_buf.shape, 1) < lengths_ref[dealing_ref[index]]
+    ).astype(jnp.float32)
 
     plan = {}
 
@@ -596,7 +611,7 @@
         unit_core(u, core).wait_send()
 
 
-def forward(shard_list, dealt_rows, cot, mask, vectors):
+def forward(shard_list, dealt_rows, cot, lengths, dealing, vectors):
     planes = lax.axis_size("dp") // 4
     widths = [shard.shape[1] for shard in shard_list]
     total = sum(width // TILE for width in widths)
@@ -610,7 +625,7 @@
     rest_rows = rest_rows.reshape(groups, padded, chunks, features // chunks)
     rest_rows = rest_rows.transpose(0, 2, 1, 3).reshape(groups, 16, features // chunks)
     sem, low, high = pltpu.SemaphoreType.DMA, jnp.bfloat16, jnp.float32
-    hbm, vmem = pl.BlockSpec(memory_space=pl.ANY), pl.BlockSpec(memory_space=pltpu.VMEM)
+    hbm = pl.BlockSpec(memory_space=pl.ANY)
     shapes = [((planes, 2, 2, *shard.shape), low) for shard in shard_list] + [
         ((tokens, features), low), ((tokens, features), low), ((tokens, 3 * head_cols), low),
         ((tokens, head_cols), low), ((tokens, features), high), ((tokens, 128), high),
@@ -621,7 +636,7 @@
     results = pl.pallas_call(
         partial(forward_kernel, planes, widths),
         out_shape=[jax.ShapeDtypeStruct(*shape) for shape in shapes],
-        in_specs=[hbm] * (len(shard_list) + 3) + [vmem] * 2,
+        in_specs=[hbm] * (len(shard_list) + 3) + [pl.BlockSpec(memory_space=pltpu.SMEM)] * 2 + [hbm] * len(vectors),
         out_specs=[hbm] * len(shapes),
         scratch_shapes=[
             pltpu.VMEM((2, planes, 2, 2, rows, TILE), low),
@@ -641,16 +656,18 @@
             pltpu.VMEM((3, 16, features), high),
             pltpu.VMEM(whole_rows.shape, low),
             pltpu.VMEM(rest_rows.shape, low),
+            pltpu.VMEM((1, 2 * head_cols + up_cols + 6 * features), high),
+            pltpu.VMEM((8, tokens), high),
             sem((total, max(planes, 7))), *[sem((total, planes))] * 5,
             sem((2, max(planes, 4))), sem((2,)), sem((2,)),
             sem((planes,)), sem((planes,)), sem((planes,)), sem((planes,)), sem((3,)), sem((12,)),
-            sem((2, groups)), sem((2, groups)),
+            sem((2, groups)), sem((2, groups)), sem((len(vectors),)),
         ],
         compiler_params=pltpu.CompilerParams(
             collective_id=0, has_side_effects=True, vmem_limit_bytes=62 * 2**20
         ),
         name="forward_gather",
-    )(*shard_list, whole_rows, rest_rows, cot, mask, vectors)
+    )(*shard_list, whole_rows, rest_rows, cot, lengths, dealing, *vectors)
     return results[: len(shard_list)], results[len(shard_list) :]
 
 
@@ -661,20 +678,20 @@
     (
         query_w, key_w, value_w, out_w, up_w, down_w,
         x_in, qkv_in, mixed_in, normed_in, inverse_in, hidden_in, active_in, slope_in, down_in, second_in,
-        sums_in, mask_ref, gain_ref,
-    ) = refs[:19]
+        sums_in, lengths_ref, dealing_ref, gain_ref,
+    ) = refs[:20]
     (
         grad_query, grad_key, grad_value, grad_out_w, grad_up, grad_down, small_out, whole_out, rest_out,
         left_own, left_far, active_far, rise_own, rise_far, mixed_far, qkv_own, qkv_far,
-    ) = refs[19:36]
+    ) = refs[20:37]
     (
         left_buf, right_buf, stage, x_land, plane_land, out_buf, tile_buf, wide_buf, low_buf, rise_buf,
         slope_buf, acc_buf, hidden_land, send_buf, qkv_buf, turn_buf, input_land, row_buf, inverse_buf,
-        sums_buf, small_land, whole_buf, rest_buf, rest_wide,
+        sums_buf, small_land, whole_buf, rest_buf, rest_wide, mask_buf,
         left_sem, right_sem, out_sem, core_send, core_recv, left_send, left_recv, x_send, x_recv,
         plane_send, plane_recv, small_send, small_recv, tile_sem, wide_sem, slope_sem, load_sem, store_sem,
         turn_sem, hidden_send, hidden_recv, input_send, input_recv, row_sem, back_send, back_recv,
-    ) = refs[36:]
+    ) = refs[37:]
     plane, across, core, tensor = place()
     far = [lax.rem(plane + k, planes) for k in range(planes)]
     x_peer = device_of(plane, 1 - across, core, tensor)
@@ -691,13 +708,15 @@
     slots = x_land.shape[0]
     thin = tile_buf.shape[-1]
 
-    jobs = [(0, active_in, active_far, s, grad_down, s) for s in range(0, up_cols, JOB)]
-    jobs += [(1, rise_own, rise_far, s, grad_up, s) for s in range(0, up_cols, JOB)]
-    jobs += [(2, mixed_in, mixed_far, s, grad_out_w, s) for s in range(0, head_cols, JOB)]
+    jobs = [(0, active_in, active_far, s, grad_down, s, JOB) for s in range(0, up_cols, JOB)]
+    jobs += [(1, rise_own, rise_far, s, grad_up, s, JOB) for s in range(0, up_cols, JOB)]
+    jobs += [(2, mixed_in, mixed_far, s, grad_out_w, s, JOB) for s in range(0, head_cols, JOB)]
     for which, result in enumerate((grad_query, grad_key, grad_value)):
         jobs += [
-            (3, qkv_own, qkv_far, which * head_cols + s, result, s) for s in range(0, head_cols, JOB)
+            (3, qkv_own, qkv_far, which * head_cols + s, result, s, JOB) for s in range(0, head_cols, JOB)
         ]
+    a, own, other, start, result, at, width = jobs.pop()
+    jobs += [(a, own, other, start + s, result, at + s, width // 2) for s in (0, width // 2)]
     total = len(jobs)
     up_first, out_first, qkv_first = (
         [job[0] for job in jobs].index(a) for a in (1, 2, 3)
@@ -740,8 +759,8 @@
         left_out(a).start()
 
     def right_out(c, source=None):
-        _, own, other, start, _, _ = jobs[c]
-        cols = pl.ds(start, JOB)
+        _, own, other, start, _, _, width = jobs[c]
+        cols = pl.ds(start, width)
         return remote(
             (own if source is None else source).at[:, cols], other.at[:, cols], core_send.at[c],
             core_recv.at[c], core_peer,
@@ -760,16 +779,19 @@
         return copies
 
     def right_load(c):
-        _, own, other, start, _, _ = jobs[c]
-        slot, cols = c % 2, pl.ds(start, JOB)
+        _, own, other, start, _, _, width = jobs[c]
+        slot, cols, there = c % 2, pl.ds(start, width), pl.ds(0, width)
         return [
-            local(own.at[:, cols], right_buf.at[slot, pl.ds(0, tokens)], right_sem.at[slot, 0]),
-            local(other.at[:, cols], right_buf.at[slot, pl.ds(tokens, tokens)], right_sem.at[slot, 1]),
+            local(own.at[:, cols], right_buf.at[slot, pl.ds(0, tokens), there], right_sem.at[slot, 0]),
+            local(other.at[:, cols], right_buf.at[slot, pl.ds(tokens, tokens), there], right_sem.at[slot, 1]),
         ]
+
+    def used(c):
+        return pl.ds(0, jobs[c][-1])
 
     def x_out(c):
         return remote(
-            stage.at[c % 3, 1 - across], x_land.at[c % slots], x_send.at[c], x_recv.at[c], x_peer
+            stage.at[c % 3, 1 - across, :, :, used(c)], x_land.at[c % slots, :, :, used(c)], x_send.at[c], x_recv.at[c], x_peer
         )
 
     relayed = planes == 4
@@ -784,13 +806,13 @@
             end = plane == 0
             target, block_at, land = jnp.where(end, 1, plane - 1), jnp.where(end, planes - 1, plane - 1), jnp.where(end, 3, 2)
         return remote(
-            x_land.at[c % slots, block_at], plane_land.at[c % slots, land], plane_send.at[c, k - 1],
+            x_land.at[c % slots, block_at, :, used(c)], plane_land.at[c % slots, land, :, used(c)], plane_send.at[c, k - 1],
             plane_recv.at[c, land], device_of(target, across, core, tensor),
         )
 
     def plane_in(c, land):
         return remote(
-            x_land.at[c % slots, plane], plane_land.at[c % slots, land], plane_send.at[c, 0],
+            x_land.at[c % slots, plane, :, used(c)], plane_land.at[c % slots, land, :, used(c)], plane_send.at[c, 0],
             plane_recv.at[c, land], x_peer,
         )
 
@@ -798,14 +820,15 @@
         @pl.when(middle)
         def _():
             plane_in(c, 3).wait_recv()
-            x_land[c % slots, far[2]] = (
-                x_land[c % slots, far[2]].astype(jnp.float32) + plane_land[c % slots, 3].astype(jnp.float32)
+            x_land[c % slots, far[2], :, used(c)] = (
+                x_land[c % slots, far[2], :, used(c)].astype(jnp.float32)
+                + plane_land[c % slots, 3, :, used(c)].astype(jnp.float32)
             ).astype(jnp.bfloat16)
             plane_out(c, 2).start()
 
     def grad_out(c):
-        _, _, _, _, result, start = jobs[c]
-        return local(out_buf.at[c % 2], result.at[:, pl.ds(start, JOB)], out_sem.at[c % 2])
+        _, _, _, _, result, start, width = jobs[c]
+        return local(out_buf.at[c % 2, :, used(c)], result.at[:, pl.ds(start, width)], out_sem.at[c % 2])
 
     def new_left(c):
         return c == 0 or jobs[c - 1][0] != jobs[c][0]
@@ -833,7 +856,7 @@
         if c >= 3:
             x_out(c - 3).wait_send()
 
-        @pl.loop(0, JOB // 256)
+        @pl.loop(0, jobs[c][-1] // 256)
         def _(n):
             cols = pl.ds(pl.multiple_of(n * 256, 256), 256)
             left = left_buf[a % 2]
@@ -851,8 +874,9 @@
 
         @pl.loop(0, planes)
         def _(p):
-            x_land[slot, p] = (
-                x_land[slot, p].astype(jnp.float32) + stage[c % 3, across, p].astype(jnp.float32)
+            x_land[slot, p, :, used(c)] = (
+                x_land[slot, p, :, used(c)].astype(jnp.float32)
+                + stage[c % 3, across, p, :, used(c)].astype(jnp.float32)
             ).astype(jnp.bfloat16)
 
         for k in range(1, planes):
@@ -868,11 +892,13 @@
             plane_out(c, k).wait_send()
         if c >= 2:
             grad_out(c - 2).wait()
-        out_buf[c % 2] = x_land[c % slots, plane].astype(jnp.float32)
+        out_buf[c % 2, :, used(c)] = x_land[c % slots, plane, :, used(c)].astype(jnp.float32)
         for land in range(planes - 1):
             def add():
                 plane_in(c, land).wait_recv()
-                out_buf[c % 2] = out_buf[c % 2] + plane_land[c % slots, land].astype(jnp.float32)
+                out_buf[c % 2, :, used(c)] = out_buf[c % 2, :, used(c)] + plane_land[
+                    c % slots, land, :, used(c)
+                ].astype(jnp.float32)
 
             if relayed and land != 1:
                 pl.when((plane > 0) if land == 0 else (plane < planes - 1))(add)
@@ -1080,7 +1106,7 @@
                 rows = slice(part * half, (part + 1) * half)
                 query, grad_mixed = rise_buf[rows, cols(0)], rise_buf[rows, cols(3)]
                 scores = contract_cols(query, key) * factor
-                scores = jnp.where(mask_ref[0:1, :] > 0.0, scores, MASKED)
+                scores = jnp.where(mask_buf[0:1, :] > 0.0, scores, MASKED)
                 expanded = jnp.exp(scores - jnp.max(scores, axis=1, keepdims=True))
                 weight = expanded / jnp.sum(expanded, axis=1, keepdims=True)
                 grad_weight = contract_cols(grad_mixed, value)
@@ -1208,6 +1234,9 @@
         right_out(c).start()
     local(down_in, low_buf, load_sem.at[0]).wait()
     turn(0, low_buf)
+    mask_buf[...] = (
+        lax.broadcasted_iota(jnp.int32, mask_buf.shape, 1) < lengths_ref[dealing_ref[index]]
+    ).astype(jnp.float32)
     small_land[0] = jnp.zeros(small_land.shape[1:], jnp.float32)
     local(sums_in, sums_buf, load_sem.at[2]).wait()
     for i, row in enumerate((10, 11, 7)):
@@ -1246,17 +1275,17 @@
         3: [(rise, 3), (turn_hidden,), (hidden_start,)],
         4: [(hidden_back, 0, planes // 2)],
         5: [(hidden_back, planes // 2, planes), (norm_start,), (start_out,), (stored,)],
-        10: [(norm_back,), (mixed_start,)],
-        11: [(turn, 2, low_buf), (mixed_back,), (load_input,)],
-        12: [(wait_qkv,), (attend_back, 0, heads // 4), (turn_input,)],
-        13: [(attend_back, heads // 4, heads // 2)],
-        14: [(attend_back, heads // 2, 3 * heads // 4)],
-        15: [(attend_back, 3 * heads // 4, heads), (attend_done,)],
-        16: [(input_back, 0, planes // 2), (small_begin, 0), (store_qkv_wait,)],
-        17: [(input_back, planes // 2, planes), (small_end, 0), (small_begin, 1)],
-        18: [(small_end, 1), (small_begin, 2)],
-        19: [(small_end, 2), (small_begin, 3)],
-        20: [(input_done,), (send_back,), (small_end, 3)],
+        11: [(norm_back,), (mixed_start,)],
+        12: [(turn, 2, low_buf), (mixed_back,), (load_input,)],
+        13: [(wait_qkv,), (attend_back, 0, heads // 4), (turn_input,)],
+        14: [(attend_back, heads // 4, heads // 2)],
+        15: [(attend_back, heads // 2, 3 * heads // 4)],
+        16: [(attend_back, 3 * heads // 4, heads), (attend_done,), (store_qkv_wait,)],
+        17: [(input_back, 0, planes // 2), (small_begin, 0)],
+        18: [(input_back, planes // 2, planes), (small_end, 0), (small_begin, 1)],
+        19: [(small_end, 1), (small_begin, 2)],
+        20: [(small_end, 2), (small_begin, 3)],
+        21: [(input_done,), (send_back,), (small_end, 3)],
     }
     for n in range(total + 4):
         if n < total:
@@ -1281,11 +1310,11 @@
         grad_out(c).wait()
 
 
-def backward(weights, saved, mask, gain):
+def backward(weights, saved, lengths, dealing, gain):
     planes, _, _, rows, head_cols = weights[0].shape
     up_cols = weights[4].shape[-1]
     tokens, features = saved[0].shape
-    total = (2 * up_cols + 4 * head_cols) // JOB
+    total = (2 * up_cols + 4 * head_cols) // JOB + 1
     slots, lands = 8, max(planes - 1, 4)
     thin, strip = 256, 64
     sem, low, high = pltpu.SemaphoreType.DMA, jnp.bfloat16, jnp.float32
@@ -1309,7 +1338,7 @@
         ((tokens, features), low), ((tokens, features), low), ((tokens, 3 * head_cols), low),
         ((planes, 2, 2, rows, tokens), low), ((tokens // 2, features), low), ((2, 2, strip, features), high),
         ((tokens, 128), high), ((3, 16, features), high), ((3 + planes, small_rows, features), high),
-        whole_shape, rest_rows, ((16, features // chunks), high),
+        whole_shape, rest_rows, ((16, features // chunks), high), ((8, tokens), high),
     ]
     sems = [
         (2, 2, 2), (2, 2), (2,), (total,), (total,), (4,), (4,), (total,), (total,),
@@ -1319,14 +1348,14 @@
     results = pl.pallas_call(
         partial(backward_kernel, planes),
         out_shape=[jax.ShapeDtypeStruct(*shape) for shape in shapes],
-        in_specs=[hbm] * 17 + [vmem] * 2,
+        in_specs=[hbm] * 17 + [pl.BlockSpec(memory_space=pltpu.SMEM)] * 2 + [vmem],
         out_specs=[hbm] * len(shapes),
         scratch_shapes=[pltpu.VMEM(*shape) for shape in scratch] + [sem(shape) for shape in sems],
         compiler_params=pltpu.CompilerParams(
             collective_id=1, has_side_effects=True, vmem_limit_bytes=62 * 2**20
         ),
         name="backward_scatter",
-    )(*weights, *saved, mask, gain)
+    )(*weights, *saved, lengths, dealing, gain)
     whole_rows, rest_rows = results[7], results[8]
     rest_rows = rest_rows.reshape(groups, chunks, padded, features // chunks).transpose(0, 2, 1, 3)
     returned = rest_rows.reshape(groups, padded, features)[:, :rest]
@@ -1356,26 +1385,18 @@
     shift_second,
     cotangent,
 ):
-    group_index = lax.axis_index("dp")
-    tensor_index = lax.axis_index("tensor")
-    ordered = jnp.take(inputs, dealing, axis=0)
+    ordered = inputs.at[dealing].get(mode="promise_in_bounds", unique_indices=True)
     features = cotangent.shape[-1]
     half_rows = cotangent.shape[1]
-    seq_len = half_rows * lax.axis_size("tensor")
-    length = lengths[dealing[group_index]]
-    key_valid = jnp.arange(seq_len) < length
-    head_cols = w_query.shape[1]
-    up_cols = w_up.shape[1]
-    query_bias = lax.dynamic_slice_in_dim(b_query, tensor_index * head_cols, head_cols)
-    value_bias = lax.dynamic_slice_in_dim(b_value, tensor_index * head_cols, head_cols)
-    up_bias = lax.dynamic_slice_in_dim(b_up, tensor_index * up_cols, up_cols)
-    vectors = jnp.concatenate(
-        (query_bias, value_bias, b_out, gain_first, shift_first, up_bias, b_down, gain_second, shift_second)
-    ).reshape(1, -1)
-    mask = jnp.broadcast_to(key_valid.astype(jnp.float32), (8, seq_len))
+    vectors = [
+        vector.reshape(1, -1)
+        for vector in (
+            b_query, b_value, b_out, gain_first, shift_first, b_up, b_down, gain_second, shift_second,
+        )
+    ]
     weights, saved = forward(
         [w_query, w_key, w_value, w_out.T, w_up, w_down.T],
-        ordered.reshape(ordered.shape[0], -1, features), cotangent.reshape(half_rows, features), mask, vectors,
+        ordered.reshape(ordered.shape[0], -1, features), cotangent.reshape(half_rows, features), lengths, dealing, vectors,
     )
     (
         full_in, _, qkv, mixed_heads, normed_full, inverse_full, full_hidden, active, slope,
@@ -1388,7 +1409,7 @@
             full_in, qkv, mixed_heads, normed_full, inverse_full, full_hidden, active, slope,
             full_grad_down, second_full, second_sums,
         ],
-        mask, gain_first.reshape(1, -1),
+        lengths, dealing, gain_first.reshape(1, -1),
     )
     returned = grad_own.reshape(inputs.shape)
     grad_inputs = jnp.zeros_like(returned).at[dealing].set(returned)

time: 725 us -> 709 us (0.978)
  local copies, waits for them, and re-layouts: 30.3 us -> 20.9 us
  Pallas kernels: 685 us -> 676 us
    pallas_call x1, Pallas kernels: 343 us -> 333 us  [forward(): pl.pallas_call(partial(forward_kernel, planes, widths), out_shape=[jax.Sh...]
    unnamed x43 -> x31, local copies, waits for them, and re-layouts: 21 us -> 15.4 us
where the time goes in v7:
time: 709 us; the launch traced here: 700 us
  Pallas kernels  676 us (95%)
  local copies, waits for them, and re-layouts  20.9 us (3%)
    pallas_call x1, Pallas kernels, backward(): pl.pallas_call(partial(backward_kernel, planes), out_shape=[jax.ShapeDtyp...  343 us
    pallas_call x1, Pallas kernels, forward(): pl.pallas_call(partial(forward_kernel, planes, widths), out_shape=[jax.Sh...  333 us
    unnamed x31, local copies, waits for them, and re-layouts  15.4 us

profile of v7, /device:TPU:0, one launch (start us, length us, event | category | flops | bytes accessed | tf_op | source)
XLA Modules:
  0.0 700.4 jit_solution(16112885337696196897)
XLA Ops:
  0.7 0.7 compare_select_fusion
  1.3 2.0 copy.50
  3.4 0.6 gather_fusion
  4.0 0.0 copy-start.2
  4.0 1.0 slice.46.refs_6_
  5.1 0.0 copy-start.7
  5.1 0.1 slice.47
  5.2 0.8 reshape.91.refs_7_
  6.0 0.0 copy-done.2
  6.0 1.3 copy.42
  7.3 0.0 copy-done.7
  7.3 0.8 copy.41
  8.1 332.9 %forward_gather.1 = (bf16[4,2,2,128,1024]{4,3,2,1,0:T(8,128)(2,1)}, bf16[4,2,2,128,1024]{4,3,2,1,0:T(8,128)(2,1)}, bf16[4,2,2,128,1024]{4,3,2,1,0:T(8,128)(2,1)}...) custom-call(bf16[128,1024]{1,0:T(8,128)(2,1)} %refs_0_.1, ...), custom_call_target="tpu_custom_call" | custom-call | tf_op jit(solution)/shard_map/forward_gather/pallas_call | solution.py:636
  341.0 343.4 %backward_scatter.1 = (f32[128,1024]{1,0:T(8,128)}, f32[128,1024]{1,0:T(8,128)}, f32[128,1024]{1,0:T(8,128)}, f32[128,1024]{1,0:T(8,128)}, f32[128,4096]{1,0:T(8...) custom-call(bf16[4,2,2,128,1024]{4,3,2,1,0:T(8,128)(2,1)} %get-tuple, ...), custom_call_target="tpu_custom_call" | custom-call | tf_op jit(solution)/shard_map/backward_scatter/pallas_call | solution.py:1348
  684.3 1.0 reshape.103
  685.4 1.4 pad_maximum_fusion
  686.8 0.2 broadcast.8
  687.0 1.1 scatter_fusion
  688.1 1.8 copy.45
  689.9 0.0 copy-start.6
  689.9 0.0 copy-start.8
  689.9 0.0 copy-start.1
  689.9 3.0 copy.47
  692.9 0.0 copy-start.5
  692.9 0.0 copy-done.6
  692.9 1.0 copy.46
  693.9 0.0 copy-start.4
  693.9 0.0 copy-done.8
  693.9 0.6 fusion
  694.6 0.6 copy.48
  695.2 0.0 copy-done.1
  695.2 0.0 copy-start.3
  695.2 1.1 copy.57
  696.3 0.0 copy-done.5
  696.3 0.0 copy-start
  696.3 0.8 copy.58
  697.1 0.0 copy-done.4
  697.1 0.8 copy.59
  697.8 0.0 copy-done.3
  697.9 0.8 copy.60
  698.6 0.0 copy-done
  698.6 1.3 copy.61
  (2 shorter events, 0.0 us)
Async XLA Ops:
  4.0 1.9 copy-start.2
  5.1 2.2 copy-start.7
  689.9 3.0 copy-start.6
  689.9 4.0 copy-start.8
  689.9 5.3 copy-start.1
  692.9 3.3 copy-start.5
  693.9 3.1 copy-start.4
  695.2 2.7 copy-start.3
  696.3 2.4 copy-start

commit v8 on v7

--- a/solution.py
+++ b/solution.py
@@ -54,7 +54,7 @@
     pl.semaphore_wait(barrier, len(peers))
 
 
-LAG, LEAD, X_FIRST, DEALT, X_LEAD, NORM = 4, (3, 2, 1), (3, 7), 7, 6, 14
+LAG, LEAD, X_FIRST, DEALT, X_LEAD, NORM = 4, (3, 2, 1), (3, 7), 8, 6, 14
 
 
 def rest_shape(count):
@@ -297,6 +297,11 @@
     def deal_own(which, land):
         return pltpu.make_async_copy(deal_refs[which].at[index], land.at[index], deal_recv.at[which, 0])
 
+    def deal_some(i):
+        for k in range(1 + i, groups, 5):
+            for which, land in deal_parts:
+                deal(which, land, k).start()
+
     def dealt():
         for which, land in deal_parts:
             deal_own(which, land).wait()
@@ -522,9 +527,7 @@
     z_begin(-1)
     for c in sorted({*range(X_LEAD), *across_first}):
         x_copy(c, 0, across).start()
-    for k in range(1, groups):
-        for which, land in deal_parts:
-            deal(which, land, k).start()
+    deal_some(0)
     z_begin(0)
     for c in range(len(tiles)):
         own_load(c).wait()
@@ -546,6 +549,8 @@
         return planes * (c + 1) + lag
 
     heads = head_cols // HEAD_DIM
+    for i in range(1, 5):
+        at_slot(i, deal_some, i)
     at_slot(DEALT, dealt)
     at_slot(ready(0), load_tile, 0)
     at_slot(ready(1), load_tile, 1)
@@ -672,6 +677,7 @@
 
 
 JOB = 512
+PLANE_FIRST = ()
 
 
 def backward_kernel(planes, *refs):
@@ -690,7 +696,7 @@
         sums_buf, small_land, whole_buf, rest_buf, rest_wide, mask_buf,
         left_sem, right_sem, out_sem, core_send, core_recv, left_send, left_recv, x_send, x_recv,
         plane_send, plane_recv, small_send, small_recv, tile_sem, wide_sem, slope_sem, load_sem, store_sem,
-        turn_sem, hidden_send, hidden_recv, input_send, input_recv, row_sem, back_send, back_recv,
+        turn_sem, hidden_send, hidden_recv, input_send, input_recv, row_sem, back_send, back_recv, first_send, first_recv,
     ) = refs[37:]
     plane, across, core, tensor = place()
     far = [lax.rem(plane + k, planes) for k in range(planes)]
@@ -797,7 +803,9 @@
     relayed = planes == 4
     middle = jnp.logical_and(plane > 0, plane < planes - 1)
 
-    def plane_out(c, k):
+    plane_first = PLANE_FIRST if relayed else ()
+
+    def route(k):
         target, block_at, land = far[k], far[k], k - 1
         if relayed and k == 1:
             end = plane == planes - 1
@@ -805,6 +813,75 @@
         if relayed and k == 3:
             end = plane == 0
             target, block_at, land = jnp.where(end, 1, plane - 1), jnp.where(end, planes - 1, plane - 1), jnp.where(end, 3, 2)
+        return target, block_at, land
+
+    def first_rows(c, side):
+        rows = x_land.shape[2]
+        return pl.ds(pl.multiple_of((plane_first.index(c) * 2 + side) * rows, rows), rows)
+
+    def first_out(c, k, side):
+        target, block_at, land = route(k)
+        at = plane_first.index(c)
+        return remote(
+            stage.at[c % 3, side, block_at],
+            qkv_buf.at[first_rows(c, side), pl.ds(pl.multiple_of(land * JOB, JOB), JOB)],
+            first_send.at[at, k - 1, side], first_recv.at[at, land, side], device_of(target, across, core, tensor),
+        )
+
+    def first_in(c, land, side):
+        here = qkv_buf.at[first_rows(c, side), pl.ds(land * JOB, JOB)]
+        at = plane_first.index(c)
+        return remote(here, here, first_send.at[at, 0, side], first_recv.at[at, land, side], x_peer)
+
+    def first_start(c):
+        for side in range(2):
+            for k in (1, 3):
+                first_out(c, k, side).start()
+
+        @pl.when(jnp.logical_not(middle))
+        def _():
+            for side in range(2):
+                first_out(c, 2, side).start()
+
+    def first_relay(c):
+        @pl.when(middle)
+        def _():
+            for side in range(2):
+                first_in(c, 3, side).wait_recv()
+                stage[c % 3, side, far[2]] = (
+                    stage[c % 3, side, far[2]].astype(jnp.float32)
+                    + qkv_buf[first_rows(c, side), 3 * JOB : 4 * JOB].astype(jnp.float32)
+                ).astype(jnp.bfloat16)
+                first_out(c, 2, side).start()
+
+    def first_x(c):
+        slot = c % slots
+        return remote(x_land.at[slot, 1], x_land.at[slot, 2], x_send.at[c], x_recv.at[c], x_peer)
+
+    def first_sum(c):
+        for side in range(2):
+            first_in(c, 1, side).wait_recv()
+
+        @pl.when(plane > 0)
+        def _():
+            for side in range(2):
+                first_in(c, 0, side).wait_recv()
+
+        @pl.when(plane < planes - 1)
+        def _():
+            for side in range(2):
+                first_in(c, 2, side).wait_recv()
+
+        for at, side in enumerate((across, 1 - across)):
+            value = stage[c % 3, side, plane].astype(jnp.float32)
+            for land, there in ((0, plane > 0), (1, None), (2, plane < planes - 1)):
+                part = qkv_buf[first_rows(c, side), land * JOB : (land + 1) * JOB].astype(jnp.float32)
+                value += part if there is None else jnp.where(there, part, 0.0)
+            x_land[c % slots, at] = value.astype(jnp.bfloat16)
+        first_x(c).start()
+
+    def plane_out(c, k):
+        target, block_at, land = route(k)
         return remote(
             x_land.at[c % slots, block_at, :, used(c)], plane_land.at[c % slots, land, :, used(c)], plane_send.at[c, k - 1],
             plane_recv.at[c, land], device_of(target, across, core, tensor),
@@ -853,7 +930,11 @@
             copy.wait()
         if c + 1 < total:
             fetch(c + 1)
-        if c >= 3:
+        if c >= 3 and c - 3 in plane_first:
+            for side in range(2):
+                for k in range(1, planes):
+                    first_out(c - 3, k, side).wait_send()
+        elif c >= 3:
             x_out(c - 3).wait_send()
 
         @pl.loop(0, jobs[c][-1] // 256)
@@ -866,9 +947,15 @@
             ).astype(jnp.bfloat16)
             stage[c % 3, :, :, :, cols] = result.reshape(*left.shape[:-1], 256)
 
-        x_out(c).start()
+        if c in plane_first:
+            first_start(c)
+        else:
+            x_out(c).start()
 
     def fold(c):
+        if c in plane_first:
+            first_sum(c)
+            return
         x_out(c).wait_recv()
         slot = c % slots
 
@@ -888,6 +975,13 @@
                 plane_out(c, k).start()
 
     def finish(c):
+        if c in plane_first:
+            first_x(c).wait()
+            if c >= 2:
+                grad_out(c - 2).wait()
+            out_buf[c % 2] = x_land[c % slots, 0].astype(jnp.float32) + x_land[c % slots, 2].astype(jnp.float32)
+            grad_out(c).start()
+            return
         for k in range(1, planes):
             plane_out(c, k).wait_send()
         if c >= 2:
@@ -1215,7 +1309,10 @@
             rest_buf[s] = rest_wide[...].astype(jnp.bfloat16)
         for part in back_parts:
             back_own(*part).start()
-            for k in range(1, groups):
+
+    def back_some(i):
+        for k in range(1 + i, groups, 5):
+            for part in back_parts:
                 back(*part, k).start()
 
     def back_wait():
@@ -1270,31 +1367,35 @@
 
     plan = {
         0: [(rise, 0)],
-        1: [(rise, 1)],
-        2: [(rise, 2)],
-        3: [(rise, 3), (turn_hidden,), (hidden_start,)],
-        4: [(hidden_back, 0, planes // 2)],
-        5: [(hidden_back, planes // 2, planes), (norm_start,), (start_out,), (stored,)],
-        11: [(norm_back,), (mixed_start,)],
-        12: [(turn, 2, low_buf), (mixed_back,), (load_input,)],
-        13: [(wait_qkv,), (attend_back, 0, heads // 4), (turn_input,)],
-        14: [(attend_back, heads // 4, heads // 2)],
-        15: [(attend_back, heads // 2, 3 * heads // 4)],
-        16: [(attend_back, 3 * heads // 4, heads), (attend_done,), (store_qkv_wait,)],
-        17: [(input_back, 0, planes // 2), (small_begin, 0)],
-        18: [(input_back, planes // 2, planes), (small_end, 0), (small_begin, 1)],
-        19: [(small_end, 1), (small_begin, 2)],
-        20: [(small_end, 2), (small_begin, 3)],
-        21: [(input_done,), (send_back,), (small_end, 3)],
+        1: [(rise, 1), (rise, 2)],
+        2: [(rise, 3), (turn_hidden,), (hidden_start,)],
+        3: [(hidden_back, 0, planes // 2)],
+        4: [(hidden_back, planes // 2, planes), (norm_start,), (start_out,), (stored,)],
+        9: [(norm_back,), (mixed_start,)],
+        10: [(turn, 2, low_buf), (mixed_back,), (load_input,)],
+        11: [(wait_qkv,), (attend_back, 0, heads // 4), (turn_input,)],
+        12: [(attend_back, heads // 4, heads // 2)],
+        13: [(attend_back, heads // 2, 3 * heads // 4)],
+        14: [(attend_back, 3 * heads // 4, heads), (attend_done,), (store_qkv_wait,)],
+        15: [(input_back, 0, planes // 2), (small_begin, 0)],
+        16: [(input_back, planes // 2, planes), (small_end, 0), (small_begin, 1)],
+        17: [(small_end, 1), (small_begin, 2)],
+        18: [(input_done,), (send_back,), (back_some, 0), (small_end, 2), (small_begin, 3)],
+        19: [(back_some, 1), (small_end, 3)],
+        20: [(back_some, 2)],
+        21: [(back_some, 3)],
+        22: [(back_some, 4)],
     }
     for n in range(total + 4):
         if n < total:
             multiply(n)
         for step in plan.get(n, []):
             step[0](*step[1:])
+        if n - 1 in plane_first:
+            first_relay(n - 1)
         if 2 <= n < total + 2:
             fold(n - 2)
-        if relayed and 3 <= n < total + 3:
+        if relayed and 3 <= n < total + 3 and n - 3 not in plane_first:
             relay(n - 3)
         if n >= 4:
             finish(n - 4)
@@ -1344,6 +1445,7 @@
         (2, 2, 2), (2, 2), (2,), (total,), (total,), (4,), (4,), (total,), (total,),
         (total, planes - 1), (total, lands), (2 + planes,), (2 + planes,), (2, planes), (2, 2), (2,),
         (4,), (5,), (1,), (planes,), (planes,), (planes,), (planes,), (2, 2), (2, groups), (2, groups),
+        (2, 3, 2), (2, 4, 2),
     ]
     results = pl.pallas_call(
         partial(backward_kernel, planes),

time: 709 us -> 710 us (level)
    pallas_call x1, Pallas kernels: 333 us -> 340 us  [forward(): pl.pallas_call(partial(forward_kernel, planes, widths), out_shape=[jax.Sh...]
where the time goes in v8:
time: 710 us; the launch traced here: 706 us
  Pallas kernels  682 us (96%)
  local copies, waits for them, and re-layouts  20.9 us (3%)
    pallas_call x1, Pallas kernels, backward(): pl.pallas_call(partial(backward_kernel, planes), out_shape=[jax.ShapeDtyp...  342 us
    pallas_call x1, Pallas kernels, forward(): pl.pallas_call(partial(forward_kernel, planes, widths), out_shape=[jax.Sh...  340 us
    unnamed x31, local copies, waits for them, and re-layouts  15.4 us

profile of v8, /device:TPU:0, one launch (start us, length us, event | category | flops | bytes accessed | tf_op | source)
XLA Modules:
  0.0 706.0 jit_solution(16640628495816172710)
XLA Ops:
  0.7 0.7 compare_select_fusion
  1.3 2.0 copy.50
  3.4 0.6 gather_fusion
  4.0 0.0 copy-start.2
  4.0 1.0 slice.46.refs_6_
  5.1 0.0 copy-start.7
  5.1 0.1 slice.47
  5.2 0.8 reshape.91.refs_7_
  6.0 0.0 copy-done.2
  6.0 1.3 copy.42
  7.3 0.0 copy-done.7
  7.3 0.8 copy.41
  8.1 340.2 %forward_gather.1 = (bf16[4,2,2,128,1024]{4,3,2,1,0:T(8,128)(2,1)}, bf16[4,2,2,128,1024]{4,3,2,1,0:T(8,128)(2,1)}, bf16[4,2,2,128,1024]{4,3,2,1,0:T(8,128)(2,1)}...) custom-call(bf16[128,1024]{1,0:T(8,128)(2,1)} %refs_0_.1, ...), custom_call_target="tpu_custom_call" | custom-call | tf_op jit(solution)/shard_map/forward_gather/pallas_call | solution.py:641
  348.3 341.9 %backward_scatter.1 = (f32[128,1024]{1,0:T(8,128)}, f32[128,1024]{1,0:T(8,128)}, f32[128,1024]{1,0:T(8,128)}, f32[128,1024]{1,0:T(8,128)}, f32[128,4096]{1,0:T(8...) custom-call(bf16[4,2,2,128,1024]{4,3,2,1,0:T(8,128)(2,1)} %get-tuple, ...), custom_call_target="tpu_custom_call" | custom-call | tf_op jit(solution)/shard_map/backward_scatter/pallas_call | solution.py:1450
  690.2 1.0 reshape.103
  691.2 1.4 pad_maximum_fusion
  692.7 0.2 broadcast.8
  692.9 1.1 scatter_fusion
  694.0 1.8 copy.45
  695.7 0.0 copy-start.6
  695.7 0.0 copy-start.8
  695.7 0.0 copy-start.1
  695.7 3.0 copy.47
  698.8 0.0 copy-start.5
  698.8 0.0 copy-done.6
  698.8 1.0 copy.46
  699.8 0.0 copy-start.4
  699.8 0.0 copy-done.8
  699.8 0.6 fusion
  700.4 0.6 copy.48
  701.1 0.0 copy-done.1
  701.1 0.0 copy-start.3
  701.1 1.1 copy.57
  702.1 0.0 copy-done.5
  702.1 0.0 copy-start
  702.1 0.8 copy.58
  702.9 0.0 copy-done.4
  702.9 0.8 copy.59
  703.7 0.0 copy-done.3
  703.7 0.8 copy.60
  704.5 0.0 copy-done
  704.5 1.3 copy.61
  (2 shorter events, 0.0 us)
Async XLA Ops:
  4.0 1.9 copy-start.2
  5.1 2.2 copy-start.7
  695.7 3.0 copy-start.6
  695.7 4.0 copy-start.8
  695.7 5.3 copy-start.1
  698.8 3.3 copy-start.5
  699.8 3.1 copy-start.4
  701.1 2.7 copy-start.3
  702.1 2.4 copy-start
